TPU v7x, 32 devices: a whole 2x2x4 slice. The times are simulated.
32 devices in a mesh: pole: 2 (over y), row: 4 (over z), col: 2 (over x), sub: 2 (over core).
Axes of the slice: x: 2, y: 2, z: 4, core: 2. Of those that a mesh axis runs over, the one named last changes fastest.
Arguments:
- parent_inverse: bfloat16 [3072, 1536], P(('pole', 'row'), 'col'), parts along dimension 0, may hold values from -0.15625 to 0.15625
- panel: bfloat16 [48, 1280, 256], P(('pole', 'row'), 'col'), parts along dimension 0, may hold values from -1.1953125 to 1.1953125
- diag_inverse: bfloat16 [48, 256, 256], P(('pole', 'row'), None, 'sub'), parts along dimension 0, may hold values from -6 to 6
- pattern: int32 [24, 5], P('row'), may hold values from 0 to 5, as said below
- widths: int32 [24], P('row'), may hold values from 64 to 256, as said below
Outputs:
- off_block: bfloat16 [48, 1280, 256], P(('pole', 'row'), 'col', 'sub'), parts along dimension 0
- diag_block: bfloat16 [48, 256, 256], P(('pole', 'row'), None, 'sub'), parts along dimension 0
There are 2 independent parts, one for each index of `pole`. A program takes and returns all parts, laid end to end along the dimension named above; an argument that names none is the same for every part. Nothing has to cross between parts.
Inputs may be any that keep to these rules, and one draw needn't show every extreme that they name: `pattern`: each row lists 5 different ancestors in rising order; the last is always the root 6 - 1, and some row names ancestor 0. `widths`: child 0 has the full padded width 256.
All inputs are finite; a program needn't handle non-finite values.
Results may differ from a plain program's by a relative error of at most 0.0045.
Values may be sent and summed in bfloat16 or wider, within the bound.
No kernel may reach another device: no remote copies, remote signals or barrier semaphores. Data moves between devices by JAX's collectives and lax.ppermute only.
A program may use at most 64 MiB of HBM per device.

v0:
```python
import jax
import jax.numpy as jnp
from jax import lax
from jax.sharding import PartitionSpec as P


def local(parent_inverse, panel, diag_inverse, pattern, widths):
    block_size = panel.shape[2]
    half_cols = block_size // lax.axis_size("sub")
    sub_idx = lax.axis_index("sub")
    col_idx = lax.axis_index("col")
    col_mask = jnp.arange(block_size)[None, :] < widths[:, None]
    masked = panel * col_mask[:, None, :].astype(jnp.bfloat16)
    half_panel = lax.dynamic_slice_in_dim(masked, sub_idx * half_cols, half_cols, 2)
    full_panel = lax.all_gather(half_panel, "col", axis=1, tiled=True)
    columns = lax.all_gather(parent_inverse, "row", axis=0, tiled=True)
    pat_blocks = pattern.shape[1]
    local_blocks = columns.shape[1] // block_size
    anc_count = columns.shape[0] // block_size
    blocks_all = columns.reshape(anc_count, block_size, columns.shape[1])
    owned_ids = col_idx * local_blocks + jnp.arange(local_blocks, dtype=jnp.int32)

    def one_child(child_items):
        chosen, slab_cols = child_items
        sel_rows = jnp.take(blocks_all, chosen, axis=0).reshape(
            pat_blocks * block_size, columns.shape[1]
        )
        onehot = (owned_ids[:, None] == chosen[None, :]).astype(jnp.bfloat16)
        placed = jnp.einsum(
            "km,mbc->kbc",
            onehot,
            slab_cols.reshape(pat_blocks, block_size, half_cols),
            preferred_element_type=jnp.float32,
        )
        placed = placed.astype(jnp.bfloat16).reshape(local_blocks * block_size, half_cols)
        return jnp.dot(sel_rows, placed, preferred_element_type=jnp.float32)

    partial_value = lax.map(one_child, (pattern, full_panel))
    summed = lax.psum_scatter(partial_value, "col", scatter_dimension=1, tiled=True)
    off_block = (-summed).astype(jnp.bfloat16)
    diag_terms = jnp.einsum("jrb,jrc->jbc", masked, off_block, preferred_element_type=jnp.float32)
    diag_total = lax.psum(diag_terms, "col")
    mask_half = lax.dynamic_slice_in_dim(col_mask, sub_idx * half_cols, half_cols, 1)
    diag_mask = (col_mask[:, :, None] & mask_half[:, None, :]).astype(jnp.float32)
    diag_block = (diag_inverse.astype(jnp.float32) * diag_mask - diag_total).astype(jnp.bfloat16)
    return (off_block, diag_block)


def solution(mesh):
    placed = (
        P(("pole", "row"), "col"),
        P(("pole", "row"), "col", None),
        P(("pole", "row"), None, "sub"),
        P("row", None),
        P("row"),
    )
    return jax.shard_map(
        local,
        mesh=mesh,
        in_specs=placed,
        out_specs=(P(("pole", "row"), "col", "sub"), P(("pole", "row"), None, "sub")),
        check_vma=False,
    )
```

profile of v0, /device:TPU:0, one launch (start us, length us, event | category | flops | bytes accessed | tf_op | source)
XLA Modules:
  0.0 238.2 jit_solution(8548665052763113600)
XLA Ops:
  7.2 0.7 iota_compare_fusion
  7.9 1.7 broadcast_multiply_fusion
  9.6 1.3 copy-done
  10.9 1.1 constant_dynamic-slice_fusion.3
  12.9 33.7 %all-gather.5.cloned.1.call-done = bf16[6,1280,128]{2,1,0:T(8,128)(2,1)} async-done(((bf16[6,640,128]{2,1,0:T(8,128)(2,1)}), bf16[6,1280,128]{2,1,0:T(8,128)(2,1)}) %all-gather.5.cloned.1.call-update) | async-done | bytes 1966096 | tf_op jit(solution)/shard_map/all_gather | solution.py:15
  46.6 52.1 %all-gather.3.cloned.1.call-done = bf16[1536,768]{1,0:T(8,128)(2,1)} async-done(((bf16[384,768]{1,0:T(8,128)(2,1)}), bf16[1536,768]{1,0:T(8,128)(2,1)}) %all-gather.3.cloned.1.call-update) | async-done | bytes 2359312 | tf_op jit(solution)/shard_map/all_gather | solution.py:16
  98.7 41.9 %while.11 = (s32[]{:T(128)}, f32[6,1280,128]{2,1,0:T(8,128)}, s32[6,5]{1,0:T(8,128)}, bf16[6,256,768]{2,1,0:T(8,128)(2,1)}, bf16[6,1280,128]{2,1,0:T(8,128)(2,1)}, /*index=5*/s32[]{:T(128)}, s32[]{:T(128)}) while((s32[]{:T(128)}, f32[6,1280,128]{2,1,0:T(8,128)}, s32[6,5]{1,0:T(8,128)}, bf16[6,256,768]{2,1,0:T(8,128)(2,1)}, ...), condition=%wide.region_1.2_spmd.clone, body=%wide.region_0.1_spmd.clone.sunk | while | flops 253723712 | bytes 12260107 | solution.py:38
  99.4 2.3 gather_fusion
  101.7 0.7 compare_and_fusion.2
  102.7 1.0 constant_dynamic-slice_fusion.5
  104.1 1.5 fusion.28
  106.3 2.3 gather_fusion
  108.7 0.7 compare_and_fusion.2
  109.6 1.0 constant_dynamic-slice_fusion.5
  111.1 1.6 fusion.28
  113.3 2.3 gather_fusion
  116.6 1.0 constant_dynamic-slice_fusion.5
  118.1 1.5 fusion.28
  120.3 2.3 gather_fusion
  123.6 1.0 constant_dynamic-slice_fusion.5
  125.0 1.5 fusion.28
  127.3 2.3 gather_fusion
  130.6 1.0 constant_dynamic-slice_fusion.5
  132.0 1.5 fusion.28
  134.3 2.3 gather_fusion
  137.6 1.0 constant_dynamic-slice_fusion.5
  139.0 1.5 fusion.28
  140.6 50.9 %reduce-scatter.2.cloned.1.call-done = f32[6,640,128]{2,1,0:T(8,128)} async-done(((f32[6,1280,128]{2,1,0:T(8,128)}), f32[6,640,128]{2,1,0:T(8,128)}) %reduce-scatter.2.cloned.1.call-update) | async-done | bytes 1966096 | tf_op jit(solution)/shard_map/reduce_scatter | solution.py:39
  191.5 1.7 negate_convert_fusion
  193.3 1.7 fusion.12
  195.0 34.5 %all-reduce.2.cloned.1.call-done = f32[6,256,128]{2,1,0:T(8,128)} async-done(((f32[6,256,128]{2,1,0:T(8,128)}), f32[6,256,128]{2,1,0:T(8,128)}) %all-reduce.2.cloned.1.call-update) | async-done | bytes 786448 | tf_op jit(solution)/shard_map/psum | solution.py:42
  229.5 2.2 subtract_convert_fusion
  (57 shorter events, 11.9 us)
Async XLA Ops:
  7.2 39.4 %all-gather.5.cloned.1.call-start = ((), (), s32[]{:S(2)}) async-start(), calls=%async_computation.2 | async-start | bytes 2949120 | tf_op jit(solution)/shard_map/all_gather | solution.py:15
  9.6 1.3 copy-start
  12.1 86.6 %all-gather.3.cloned.1.call-start = ((), (), s32[]{:S(2)}) async-start(), calls=%async_computation.1 | async-start | bytes 2949120 | tf_op jit(solution)/shard_map/all_gather | solution.py:16
  12.8 178.7 %reduce-scatter.2.cloned.1.call-start = ((), (), s32[]{:S(2)}) async-start(), calls=%async_computation.3 | async-start | bytes 5898240 | tf_op jit(solution)/shard_map/reduce_scatter | solution.py:39
  140.6 52.7 %copy-start.1 = (bf16[6,640,256]{2,1,0:T(8,128)(2,1)S(1)}, bf16[6,640,256]{2,1,0:T(8,128)(2,1)}, u32[]{:S(2)}) copy-start(bf16[6,640,256]{2,1,0:T(8,128)(2,1)} %copy-done) | copy-start | bytes 5898244
  140.6 88.9 %all-reduce.2.cloned.1.call-start = ((), (), s32[]{:S(2)}) async-start(), calls=%async_computation.4 | async-start | bytes 1572864 | tf_op jit(solution)/shard_map/psum | solution.py:42
  193.2 1.7 copy-start.2
  193.2 36.3 %copy-start.3 = (bf16[6,256,128]{2,1,0:T(8,128)(2,1)S(1)}, bf16[6,256,128]{2,1,0:T(8,128)(2,1)}, u32[]{:S(2)}) copy-start(bf16[6,256,128]{2,1,0:T(8,128)(2,1)} %param.9) | copy-start | bytes 1179652
Sparse Core Ops, SparseCore 0:
  12.2 34.3 all-gather.4
  48.1 50.4 all-gather.2
  140.7 50.7 reduce-scatter.1
  195.1 34.3 all-reduce.1
where the time goes:
time: 239 us; the launch traced here: 238 us
  waiting for transfers between devices  172 us (72%)
  local copies, waits for them, and re-layouts  22.7 us (9%)
  other arithmetic  16.3 us (7%)
  between operations  13.8 us (6%)
  matrix products  13.1 us (5%)
    all_gather x1, waiting for transfers between devices, local(): columns = lax.all_gather(parent_inverse, 'row', axis=0, tiled=True)  52.1 us
    reduce_scatter x1, waiting for transfers between devices, local(): lax.psum_scatter(partial_value, 'col', scatter_dimension=1, tiled=True)  50.9 us
    psum x1, waiting for transfers between devices, local(): diag_total = lax.psum(diag_terms, 'col')  34.5 us
    all_gather x1, waiting for transfers between devices, local(): full_panel = lax.all_gather(half_panel, 'col', axis=1, tiled=True)  33.7 us
    gather x6, local copies, waits for them, and re-layouts, one_child(): jnp.take(blocks_all, chosen, axis=0)  14 us
    dot_general x6, matrix products, one_child(): return jnp.dot(sel_rows, placed, preferred_element_type=jnp.float32)  9.24 us
    dynamic_slice x6, local copies, waits for them, and re-layouts, local(): partial_value = lax.map(one_child, (pattern, full_panel))  6.01 us
    select_n x12, other arithmetic, one_child(): jnp.take(blocks_all, chosen, axis=0)  5.68 us
  transfers between devices with their start and end apart: 4, of which 4 were waited for; matrix products, arithmetic and copies ran while one was open for 0% of the time, Pallas kernels for 0%

commit v1 on v0

v1 whole, which is shorter than its diff:
```python
import functools

import jax
import jax.numpy as jnp
from jax import lax
from jax.experimental import pallas as pl
from jax.experimental.pallas import tpu as pltpu
from jax.sharding import PartitionSpec as P

SWAP = [(0, 1), (1, 0)]
F32 = jnp.float32
BF16 = jnp.bfloat16


def generic(parent_inverse, panel, diag_inverse, pattern, widths):
    block_size = panel.shape[2]
    half_cols = block_size // lax.axis_size("sub")
    sub_idx = lax.axis_index("sub")
    col_idx = lax.axis_index("col")
    col_mask = jnp.arange(block_size)[None, :] < widths[:, None]
    masked = panel * col_mask[:, None, :].astype(BF16)
    half_panel = lax.dynamic_slice_in_dim(masked, sub_idx * half_cols, half_cols, 2)
    full_panel = lax.all_gather(half_panel, "col", axis=1, tiled=True)
    columns = lax.all_gather(parent_inverse, "row", axis=0, tiled=True)
    pat_blocks = pattern.shape[1]
    local_blocks = columns.shape[1] // block_size
    anc_count = columns.shape[0] // block_size
    blocks_all = columns.reshape(anc_count, block_size, columns.shape[1])
    owned_ids = col_idx * local_blocks + jnp.arange(local_blocks, dtype=jnp.int32)

    def one_child(child_items):
        chosen, slab_cols = child_items
        sel_rows = jnp.take(blocks_all, chosen, axis=0).reshape(pat_blocks * block_size, columns.shape[1])
        onehot = (owned_ids[:, None] == chosen[None, :]).astype(BF16)
        slab = slab_cols.reshape(pat_blocks, block_size, half_cols)
        placed = jnp.einsum("km,mbc->kbc", onehot, slab, preferred_element_type=F32)
        placed = placed.astype(BF16).reshape(local_blocks * block_size, half_cols)
        return jnp.dot(sel_rows, placed, preferred_element_type=F32)

    partial_value = lax.map(one_child, (pattern, full_panel))
    summed = lax.psum_scatter(partial_value, "col", scatter_dimension=1, tiled=True)
    off_block = (-summed).astype(BF16)
    diag_terms = jnp.einsum("jrb,jrc->jbc", masked, off_block, preferred_element_type=F32)
    diag_total = lax.psum(diag_terms, "col")
    mask_half = lax.dynamic_slice_in_dim(col_mask, sub_idx * half_cols, half_cols, 1)
    diag_mask = (col_mask[:, :, None] & mask_half[:, None, :]).astype(F32)
    diag_block = (diag_inverse.astype(F32) * diag_mask - diag_total).astype(BF16)
    return (off_block, diag_block)


def spread_kernel(ids, pat, mine, other, out):
    children, rows, width = mine.shape
    c = ids[1]
    blocks = out.shape[0] // 256
    per_col = blocks // 2
    chunks = rows // 128
    out[...] = jnp.zeros_like(out)
    for who, src in ((c, mine), (1 - c, other)):
        for j in range(children):
            for q in range(chunks):
                g = who * chunks + q
                anc = pat[j, g // 2]
                side = jnp.where(anc // per_col == c, 0, per_col)
                start = (side + anc % per_col) * 256 + (g % 2) * 128
                out[pl.ds(pl.multiple_of(start, 128), 128), j * width : (j + 1) * width] = src[
                    j, q * 128 : (q + 1) * 128, :
                ]


def product_kernel(a0, a1, b0, b1, spread, out, rows):
    half, wide = a0.shape
    rows[:half, :wide] = a0[...]
    rows[half:, :wide] = a1[...]
    rows[:half, wide:] = b0[...]
    rows[half:, wide:] = b1[...]
    out[...] = (-jnp.dot(rows[...], spread[...], preferred_element_type=F32)).astype(BF16)


def final_kernel(ids, pat, widths, y0, y1, y2, y3, panel, same, cross, dinv, off_out, diag_out, full, off):
    j = pl.program_id(0)
    r, c, s = ids[0], ids[1], ids[2]
    _, rows, width = panel.shape
    half = y0.shape[0] // 2
    lane = y0.shape[1] // pl.num_programs(0)

    @pl.when(j == 0)
    def _():
        for k, y in enumerate((y0, y1, y2, y3)):
            shard = jnp.bitwise_xor(r, k)
            for side in range(2):
                where = jnp.where(s == side, 0, half)
                full[pl.ds(pl.multiple_of(shard * 2 * half + side * half, 64), half), :] = y[
                    pl.ds(pl.multiple_of(where, 64), half), :
                ]

    col = pl.ds(pl.multiple_of(j * lane, 128), lane)
    chunks = rows // 128
    for n, who in enumerate((c, 1 - c)):
        for q in range(chunks):
            g = who * chunks + q
            start = pat[j, g // 2] * 256 + (g % 2) * 128
            off[n * rows + q * 128 : n * rows + (q + 1) * 128, :] = full[
                pl.ds(pl.multiple_of(start, 128), 128), col
            ]
    w = widths[j]
    keep_b = s * lane + lax.broadcasted_iota(jnp.int32, (1, lane), 1) < w
    keep_a = lax.broadcasted_iota(jnp.int32, (width, 1), 0) < w
    own = off[:rows, :]
    off_out[0] = jnp.where(keep_b, own, jnp.zeros_like(own))
    dims = (((0,), (0,)), ((), ()))
    terms = lax.dot_general(panel[j], own, dims, preferred_element_type=F32)
    oth = off[rows:, :]
    t_same = lax.dot_general(same[j], oth, dims, preferred_element_type=F32)
    t_cross = lax.dot_general(cross[j], oth, dims, preferred_element_type=F32)
    low = jnp.where(s == 0, t_same, t_cross)
    high = jnp.where(s == 0, t_cross, t_same)
    terms = terms + jnp.concatenate([low, high], axis=0)
    diag = dinv[0].astype(F32) - terms
    diag_out[0] = jnp.where(keep_a & keep_b, diag, 0.0).astype(BF16)


VMEM = pl.BlockSpec(memory_space=pltpu.VMEM)
SMEM = pl.BlockSpec(memory_space=pltpu.SMEM)


def gathered(parent, panel, diag_inverse, pattern, widths):
    r, c, s = lax.axis_index("row"), lax.axis_index("col"), lax.axis_index("sub")
    children, rows, width = panel.shape
    lane = width // 2
    half, wide = parent.shape[0] // 2, parent.shape[1]
    ids = jnp.stack([r, c, s]).astype(jnp.int32)

    def xor(d):
        return [(i, i ^ d) for i in range(4)]

    def sib(x):
        return lax.ppermute(x, "sub", SWAP)

    own = lax.dynamic_slice_in_dim(parent, s * half, half, 0)
    own_sib = lax.dynamic_slice_in_dim(parent, (1 - s) * half, half, 0)
    mine = lax.dynamic_slice_in_dim(panel, s * lane, lane, 2)
    b0 = lax.ppermute(own, "col", SWAP)
    same = lax.ppermute(mine, "col", SWAP)
    a1, a2, a3 = (lax.ppermute(own, "row", xor(d)) for d in (1, 2, 3))
    b1 = lax.ppermute(b0, "row", xor(1))
    cut = half // 2
    b2 = jnp.concatenate(
        [lax.ppermute(b0[:cut], "row", xor(2)), lax.ppermute(a2[cut:], "col", SWAP)], axis=0
    )
    b3 = lax.ppermute(a3, "col", SWAP)
    cross = sib(same)

    spread = pl.pallas_call(
        spread_kernel,
        out_shape=jax.ShapeDtypeStruct((2 * wide, children * lane), BF16),
        in_specs=[SMEM, SMEM, VMEM, VMEM],
        out_specs=VMEM,
        cost_estimate=pl.CostEstimate(flops=0, bytes_accessed=4 << 20, transcendentals=0),
        name="spread",
    )(ids, pattern, mine, same)

    product = pl.pallas_call(
        product_kernel,
        out_shape=jax.ShapeDtypeStruct((2 * half, children * lane), BF16),
        in_specs=[VMEM] * 5,
        out_specs=VMEM,
        scratch_shapes=[pltpu.VMEM((2 * half, 2 * wide), BF16)],
        cost_estimate=pl.CostEstimate(
            flops=2 * 2 * half * 2 * wide * children * lane, bytes_accessed=4 << 20, transcendentals=0
        ),
        compiler_params=pltpu.CompilerParams(vmem_limit_bytes=24 << 20),
        name="product",
    )
    ys = [
        product(own, own_sib, b0, sib(b0), spread),
        product(a1, sib(a1), b1, sib(b1), spread),
        product(a2, sib(a2), b2, sib(b2), spread),
        product(a3, sib(a3), b3, sib(b3), spread),
    ]
    return pl.pallas_call(
        final_kernel,
        grid=(children,),
        out_shape=(
            jax.ShapeDtypeStruct((children, rows, lane), BF16),
            jax.ShapeDtypeStruct((children, width, lane), BF16),
        ),
        in_specs=[SMEM, SMEM, SMEM] + [VMEM] * 7 + [pl.BlockSpec((1, width, lane), lambda j: (j, 0, 0))],
        out_specs=(
            pl.BlockSpec((1, rows, lane), lambda j: (j, 0, 0)),
            pl.BlockSpec((1, width, lane), lambda j: (j, 0, 0)),
        ),
        scratch_shapes=[
            pltpu.VMEM((4 * 2 * half, children * lane), BF16),
            pltpu.VMEM((2 * rows, lane), BF16),
        ],
        cost_estimate=pl.CostEstimate(
            flops=2 * children * width * 2 * rows * lane, bytes_accessed=8 << 20, transcendentals=0
        ),
        compiler_params=pltpu.CompilerParams(vmem_limit_bytes=24 << 20),
        name="final",
    )(ids, pattern, widths, *ys, panel, same, cross, diag_inverse)


def solution(mesh):
    placed = (
        P(("pole", "row"), "col"),
        P(("pole", "row"), "col", None),
        P(("pole", "row"), None, "sub"),
        P("row", None),
        P("row"),
    )
    shape = dict(mesh.shape)
    fits = (shape["row"], shape["col"], shape["sub"]) == (4, 2, 2)
    return jax.shard_map(
        gathered if fits else generic,
        mesh=mesh,
        in_specs=placed,
        out_specs=(P(("pole", "row"), "col", "sub"), P(("pole", "row"), None, "sub")),
        check_vma=False,
    )
```

time: 239 us -> 75 us (0.31)
  waiting for transfers between devices: 172 us -> 33.6 us
  local copies, waits for them, and re-layouts: 22.7 us -> 6.25 us
  starting transfers between devices: 0.16 us -> 16.6 us
  Pallas kernels: 0 us -> 16 us
  other arithmetic: 16.3 us -> 0.65 us
  matrix products: 13.1 us -> 0 us
  between operations: 13.8 us -> 0.92 us
    all_gather x2 -> x0, waiting for transfers between devices: 85.8 us -> none  [the longest x1 52.1 us: local(): columns = lax.all_gather(parent_inverse, 'row', axis=0, tiled=True)]
    reduce_scatter x1 -> x0, waiting for transfers between devices: 50.9 us -> none  [local(): lax.psum_scatter(partial_value, 'col', scatter_dimension=1, tiled=True)]
    psum x1 -> x0, waiting for transfers between devices: 34.5 us -> none  [local(): diag_total = lax.psum(diag_terms, 'col')]
    ppermute x0 -> x17, waiting for transfers between devices: none -> 33.6 us  [the longest x1 23.3 us: gathered(): b0 = lax.ppermute(own, 'col', SWAP)]
    ppermute x0 -> x17, starting transfers between devices: none -> 16.6 us  [the longest x3 4.67 us: gathered(): a1, a2, a3 = (lax.ppermute(own, 'row', xor(d)) for d in (1, 2, 3))]
    pallas_call x0 -> x6, Pallas kernels: none -> 16 us  [the longest x1 4.46 us: gathered(): pl.pallas_call(final_kernel, grid=(children,), out_shape=(jax.ShapeDtypeS...]
    gather x6 -> x0, local copies, waits for them, and re-layouts: 14 us -> none  [one_child(): jnp.take(blocks_all, chosen, axis=0)]
    dot_general x13 -> x0, matrix products: 13.1 us -> none  [the longest x6 9.24 us: one_child(): return jnp.dot(sel_rows, placed, preferred_element_type=jnp.float32)]
  transfers between devices with their start and end apart: 4 -> 17, of which waited for: 4 -> 3; matrix products, arithmetic and copies ran while one was open for 0% -> 1% of each run, Pallas kernels for 0% -> 16%
where the time goes in v1:
time: 75 us; the launch traced here: 74.1 us
  waiting for transfers between devices  33.6 us (45%)
  starting transfers between devices  16.6 us (22%)
  Pallas kernels  16 us (21%)
  local copies, waits for them, and re-layouts  6.25 us (8%)
  between operations  0.92 us (1%)
    ppermute x1, waiting for transfers between devices, gathered(): b0 = lax.ppermute(own, 'col', SWAP)  23.3 us
    ppermute x1, waiting for transfers between devices, gathered(): b3 = lax.ppermute(a3, 'col', SWAP)  6.02 us
    unnamed x33, local copies, waits for them, and re-layouts  4.85 us
    ppermute x3, starting transfers between devices, gathered(): a1, a2, a3 = (lax.ppermute(own, 'row', xor(d)) for d in (1, 2, 3))  4.67 us
    pallas_call x1, Pallas kernels, gathered(): pl.pallas_call(final_kernel, grid=(children,), out_shape=(jax.ShapeDtypeS...  4.46 us
    ppermute x1, waiting for transfers between devices, gathered(): lax.ppermute(b0[:cut], 'row', xor(2))  4.31 us
    pallas_call x1, Pallas kernels, gathered(): pl.pallas_call(spread_kernel, out_shape=jax.ShapeDtypeStruct((2 * wide, c...  3.77 us
    ppermute x1, starting transfers between devices, gathered(): same = lax.ppermute(mine, 'col', SWAP)  3 us
  transfers between devices with their start and end apart: 17, of which 3 were waited for; matrix products, arithmetic and copies ran while one was open for 1% of the time, Pallas kernels for 16%

profile of v1, /device:TPU:0, one launch (start us, length us, event | category | flops | bytes accessed | tf_op | source)
XLA Modules:
  0.0 74.1 jit_solution(17827575688382574019)
XLA Ops:
  0.6 1.3 %constant_dynamic-slice_fusion.mine = bf16[6,640,128]{2,1,0:T(8,128)(2,1)S(1)} fusion(bf16[6,640,256]{2,1,0:T(8,128)(2,1)} %panel.1, s32[]{:T(128)S(6)} %select_n.11), kind=kLoop, calls=%fused_computation.2 | loop fusion | bytes 1966084 | tf_op jit(solution)/shard_map/dynamic_slice | solution.py:141
  2.0 0.0 copy-start.14
  2.0 3.0 %collective-permute-start.2 = (bf16[6,640,128]{2,1,0:T(8,128)(2,1)S(1)}, bf16[6,640,128]{2,1,0:T(8,128)(2,1)S(1)}, u32[]{:S(2)}, u32[]{:S(2)}) collective-permute-start(bf16[6,640,128]{2,1,0:T(8,128)(2,1)S(1)} %constant_dynamic-slice_fusion.mine), channel_id=1, source_target_pairs={{0,2},{2,0},{1,3},{3,1},{4,6},{6,4},{5,7},{7,5},{8,10},{10,8},{9,1... | collective-permute-start | bytes 2949128 | tf_op jit(solution)/shard_map/ppermute | solution.py:143
  5.0 0.1 collective-permute-start
  5.1 3.1 %collective-permute-start.7 = (bf16[192,768]{1,0:T(8,128)(2,1)S(1)}, bf16[192,768]{1,0:T(8,128)(2,1)S(1)}, u32[]{:S(2)}, u32[]{:S(2)}) collective-permute-start(bf16[192,768]{1,0:T(8,128)(2,1)S(1)} %get-tuple-element.3.a0), channel_id=1, source_target_pairs={{0,8},{4,12},{8,0},{12,4},{1,9},{5,13},{9,1},{13,5},{2,10},{6,14},... | collective-permute-start | bytes 884744 | tf_op jit(solution)/shard_map/ppermute | solution.py:144
  8.2 1.6 %collective-permute-start.3 = (bf16[192,768]{1,0:T(8,128)(2,1)S(1)}, bf16[192,768]{1,0:T(8,128)(2,1)S(1)}, u32[]{:S(2)}, u32[]{:S(2)}) collective-permute-start(bf16[192,768]{1,0:T(8,128)(2,1)S(1)} %get-tuple-element.3.a0), channel_id=1, source_target_pairs={{0,4},{4,0},{8,12},{12,8},{1,5},{5,1},{9,13},{13,9},{2,6},{6,2},{1... | collective-permute-start | bytes 884744 | tf_op jit(solution)/shard_map/ppermute | solution.py:144
  9.8 23.3 %collective-permute-done.b0 = bf16[192,768]{1,0:T(8,128)(2,1)S(1)} collective-permute-done((bf16[192,768]{1,0:T(8,128)(2,1)S(1)}, bf16[192,768]{1,0:T(8,128)(2,1)S(1)}, u32[]{:S(2)}, u32[]{:S(2)}) %collective-permute-start) | collective-permute-done | bytes 294944 | tf_op jit(solution)/shard_map/ppermute | solution.py:142
  33.1 1.8 %collective-permute-start.5 = (bf16[192,768]{1,0:T(8,128)(2,1)S(1)}, bf16[192,768]{1,0:T(8,128)(2,1)}, u32[]{:S(2)}, u32[]{:S(2)}) collective-permute-start(bf16[192,768]{1,0:T(8,128)(2,1)S(1)} %collective-permute-done.b0), channel_id=1, source_target_pairs={{0,4},{4,0},{8,12},{12,8},{1,5},{5,1},{9,13},{13,9},{2,6},{6,2},{1... | collective-permute-start | bytes 884744 | tf_op jit(solution)/shard_map/ppermute | solution.py:145
  34.9 0.1 collective-permute-start.16
  35.0 2.7 %collective-permute-start.9 = (bf16[96,768]{1,0:T(8,128)(2,1)S(1)}, bf16[96,768]{1,0:T(8,128)(2,1)S(1)}, u32[]{:S(2)}, u32[]{:S(2)}) collective-permute-start(bf16[96,768]{1,0:T(8,128)(2,1)S(1)} %slice.8), channel_id=1, source_target_pairs={{0,8},{4,12},{8,0},{12,4},{1,9},{5,13},{9,1},{13,5},{2,10},{6,14},... | collective-permute-start | bytes 442376 | tf_op jit(solution)/shard_map/ppermute | solution.py:148
  37.7 1.6 %collective-permute-start.10 = (bf16[96,768]{1,0:T(8,128)(2,1)S(1)}, bf16[96,768]{1,0:T(8,128)(2,1)S(1)}, u32[]{:S(2)}, u32[]{:S(2)}) collective-permute-start(bf16[96,768]{1,0:T(8,128)(2,1)S(1)} %slice.9), channel_id=1, source_target_pairs={{0,2},{2,0},{1,3},{3,1},{4,6},{6,4},{5,7},{7,5},{8,10},{10,8},{9,1... | collective-permute-start | bytes 442376 | tf_op jit(solution)/shard_map/ppermute | solution.py:148
  39.2 4.3 %collective-permute-done.9 = bf16[96,768]{1,0:T(8,128)(2,1)S(1)} collective-permute-done((bf16[96,768]{1,0:T(8,128)(2,1)S(1)}, bf16[96,768]{1,0:T(8,128)(2,1)S(1)}, u32[]{:S(2)}, u32[]{:S(2)}) %collective-permute-start.9) | collective-permute-done | bytes 147488 | tf_op jit(solution)/shard_map/ppermute | solution.py:148
  43.6 0.7 copy-done.5
  44.3 1.5 %collective-permute-start.14 = (bf16[192,768]{1,0:T(8,128)(2,1)}, bf16[192,768]{1,0:T(8,128)(2,1)}, u32[]{:S(2)}, u32[]{:S(2)}) collective-permute-start(bf16[192,768]{1,0:T(8,128)(2,1)} %collective-permute-done.12.a0), channel_id=1, source_target_pairs={{0,2},{2,0},{1,3},{3,1},{4,6},{6,4},{5,7},{7,5},{8,10},{10,8},{9,1... | collective-permute-start | bytes 884744 | tf_op jit(solution)/shard_map/ppermute | solution.py:150
  45.8 0.2 collective-permute-start.6
  46.1 0.7 copy-done.7
  46.8 0.3 collective-permute-start.8
  47.1 0.7 copy-done.9
  47.8 0.2 collective-permute-start.11
  48.0 6.0 %collective-permute-done.14.b0 = bf16[192,768]{1,0:T(8,128)(2,1)} collective-permute-done((bf16[192,768]{1,0:T(8,128)(2,1)}, bf16[192,768]{1,0:T(8,128)(2,1)}, u32[]{:S(2)}, u32[]{:S(2)}) %collective-permute-start.14) | collective-permute-done | bytes 294944 | tf_op jit(solution)/shard_map/ppermute | solution.py:150
  54.0 0.5 collective-permute-start.15
  54.6 0.6 pad_add_fusion.ids
  55.2 3.8 %spread.1 = bf16[1536,768]{1,0:T(8,128)(2,1)} custom-call(s32[3]{0:T(128)} %pad_add_fusion.ids, s32[6,5]{1,0:T(8,128)} %pat.3, bf16[6,640,128]{2,1,0:T(8,128)(2,1)} %copy-done.14, bf16[6,640,128]{2,1,0:T(8,128)(2,1)} %copy-done.2), custom_call_target="tpu_custom_call" | custom-call | bytes 4194304 | tf_op jit(solution)/shard_map/spread/pallas_call | solution.py:153
  59.0 1.7 %copy-done = bf16[1536,768]{1,0:T(8,128)(2,1)S(1)} copy-done((bf16[1536,768]{1,0:T(8,128)(2,1)S(1)}, bf16[1536,768]{1,0:T(8,128)(2,1)}, u32[]{:S(2)}) %copy-start) | copy-done | bytes 2359320
  60.6 1.0 %copy-done.8 = bf16[192,768]{1,0:T(8,128)(2,1)S(1)} copy-done((bf16[192,768]{1,0:T(8,128)(2,1)S(1)}, bf16[192,768]{1,0:T(8,128)(2,1)}, u32[]{:S(2)}) %copy-start.8) | copy-done | bytes 294936
  61.6 1.1 %product.4.y0 = bf16[384,768]{1,0:T(8,128)(2,1)S(1)} custom-call(bf16[192,768]{1,0:T(8,128)(2,1)S(1)} %get-tuple-element.3.a0, bf16[192,768]{1,0:T(8,128)(2,1)S(1)} %get-tuple-element.2.a1, bf16[192,768]{1,0:T(8,128)(2,1)S(1)} %collective-permute-done.b0, bf16[192,768]{1,0:T(8,128)(2,1)S(1)} %copy-done.8, bf16[1536,768]{1,0:T(8,128)(2,1)S(1)} %copy-done), custom_call_target="tpu_custom_call" | custom-call | flops 905969664 | bytes 4194304 | tf_op jit(solution)/shard_map/product/pallas_call | solution.py:175
  62.7 2.1 %product.5.y1 = bf16[384,768]{1,0:T(8,128)(2,1)S(1)} custom-call(bf16[192,768]{1,0:T(8,128)(2,1)S(1)} %copy-done.6, bf16[192,768]{1,0:T(8,128)(2,1)S(1)} %copy-done.10, bf16[192,768]{1,0:T(8,128)(2,1)} %collective-permute-done.5.b0, bf16[192,768]{1,0:T(8,128)(2,1)} %collective-permute-done.6.b1, bf16[1536,768]{1,0:T(8,128)(2,1)S(1)} %copy-done), custom_call_target="tpu_custom_call" | custom-call | flops 905969664 | bytes 4194304 | tf_op jit(solution)/shard_map/product/pallas_call | solution.py:176
  64.9 2.1 %product.6.y2 = bf16[384,768]{1,0:T(8,128)(2,1)S(1)} custom-call(bf16[192,768]{1,0:T(8,128)(2,1)S(1)} %collective-permute-done.7.a0, bf16[192,768]{1,0:T(8,128)(2,1)} %collective-permute-done.8.a1, bf16[192,768]{1,0:T(8,128)(2,1)S(1)} %constant_dynamic-update-slice_fusion.b0, bf16[192,768]{1,0:T(8,128)(2,1)} %collective-permute-done.11.b1, ...), custom_call_target="tpu_custom_call" | custom-call | flops 905969664 | bytes 4194304 | tf_op jit(solution)/shard_map/product/pallas_call | solution.py:177
  67.0 0.0 copy-start.1
  67.1 0.0 copy-start.13
  67.1 2.5 %product.7.y3 = bf16[384,768]{1,0:T(8,128)(2,1)S(1)} custom-call(bf16[192,768]{1,0:T(8,128)(2,1)} %collective-permute-done.12.a0, bf16[192,768]{1,0:T(8,128)(2,1)} %collective-permute-done.13.a1, bf16[192,768]{1,0:T(8,128)(2,1)} %collective-permute-done.14.b0, bf16[192,768]{1,0:T(8,128)(2,1)} %collective-permute-done.15.b1, bf16[1536,768]{1,0:T(8,128)(2,1)S(1)} %copy-done), custom_call_target="tpu_custom_call" | custom-call | flops 905969664 | bytes 4194304 | tf_op jit(solution)/shard_map/product/pallas_call | solution.py:178
  69.6 4.5 %final.1 = (bf16[6,640,128]{2,1,0:T(8,128)(2,1)}, bf16[6,256,128]{2,1,0:T(8,128)(2,1)}) custom-call(s32[3]{0:T(128)S(1)} %copy-done.12, s32[6,5]{1,0:T(8,128)S(1)} %copy-done.11, s32[6]{0:T(128)S(1)} %copy-done.13, bf16[384,768]{1,0:T(8,128)(2,1)S(1)} %product.4.y0, bf16[384,768]{1,0:T(8,128)(2,1)S(1)} %product.5.y1, bf16[384,768]{1,0:T(8,128)(2,1)S(1)} %product.6.y2, ...), custom_call_target="tpu_custom_call" | custom-call | flops 503316480 | bytes 8388608 | tf_op jit(solution)/shard_map/final/pallas_call | solution.py:180
  (47 shorter events, 0.2 us)
Async XLA Ops:
  0.6 4.4 %copy-start.15 = (bf16[384,768]{1,0:T(8,128)(2,1)S(1)}, bf16[384,768]{1,0:T(8,128)(2,1)}, u32[]{:S(2)}) copy-start(bf16[384,768]{1,0:T(8,128)(2,1)} %param.5) | copy-start | bytes 1769476
  2.0 32.9 %copy-start.14 = (bf16[6,640,128]{2,1,0:T(8,128)(2,1)}, bf16[6,640,128]{2,1,0:T(8,128)(2,1)S(1)}, u32[]{:S(2)}) copy-start(bf16[6,640,128]{2,1,0:T(8,128)(2,1)S(1)} %constant_dynamic-slice_fusion.mine) | copy-start | bytes 2949124
  2.0 32.9 %collective-permute-start.2 = (bf16[6,640,128]{2,1,0:T(8,128)(2,1)S(1)}, bf16[6,640,128]{2,1,0:T(8,128)(2,1)S(1)}, u32[]{:S(2)}, u32[]{:S(2)}) collective-permute-start(bf16[6,640,128]{2,1,0:T(8,128)(2,1)S(1)} %constant_dynamic-slice_fusion.mine), channel_id=1, source_target_pairs={{0,2},{2,0},{1,3},{3,1},{4,6},{6,4},{5,7},{7,5},{8,10},{10,8},{9,1... | collective-permute-start | bytes 2949128 | tf_op jit(solution)/shard_map/ppermute | solution.py:143
  5.0 28.0 %collective-permute-start = (bf16[192,768]{1,0:T(8,128)(2,1)S(1)}, bf16[192,768]{1,0:T(8,128)(2,1)S(1)}, u32[]{:S(2)}, u32[]{:S(2)}) collective-permute-start(bf16[192,768]{1,0:T(8,128)(2,1)S(1)} %get-tuple-element.3.a0), channel_id=1, source_target_pairs={{0,2},{2,0},{1,3},{3,1},{4,6},{6,4},{5,7},{7,5},{8,10},{10,8},{9,1... | collective-permute-start | bytes 884744 | tf_op jit(solution)/shard_map/ppermute | solution.py:142
  5.1 29.9 %collective-permute-start.7 = (bf16[192,768]{1,0:T(8,128)(2,1)S(1)}, bf16[192,768]{1,0:T(8,128)(2,1)S(1)}, u32[]{:S(2)}, u32[]{:S(2)}) collective-permute-start(bf16[192,768]{1,0:T(8,128)(2,1)S(1)} %get-tuple-element.3.a0), channel_id=1, source_target_pairs={{0,8},{4,12},{8,0},{12,4},{1,9},{5,13},{9,1},{13,5},{2,10},{6,14},... | collective-permute-start | bytes 884744 | tf_op jit(solution)/shard_map/ppermute | solution.py:144
  8.2 29.4 %collective-permute-start.3 = (bf16[192,768]{1,0:T(8,128)(2,1)S(1)}, bf16[192,768]{1,0:T(8,128)(2,1)S(1)}, u32[]{:S(2)}, u32[]{:S(2)}) collective-permute-start(bf16[192,768]{1,0:T(8,128)(2,1)S(1)} %get-tuple-element.3.a0), channel_id=1, source_target_pairs={{0,4},{4,0},{8,12},{12,8},{1,5},{5,1},{9,13},{13,9},{2,6},{6,2},{1... | collective-permute-start | bytes 884744 | tf_op jit(solution)/shard_map/ppermute | solution.py:144
  9.8 29.4 %collective-permute-start.12 = (bf16[192,768]{1,0:T(8,128)(2,1)S(1)}, bf16[192,768]{1,0:T(8,128)(2,1)}, u32[]{:S(2)}, u32[]{:S(2)}) collective-permute-start(bf16[192,768]{1,0:T(8,128)(2,1)S(1)} %get-tuple-element.3.a0), channel_id=1, source_target_pairs={{0,12},{4,8},{8,4},{12,0},{1,13},{5,9},{9,5},{13,1},{2,14},{6,10},... | collective-permute-start | bytes 884744 | tf_op jit(solution)/shard_map/ppermute | solution.py:144
  33.1 12.7 %collective-permute-start.5 = (bf16[192,768]{1,0:T(8,128)(2,1)S(1)}, bf16[192,768]{1,0:T(8,128)(2,1)}, u32[]{:S(2)}, u32[]{:S(2)}) collective-permute-start(bf16[192,768]{1,0:T(8,128)(2,1)S(1)} %collective-permute-done.b0), channel_id=1, source_target_pairs={{0,4},{4,0},{8,12},{12,8},{1,5},{5,1},{9,13},{13,9},{2,6},{6,2},{1... | collective-permute-start | bytes 884744 | tf_op jit(solution)/shard_map/ppermute | solution.py:145
  34.9 20.3 %copy-start.2 = (bf16[6,640,128]{2,1,0:T(8,128)(2,1)}, bf16[6,640,128]{2,1,0:T(8,128)(2,1)S(1)}, u32[]{:S(2)}) copy-start(bf16[6,640,128]{2,1,0:T(8,128)(2,1)S(1)} %collective-permute-done.2.other.same) | copy-start | bytes 2949124
  34.9 34.7 %collective-permute-start.16 = (bf16[6,640,128]{2,1,0:T(8,128)(2,1)S(1)}, bf16[6,640,128]{2,1,0:T(8,128)(2,1)S(1)}, u32[]{:S(2)}, u32[]{:S(2)}) collective-permute-start(bf16[6,640,128]{2,1,0:T(8,128)(2,1)S(1)} %collective-permute-done.2.other.same), channel_id=1, source_target_pairs={{0,1},{1,0},{2,3},{3,2},{4,5},{5,4},{6,7},{7,6},{8,9},{9,8},{10,11... | collective-permute-start | bytes 2949128 | tf_op jit(solution)/shard_map/ppermute | solution.py:137
  35.0 8.6 %collective-permute-start.9 = (bf16[96,768]{1,0:T(8,128)(2,1)S(1)}, bf16[96,768]{1,0:T(8,128)(2,1)S(1)}, u32[]{:S(2)}, u32[]{:S(2)}) collective-permute-start(bf16[96,768]{1,0:T(8,128)(2,1)S(1)} %slice.8), channel_id=1, source_target_pairs={{0,8},{4,12},{8,0},{12,4},{1,9},{5,13},{9,1},{13,5},{2,10},{6,14},... | collective-permute-start | bytes 442376 | tf_op jit(solution)/shard_map/ppermute | solution.py:148
  37.7 6.6 %collective-permute-start.10 = (bf16[96,768]{1,0:T(8,128)(2,1)S(1)}, bf16[96,768]{1,0:T(8,128)(2,1)S(1)}, u32[]{:S(2)}, u32[]{:S(2)}) collective-permute-start(bf16[96,768]{1,0:T(8,128)(2,1)S(1)} %slice.9), channel_id=1, source_target_pairs={{0,2},{2,0},{1,3},{3,1},{4,6},{6,4},{5,7},{7,5},{8,10},{10,8},{9,1... | collective-permute-start | bytes 442376 | tf_op jit(solution)/shard_map/ppermute | solution.py:148
  39.2 6.8 %collective-permute-start.1 = (bf16[192,768]{1,0:T(8,128)(2,1)S(1)}, bf16[192,768]{1,0:T(8,128)(2,1)S(1)}, u32[]{:S(2)}, u32[]{:S(2)}) collective-permute-start(bf16[192,768]{1,0:T(8,128)(2,1)S(1)} %collective-permute-done.b0), channel_id=1, source_target_pairs={{0,1},{1,0},{2,3},{3,2},{4,5},{5,4},{6,7},{7,6},{8,9},{9,8},{10,11... | collective-permute-start | bytes 884744 | tf_op jit(solution)/shard_map/ppermute | solution.py:137
  43.6 3.5 %collective-permute-start.4 = (bf16[192,768]{1,0:T(8,128)(2,1)S(1)}, bf16[192,768]{1,0:T(8,128)(2,1)S(1)}, u32[]{:S(2)}, u32[]{:S(2)}) collective-permute-start(bf16[192,768]{1,0:T(8,128)(2,1)S(1)} %collective-permute-done.3.a0), channel_id=1, source_target_pairs={{0,1},{1,0},{2,3},{3,2},{4,5},{5,4},{6,7},{7,6},{8,9},{9,8},{10,11... | collective-permute-start | bytes 884744 | tf_op jit(solution)/shard_map/ppermute | solution.py:137
  43.6 0.7 copy-start.5
  44.3 9.7 %collective-permute-start.14 = (bf16[192,768]{1,0:T(8,128)(2,1)}, bf16[192,768]{1,0:T(8,128)(2,1)}, u32[]{:S(2)}, u32[]{:S(2)}) collective-permute-start(bf16[192,768]{1,0:T(8,128)(2,1)} %collective-permute-done.12.a0), channel_id=1, source_target_pairs={{0,2},{2,0},{1,3},{3,1},{4,6},{6,4},{5,7},{7,5},{8,10},{10,8},{9,1... | collective-permute-start | bytes 884744 | tf_op jit(solution)/shard_map/ppermute | solution.py:150
  45.8 8.2 %collective-permute-start.6 = (bf16[192,768]{1,0:T(8,128)(2,1)}, bf16[192,768]{1,0:T(8,128)(2,1)}, u32[]{:S(2)}, u32[]{:S(2)}) collective-permute-start(bf16[192,768]{1,0:T(8,128)(2,1)} %collective-permute-done.5.b0), channel_id=1, source_target_pairs={{0,1},{1,0},{2,3},{3,2},{4,5},{5,4},{6,7},{7,6},{8,9},{9,8},{10,11... | collective-permute-start | bytes 884744 | tf_op jit(solution)/shard_map/ppermute | solution.py:137
  46.1 0.7 copy-start.7
  46.8 18.1 %collective-permute-start.8 = (bf16[192,768]{1,0:T(8,128)(2,1)S(1)}, bf16[192,768]{1,0:T(8,128)(2,1)}, u32[]{:S(2)}, u32[]{:S(2)}) collective-permute-start(bf16[192,768]{1,0:T(8,128)(2,1)S(1)} %collective-permute-done.7.a0), channel_id=1, source_target_pairs={{0,1},{1,0},{2,3},{3,2},{4,5},{5,4},{6,7},{7,6},{8,9},{9,8},{10,11... | collective-permute-start | bytes 884744 | tf_op jit(solution)/shard_map/ppermute | solution.py:137
  47.8 17.1 %collective-permute-start.11 = (bf16[192,768]{1,0:T(8,128)(2,1)S(1)}, bf16[192,768]{1,0:T(8,128)(2,1)}, u32[]{:S(2)}, u32[]{:S(2)}) collective-permute-start(bf16[192,768]{1,0:T(8,128)(2,1)S(1)} %constant_dynamic-update-slice_fusion.b0), channel_id=1, source_target_pairs={{0,1},{1,0},{2,3},{3,2},{4,5},{5,4},{6,7},{7,6},{8,9},{9,8},{10,11... | collective-permute-start | bytes 884744 | tf_op jit(solution)/shard_map/ppermute | solution.py:137
  54.0 13.0 %collective-permute-start.13 = (bf16[192,768]{1,0:T(8,128)(2,1)}, bf16[192,768]{1,0:T(8,128)(2,1)}, u32[]{:S(2)}, u32[]{:S(2)}) collective-permute-start(bf16[192,768]{1,0:T(8,128)(2,1)} %collective-permute-done.12.a0), channel_id=1, source_target_pairs={{0,1},{1,0},{2,3},{3,2},{4,5},{5,4},{6,7},{7,6},{8,9},{9,8},{10,11... | collective-permute-start | bytes 884744 | tf_op jit(solution)/shard_map/ppermute | solution.py:137
  54.0 13.1 %collective-permute-start.15 = (bf16[192,768]{1,0:T(8,128)(2,1)}, bf16[192,768]{1,0:T(8,128)(2,1)}, u32[]{:S(2)}, u32[]{:S(2)}) collective-permute-start(bf16[192,768]{1,0:T(8,128)(2,1)} %collective-permute-done.14.b0), channel_id=1, source_target_pairs={{0,1},{1,0},{2,3},{3,2},{4,5},{5,4},{6,7},{7,6},{8,9},{9,8},{10,11... | collective-permute-start | bytes 884744 | tf_op jit(solution)/shard_map/ppermute | solution.py:137
  59.0 1.7 %copy-start = (bf16[1536,768]{1,0:T(8,128)(2,1)S(1)}, bf16[1536,768]{1,0:T(8,128)(2,1)}, u32[]{:S(2)}) copy-start(bf16[1536,768]{1,0:T(8,128)(2,1)} %spread.1) | copy-start | bytes 7077892
  60.6 1.0 %copy-start.8 = (bf16[192,768]{1,0:T(8,128)(2,1)S(1)}, bf16[192,768]{1,0:T(8,128)(2,1)}, u32[]{:S(2)}) copy-start(bf16[192,768]{1,0:T(8,128)(2,1)} %copy-done.7) | copy-start | bytes 884740
  61.6 1.1 %copy-start.6 = (bf16[192,768]{1,0:T(8,128)(2,1)S(1)}, bf16[192,768]{1,0:T(8,128)(2,1)}, u32[]{:S(2)}) copy-start(bf16[192,768]{1,0:T(8,128)(2,1)} %copy-done.5) | copy-start | bytes 884740
  61.6 1.1 %copy-start.10 = (bf16[192,768]{1,0:T(8,128)(2,1)S(1)}, bf16[192,768]{1,0:T(8,128)(2,1)}, u32[]{:S(2)}) copy-start(bf16[192,768]{1,0:T(8,128)(2,1)} %copy-done.9) | copy-start | bytes 884740
  67.0 2.6 %copy-start.1 = (bf16[6,640,256]{2,1,0:T(8,128)(2,1)S(1)}, bf16[6,640,256]{2,1,0:T(8,128)(2,1)}, u32[]{:S(2)}) copy-start(bf16[6,640,256]{2,1,0:T(8,128)(2,1)} %panel.1) | copy-start | bytes 5898244
  67.0 2.6 %copy-start.3 = (bf16[6,640,128]{2,1,0:T(8,128)(2,1)S(1)}, bf16[6,640,128]{2,1,0:T(8,128)(2,1)}, u32[]{:S(2)}) copy-start(bf16[6,640,128]{2,1,0:T(8,128)(2,1)} %copy-done.2) | copy-start | bytes 2949124
  67.0 2.6 %copy-start.4 = (bf16[6,256,128]{2,1,0:T(8,128)(2,1)S(1)}, bf16[6,256,128]{2,1,0:T(8,128)(2,1)}, u32[]{:S(2)}) copy-start(bf16[6,256,128]{2,1,0:T(8,128)(2,1)} %dinv.1) | copy-start | bytes 1179652
  67.0 2.6 %copy-start.11 = (s32[6,5]{1,0:T(8,128)S(1)}, s32[6,5]{1,0:T(8,128)}, u32[]{:S(2)}) copy-start(s32[6,5]{1,0:T(8,128)} %pat.3) | copy-start | bytes 364
  67.1 2.6 %copy-start.12 = (s32[3]{0:T(128)S(1)}, s32[3]{0:T(128)}, u32[]{:S(2)}) copy-start(s32[3]{0:T(128)} %pad_add_fusion.ids) | copy-start | bytes 40
  67.1 2.6 %copy-start.13 = (s32[6]{0:T(128)S(1)}, s32[6]{0:T(128)}, u32[]{:S(2)}) copy-start(s32[6]{0:T(128)} %widths.1) | copy-start | bytes 76
  (1 other events, 0.7 us)

commit v2 on v0

v2 whole, which is shorter than its diff:
```python
import jax
import jax.numpy as jnp
from jax import lax
from jax.experimental import pallas as pl
from jax.experimental.pallas import tpu as pltpu
from jax.sharding import PartitionSpec as P

SWAP = [(0, 1), (1, 0)]
F32 = jnp.float32
BF16 = jnp.bfloat16


def generic(parent_inverse, panel, diag_inverse, pattern, widths):
    block_size = panel.shape[2]
    half_cols = block_size // lax.axis_size("sub")
    sub_idx = lax.axis_index("sub")
    col_idx = lax.axis_index("col")
    col_mask = jnp.arange(block_size)[None, :] < widths[:, None]
    masked = panel * col_mask[:, None, :].astype(BF16)
    half_panel = lax.dynamic_slice_in_dim(masked, sub_idx * half_cols, half_cols, 2)
    full_panel = lax.all_gather(half_panel, "col", axis=1, tiled=True)
    columns = lax.all_gather(parent_inverse, "row", axis=0, tiled=True)
    pat_blocks = pattern.shape[1]
    local_blocks = columns.shape[1] // block_size
    anc_count = columns.shape[0] // block_size
    blocks_all = columns.reshape(anc_count, block_size, columns.shape[1])
    owned_ids = col_idx * local_blocks + jnp.arange(local_blocks, dtype=jnp.int32)

    def one_child(child_items):
        chosen, slab_cols = child_items
        sel_rows = jnp.take(blocks_all, chosen, axis=0).reshape(pat_blocks * block_size, columns.shape[1])
        onehot = (owned_ids[:, None] == chosen[None, :]).astype(BF16)
        slab = slab_cols.reshape(pat_blocks, block_size, half_cols)
        placed = jnp.einsum("km,mbc->kbc", onehot, slab, preferred_element_type=F32)
        placed = placed.astype(BF16).reshape(local_blocks * block_size, half_cols)
        return jnp.dot(sel_rows, placed, preferred_element_type=F32)

    partial_value = lax.map(one_child, (pattern, full_panel))
    summed = lax.psum_scatter(partial_value, "col", scatter_dimension=1, tiled=True)
    off_block = (-summed).astype(BF16)
    diag_terms = jnp.einsum("jrb,jrc->jbc", masked, off_block, preferred_element_type=F32)
    diag_total = lax.psum(diag_terms, "col")
    mask_half = lax.dynamic_slice_in_dim(col_mask, sub_idx * half_cols, half_cols, 1)
    diag_mask = (col_mask[:, :, None] & mask_half[:, None, :]).astype(F32)
    diag_block = (diag_inverse.astype(F32) * diag_mask - diag_total).astype(BF16)
    return (off_block, diag_block)


def pack_kernel(ids, parent, panel, tile, half_panel, sems):
    s = ids[2]
    half, lane = tile.shape[0], half_panel.shape[2]
    copies = [
        pltpu.make_async_copy(parent.at[pl.ds(pl.multiple_of(s * half, 64), half), :], tile, sems.at[0]),
        pltpu.make_async_copy(panel.at[:, :, pl.ds(pl.multiple_of(s * lane, 128), lane)], half_panel, sems.at[1]),
    ]
    for copy in copies:
        copy.start()
    for copy in copies:
        copy.wait()


def spread_kernel(ids, pat, panel, same, cross, out, full):
    children, rows, width = panel.shape
    lane = width // 2
    c, s = ids[1], ids[2]
    blocks = out.shape[0] // width
    per_col = blocks // 2
    chunks = rows // 128
    low = pl.ds(pl.multiple_of(s * lane, 128), lane)
    out[...] = jnp.zeros_like(out)
    full[...] = jnp.zeros_like(full)
    for j in range(children):
        for q in range(2 * chunks):
            g = (c if q < chunks else 1 - c) * chunks + q % chunks
            anc = pat[j, g // 2]
            side = jnp.where(anc // per_col == c, 0, per_col)
            start = (side + anc % per_col) * width + (g % 2) * 128
            here = pl.ds(pl.multiple_of(start, 128), 128)
            band = slice(q % chunks * 128, (q % chunks + 1) * 128)
            mine = slice(j * lane, (j + 1) * lane)
            if q < chunks:
                out[here, mine] = panel[j, band, low]
                full[here, j * width : (j + 1) * width] = panel[j, band, :]
            else:
                block = same[j, band, :]
                out[here, mine] = block
                full[here, pl.ds(pl.multiple_of(j * width + s * lane, 128), lane)] = block
                full[here, pl.ds(pl.multiple_of(j * width + (1 - s) * lane, 128), lane)] = cross[j, band, :]


def halves(ids, half):
    s = ids[2]
    return [pl.ds(pl.multiple_of(side * half, 64), half) for side in (s, 1 - s)]


def early_kernel(ids, parent, a, a_sib, spread, y0, acc, rows):
    tall, wide = parent.shape
    half = tall // 2
    own, sib = halves(ids, half)
    rows[:, :wide] = parent[...]
    for here, piece in ((own, a), (sib, a_sib)):
        rows[here, wide:] = piece[:half, :]
    y0[...] = (-jnp.dot(rows[...], spread[...], preferred_element_type=F32)).astype(BF16)
    for k in range(1, 4):
        for here, piece in ((own, a), (sib, a_sib)):
            rows[here, :wide] = piece[k * half : (k + 1) * half, :]
        acc[(k - 1) * tall : k * tall, :] = jnp.dot(rows[:, :wide], spread[:wide, :], preferred_element_type=F32)


def final_kernel(ids, pat, widths, b, b_sib, spread, full, y0, acc, dinv, off_out, diag_out, rows, y_all):
    r, c, s = ids[0], ids[1], ids[2]
    children, width, lane = dinv.shape
    tall, wide = rows.shape
    half = tall // 2
    total = y_all.shape[0]
    own, sib = halves(ids, half)

    def place(k, y):
        at = lax.rem(jnp.bitwise_xor(r, k) * tall + c * wide, total)
        y_all[pl.ds(pl.multiple_of(at, 128), tall), :] = y

    place(0, y0[...])
    for k in range(1, 4):
        for here, piece in ((own, b), (sib, b_sib)):
            rows[here, :] = piece[(k - 1) * half : k * half, :]
        term = jnp.dot(rows[...], spread[wide:, :], preferred_element_type=F32)
        place(k, (-(acc[(k - 1) * tall : k * tall, :] + term)).astype(BF16))
    chunks = off_out.shape[1] // 128
    for j in range(children):
        w = widths[j]
        mine = slice(j * lane, (j + 1) * lane)
        keep_b = s * lane + lax.broadcasted_iota(jnp.int32, (1, lane), 1) < w
        keep_a = lax.broadcasted_iota(jnp.int32, (width, 1), 0) < w
        for q in range(chunks):
            g = c * chunks + q
            start = lax.rem(pat[j, g // 2] * width + (g % 2) * 128 + c * wide, total)
            got = y_all[pl.ds(pl.multiple_of(start, 128), 128), mine]
            off_out[j, q * 128 : (q + 1) * 128, :] = jnp.where(keep_b, got, jnp.zeros_like(got))
        terms = lax.dot_general(
            y_all[:, mine], full[:, j * width : (j + 1) * width], (((0,), (0,)), ((), ())), preferred_element_type=F32
        )
        diag = dinv[j].astype(F32) - terms.T
        diag_out[j] = jnp.where(keep_a & keep_b, diag, 0.0).astype(BF16)


VMEM = pl.BlockSpec(memory_space=pltpu.VMEM)
SMEM = pl.BlockSpec(memory_space=pltpu.SMEM)
ANY = pl.BlockSpec(memory_space=pl.ANY)
FREE = pl.CostEstimate(flops=0, bytes_accessed=0, transcendentals=0)


def gathered(parent, panel, diag_inverse, pattern, widths):
    r, c, s = lax.axis_index("row"), lax.axis_index("col"), lax.axis_index("sub")
    children, rows, width = panel.shape
    lane = width // 2
    tall, wide = parent.shape
    half = tall // 2
    lanes = children * lane
    ids = jnp.stack([r, c, s]).astype(jnp.int32)

    def xor(d):
        return [(i, i ^ d) for i in range(4)]

    def sib(x):
        return lax.ppermute(x, "sub", SWAP)

    def params(mib):
        return pltpu.CompilerParams(vmem_limit_bytes=mib << 20)

    tile, mine = pl.pallas_call(
        pack_kernel,
        out_shape=(
            jax.ShapeDtypeStruct((half, wide), BF16),
            jax.ShapeDtypeStruct((children, rows, lane), BF16),
        ),
        in_specs=[SMEM, ANY, ANY],
        out_specs=(VMEM, VMEM),
        scratch_shapes=[pltpu.SemaphoreType.DMA((2,))],
        cost_estimate=FREE,
        compiler_params=params(8),
        name="pack",
    )(ids, parent, panel)
    a1, a2, a3 = (lax.ppermute(tile, "row", xor(d)) for d in (1, 2, 3))
    b0 = lax.ppermute(tile, "col", SWAP)
    same = lax.ppermute(mine, "col", SWAP)
    a1, a2, a3, b0 = lax.optimization_barrier((a1, a2, a3, b0))
    cut = half // 2
    b1 = lax.ppermute(b0, "row", xor(1))
    b3z = lax.ppermute(b0[:cut], "row", xor(3))
    b23 = lax.ppermute(jnp.concatenate([a2, a3[cut:]]), "col", SWAP)
    a = jnp.concatenate([b0, a1, a2, a3])
    a_sib = sib(a)
    cross = sib(same)

    spread, full = pl.pallas_call(
        spread_kernel,
        out_shape=(
            jax.ShapeDtypeStruct((2 * wide, lanes), BF16),
            jax.ShapeDtypeStruct((2 * wide, 2 * lanes), BF16),
        ),
        in_specs=[SMEM, SMEM] + [VMEM] * 3,
        out_specs=(VMEM, VMEM),
        cost_estimate=FREE,
        compiler_params=params(12),
        name="spread",
    )(ids, pattern, panel, same, cross)
    y0, acc = pl.pallas_call(
        early_kernel,
        out_shape=(
            jax.ShapeDtypeStruct((tall, lanes), BF16),
            jax.ShapeDtypeStruct((3 * tall, lanes), F32),
        ),
        in_specs=[SMEM] + [VMEM] * 4,
        out_specs=(VMEM, VMEM),
        scratch_shapes=[pltpu.VMEM((tall, 2 * wide), BF16)],
        cost_estimate=FREE,
        compiler_params=params(12),
        name="early",
    )(ids, parent, a, a_sib, spread)
    b1, b3z, b23, y0, acc = lax.optimization_barrier((b1, b3z, b23, y0, acc))
    b = jnp.concatenate([b1, b23[:half], b3z, b23[half:]])
    b_sib = sib(b)
    return pl.pallas_call(
        final_kernel,
        out_shape=(
            jax.ShapeDtypeStruct((children, rows, lane), BF16),
            jax.ShapeDtypeStruct((children, width, lane), BF16),
        ),
        in_specs=[SMEM, SMEM, SMEM] + [VMEM] * 7,
        out_specs=(VMEM, VMEM),
        scratch_shapes=[
            pltpu.VMEM((tall, wide), BF16),
            pltpu.VMEM((4 * tall, lanes), BF16),
        ],
        cost_estimate=FREE,
        compiler_params=params(16),
        name="final",
    )(ids, pattern, widths, b, b_sib, spread, full, y0, acc, diag_inverse)


def solution(mesh):
    placed = (
        P(("pole", "row"), "col"),
        P(("pole", "row"), "col", None),
        P(("pole", "row"), None, "sub"),
        P("row", None),
        P("row"),
    )
    shape = dict(mesh.shape)
    fits = (shape["row"], shape["col"], shape["sub"]) == (4, 2, 2)
    return jax.shard_map(
        gathered if fits else generic,
        mesh=mesh,
        in_specs=placed,
        out_specs=(P(("pole", "row"), "col", "sub"), P(("pole", "row"), None, "sub")),
        check_vma=False,
    )
```

time: 239 us -> 59.1 us (0.25)
  waiting for transfers between devices: 172 us -> 30.7 us
  local copies, waits for them, and re-layouts: 22.7 us -> 2.78 us
  other arithmetic: 16.3 us -> 0.17 us
  starting transfers between devices: 0.16 us -> 13.7 us
  matrix products: 13.1 us -> 0 us
  between operations: 13.8 us -> 0.82 us
  Pallas kernels: 0 us -> 10.7 us
    all_gather x2 -> x0, waiting for transfers between devices: 85.8 us -> none  [the longest x1 52.1 us: local(): columns = lax.all_gather(parent_inverse, 'row', axis=0, tiled=True)]
    reduce_scatter x1 -> x0, waiting for transfers between devices: 50.9 us -> none  [local(): lax.psum_scatter(partial_value, 'col', scatter_dimension=1, tiled=True)]
    psum x1 -> x0, waiting for transfers between devices: 34.5 us -> none  [local(): diag_total = lax.psum(diag_terms, 'col')]
    ppermute x0 -> x11, waiting for transfers between devices: none -> 30.7 us  [the longest x1 23.4 us: gathered(): b0 = lax.ppermute(tile, 'col', SWAP)]
    gather x6 -> x0, local copies, waits for them, and re-layouts: 14 us -> none  [one_child(): jnp.take(blocks_all, chosen, axis=0)]
    ppermute x0 -> x11, starting transfers between devices: none -> 13.7 us  [the longest x3 4.62 us: gathered(): a1, a2, a3 = (lax.ppermute(tile, 'row', xor(d)) for d in (1, 2, 3))]
    dot_general x13 -> x0, matrix products: 13.1 us -> none  [the longest x6 9.24 us: one_child(): return jnp.dot(sel_rows, placed, preferred_element_type=jnp.float32)]
    pallas_call x0 -> x4, Pallas kernels: none -> 10.7 us  [the longest x1 4.52 us: gathered(): pl.pallas_call(final_kernel, out_shape=(jax.ShapeDtypeStruct((children, r...]
  transfers between devices with their start and end apart: 4 -> 11, of which waited for: 4 -> 4; matrix products, arithmetic and copies ran while one was open for 0% -> 0% of each run, Pallas kernels for 0% -> 9%
where the time goes in v2:
time: 59.1 us; the launch traced here: 58.9 us
  waiting for transfers between devices  30.7 us (52%)
  starting transfers between devices  13.7 us (23%)
  Pallas kernels  10.7 us (18%)
  local copies, waits for them, and re-layouts  2.78 us (5%)
  between operations  0.82 us (1%)
    ppermute x1, waiting for transfers between devices, gathered(): b0 = lax.ppermute(tile, 'col', SWAP)  23.4 us
    ppermute x3, starting transfers between devices, gathered(): a1, a2, a3 = (lax.ppermute(tile, 'row', xor(d)) for d in (1, 2, 3))  4.62 us
    pallas_call x1, Pallas kernels, gathered(): pl.pallas_call(final_kernel, out_shape=(jax.ShapeDtypeStruct((children, r...  4.52 us
    ppermute x1, waiting for transfers between devices, gathered(): b3z = lax.ppermute(b0[:cut], 'row', xor(3))  4.3 us
    pallas_call x1, Pallas kernels, gathered(): pl.pallas_call(early_kernel, out_shape=(jax.ShapeDtypeStruct((tall, lanes...  3.09 us
    ppermute x1, starting transfers between devices, gathered(): same = lax.ppermute(mine, 'col', SWAP)  3 us
    unnamed x17, local copies, waits for them, and re-layouts  2.71 us
    ppermute x1, starting transfers between devices, gathered(): b3z = lax.ppermute(b0[:cut], 'row', xor(3))  2.54 us
  transfers between devices with their start and end apart: 11, of which 4 were waited for; matrix products, arithmetic and copies ran while one was open for 0% of the time, Pallas kernels for 9%

profile of v2, /device:TPU:0, one launch (start us, length us, event | category | flops | bytes accessed | tf_op | source)
XLA Modules:
  0.0 58.9 jit_solution(13612913385556803907)
XLA Ops:
  0.6 0.1 pad_add_fusion.ids
  0.7 1.5 %copy-done = bf16[6,640,256]{2,1,0:T(8,128)(2,1)S(1)} copy-done((bf16[6,640,256]{2,1,0:T(8,128)(2,1)S(1)}, bf16[6,640,256]{2,1,0:T(8,128)(2,1)}, u32[]{:S(2)}) %copy-start) | copy-done | bytes 1966104
  2.3 1.1 %copy-done.2 = bf16[384,768]{1,0:T(8,128)(2,1)S(1)} copy-done((bf16[384,768]{1,0:T(8,128)(2,1)S(1)}, bf16[384,768]{1,0:T(8,128)(2,1)}, u32[]{:S(2)}) %copy-start.2) | copy-done | bytes 589848
  3.3 0.8 %pack.1 = (bf16[192,768]{1,0:T(8,128)(2,1)S(1)}, bf16[6,640,128]{2,1,0:T(8,128)(2,1)S(1)}) custom-call(s32[3]{0:T(128)S(1)} %pad_add_fusion.ids, bf16[384,768]{1,0:T(8,128)(2,1)S(1)} %copy-done.2, bf16[6,640,256]{2,1,0:T(8,128)(2,1)S(1)} %copy-done), custom_call_target="tpu_custom_call" | custom-call | tf_op jit(solution)/shard_map/pack/pallas_call | solution.py:170
  4.1 3.0 %collective-permute-start.8 = (bf16[6,640,128]{2,1,0:T(8,128)(2,1)S(1)}, bf16[6,640,128]{2,1,0:T(8,128)(2,1)S(1)}, u32[]{:S(2)}, u32[]{:S(2)}) collective-permute-start(bf16[6,640,128]{2,1,0:T(8,128)(2,1)S(1)} %get-tuple-element.22), channel_id=1, source_target_pairs={{0,2},{2,0},{1,3},{3,1},{4,6},{6,4},{5,7},{7,5},{8,10},{10,8},{9,1... | collective-permute-start | bytes 2949128 | tf_op jit(solution)/shard_map/ppermute | solution.py:185
  7.1 0.1 collective-permute-start.3
  7.2 4.1 %collective-permute-start.2 = (bf16[192,768]{1,0:T(8,128)(2,1)S(1)}, bf16[192,768]{1,0:T(8,128)(2,1)S(1)}, u32[]{:S(2)}, u32[]{:S(2)}) collective-permute-start(bf16[192,768]{1,0:T(8,128)(2,1)S(1)} %get-tuple-element.17), channel_id=1, source_target_pairs={{0,12},{4,8},{8,4},{12,0},{1,13},{5,9},{9,5},{13,1},{2,14},{6,10},... | collective-permute-start | bytes 884744 | tf_op jit(solution)/shard_map/ppermute | solution.py:183
  11.3 0.0 collective-permute-start.1
  11.3 0.6 collective-permute-start
  11.8 23.4 %collective-permute-done.3 = bf16[192,768]{1,0:T(8,128)(2,1)S(1)} collective-permute-done((bf16[192,768]{1,0:T(8,128)(2,1)S(1)}, bf16[192,768]{1,0:T(8,128)(2,1)S(1)}, u32[]{:S(2)}, u32[]{:S(2)}) %collective-permute-start.3) | collective-permute-done | bytes 294944 | tf_op jit(solution)/shard_map/ppermute | solution.py:184
  35.2 0.0 collective-permute-done.2
  35.2 0.6 %collective-permute-done.1 = bf16[192,768]{1,0:T(8,128)(2,1)S(1)} collective-permute-done((bf16[192,768]{1,0:T(8,128)(2,1)S(1)}, bf16[192,768]{1,0:T(8,128)(2,1)S(1)}, u32[]{:S(2)}, u32[]{:S(2)}) %collective-permute-start.1) | collective-permute-done | bytes 294944 | tf_op jit(solution)/shard_map/ppermute | solution.py:183
  35.9 0.0 copy-start.1
  35.9 0.0 copy-start.5
  36.0 0.1 collective-permute-start.7
  36.0 0.0 collective-permute-done.8.same
  36.1 0.5 collective-permute-start.9
  36.6 1.6 %collective-permute-start.6 = (bf16[288,768]{1,0:T(8,128)(2,1)S(1)}, bf16[288,768]{1,0:T(8,128)(2,1)S(1)}, u32[]{:S(2)}, u32[]{:S(2)}) collective-permute-start(bf16[288,768]{1,0:T(8,128)(2,1)S(1)} %pad_maximum_fusion.1), channel_id=1, source_target_pairs={{0,2},{2,0},{1,3},{3,1},{4,6},{6,4},{5,7},{7,5},{8,10},{10,8},{9,1... | collective-permute-start | bytes 1327112 | tf_op jit(solution)/shard_map/ppermute | solution.py:190
  38.2 1.2 %collective-permute-start.4 = (bf16[192,768]{1,0:T(8,128)(2,1)S(1)}, bf16[192,768]{1,0:T(8,128)(2,1)S(1)}, u32[]{:S(2)}, u32[]{:S(2)}) collective-permute-start(bf16[192,768]{1,0:T(8,128)(2,1)S(1)} %collective-permute-done.3), channel_id=1, source_target_pairs={{0,4},{4,0},{8,12},{12,8},{1,5},{5,1},{9,13},{13,9},{2,6},{6,2},{1... | collective-permute-start | bytes 884744 | tf_op jit(solution)/shard_map/ppermute | solution.py:188
  39.4 0.0 copy-start.3
  39.4 2.5 %collective-permute-start.5 = (bf16[96,768]{1,0:T(8,128)(2,1)S(1)}, bf16[96,768]{1,0:T(8,128)(2,1)S(1)}, u32[]{:S(2)}, u32[]{:S(2)}) collective-permute-start(bf16[96,768]{1,0:T(8,128)(2,1)S(1)} %slice.12), channel_id=1, source_target_pairs={{0,12},{4,8},{8,4},{12,0},{1,13},{5,9},{9,5},{13,1},{2,14},{6,10},... | collective-permute-start | bytes 442376 | tf_op jit(solution)/shard_map/ppermute | solution.py:189
  42.0 2.3 %spread.1 = (bf16[1536,768]{1,0:T(8,128)(2,1)S(1)}, bf16[1536,1536]{1,0:T(8,128)(2,1)S(1)}) custom-call(s32[3]{0:T(128)S(1)} %pad_add_fusion.ids, s32[6,5]{1,0:T(8,128)S(1)} %copy-done.5, bf16[6,640,256]{2,1,0:T(8,128)(2,1)S(1)} %copy-done.1, bf16[6,640,128]{2,1,0:T(8,128)(2,1)S(1)} %collective-permute-done.8.same, ...), custom_call_target="tpu_custom_call" | custom-call | tf_op jit(solution)/shard_map/spread/pallas_call | solution.py:195
  44.3 0.0 collective-permute-done.7.a_sib
  44.3 3.1 %early.1 = (bf16[384,768]{1,0:T(8,128)(2,1)S(1)}, f32[1152,768]{1,0:T(8,128)S(1)}) custom-call(s32[3]{0:T(128)S(1)} %pad_add_fusion.ids, bf16[384,768]{1,0:T(8,128)(2,1)S(1)} %copy-done.3, bf16[768,768]{1,0:T(8,128)(2,1)S(1)} %constant_dynamic-update-slice_fusion.a, bf16[768,768]{1,0:T(8,128)(2,1)S(1)} %collective-permute-done.7.a_sib, ...), custom_call_target="tpu_custom_call" | custom-call | tf_op jit(solution)/shard_map/early/pallas_call | solution.py:207
  47.4 4.3 %collective-permute-done.5 = bf16[96,768]{1,0:T(8,128)(2,1)S(1)} collective-permute-done((bf16[96,768]{1,0:T(8,128)(2,1)S(1)}, bf16[96,768]{1,0:T(8,128)(2,1)S(1)}, u32[]{:S(2)}, u32[]{:S(2)}) %collective-permute-start.5) | collective-permute-done | bytes 147488 | tf_op jit(solution)/shard_map/ppermute | solution.py:189
  51.7 0.0 collective-permute-done.6
  51.7 0.0 copy-start.4
  51.7 0.0 copy-start.6
  51.8 0.1 pad_maximum_fusion.b
  51.8 0.1 collective-permute-start.10
  51.9 2.4 %collective-permute-done.10.b_sib = bf16[576,768]{1,0:T(8,128)(2,1)S(1)} collective-permute-done((bf16[576,768]{1,0:T(8,128)(2,1)S(1)}, bf16[576,768]{1,0:T(8,128)(2,1)S(1)}, u32[]{:S(2)}, u32[]{:S(2)}) %collective-permute-start.10) | collective-permute-done | bytes 884768 | tf_op jit(solution)/shard_map/ppermute | solution.py:165
  54.3 4.5 %final.1 = (bf16[6,640,128]{2,1,0:T(8,128)(2,1)}, bf16[6,256,128]{2,1,0:T(8,128)(2,1)}) custom-call(s32[3]{0:T(128)S(1)} %pad_add_fusion.ids, s32[6,5]{1,0:T(8,128)S(1)} %copy-done.5, s32[6]{0:T(128)S(1)} %copy-done.6, bf16[576,768]{1,0:T(8,128)(2,1)S(1)} %pad_maximum_fusion.b, bf16[576,768]{1,0:T(8,128)(2,1)S(1)} %collective-permute-done.10.b_sib, ...), custom_call_target="tpu_custom_call" | custom-call | tf_op jit(solution)/shard_map/final/pallas_call | solution.py:223
  (19 shorter events, 0.2 us)
Async XLA Ops:
  0.7 1.5 %copy-start = (bf16[6,640,256]{2,1,0:T(8,128)(2,1)S(1)}, bf16[6,640,256]{2,1,0:T(8,128)(2,1)}, u32[]{:S(2)}) copy-start(bf16[6,640,256]{2,1,0:T(8,128)(2,1)} %panel.3) | copy-start | bytes 5898244
  2.3 1.1 %copy-start.2 = (bf16[384,768]{1,0:T(8,128)(2,1)S(1)}, bf16[384,768]{1,0:T(8,128)(2,1)}, u32[]{:S(2)}) copy-start(bf16[384,768]{1,0:T(8,128)(2,1)} %parent.3) | copy-start | bytes 1769476
  4.1 31.9 %collective-permute-start.8 = (bf16[6,640,128]{2,1,0:T(8,128)(2,1)S(1)}, bf16[6,640,128]{2,1,0:T(8,128)(2,1)S(1)}, u32[]{:S(2)}, u32[]{:S(2)}) collective-permute-start(bf16[6,640,128]{2,1,0:T(8,128)(2,1)S(1)} %get-tuple-element.22), channel_id=1, source_target_pairs={{0,2},{2,0},{1,3},{3,1},{4,6},{6,4},{5,7},{7,5},{8,10},{10,8},{9,1... | collective-permute-start | bytes 2949128 | tf_op jit(solution)/shard_map/ppermute | solution.py:185
  7.1 28.1 %collective-permute-start.3 = (bf16[192,768]{1,0:T(8,128)(2,1)S(1)}, bf16[192,768]{1,0:T(8,128)(2,1)S(1)}, u32[]{:S(2)}, u32[]{:S(2)}) collective-permute-start(bf16[192,768]{1,0:T(8,128)(2,1)S(1)} %get-tuple-element.17), channel_id=1, source_target_pairs={{0,2},{2,0},{1,3},{3,1},{4,6},{6,4},{5,7},{7,5},{8,10},{10,8},{9,1... | collective-permute-start | bytes 884744 | tf_op jit(solution)/shard_map/ppermute | solution.py:184
  7.2 28.0 %collective-permute-start.2 = (bf16[192,768]{1,0:T(8,128)(2,1)S(1)}, bf16[192,768]{1,0:T(8,128)(2,1)S(1)}, u32[]{:S(2)}, u32[]{:S(2)}) collective-permute-start(bf16[192,768]{1,0:T(8,128)(2,1)S(1)} %get-tuple-element.17), channel_id=1, source_target_pairs={{0,12},{4,8},{8,4},{12,0},{1,13},{5,9},{9,5},{13,1},{2,14},{6,10},... | collective-permute-start | bytes 884744 | tf_op jit(solution)/shard_map/ppermute | solution.py:183
  11.3 24.6 %collective-permute-start.1 = (bf16[192,768]{1,0:T(8,128)(2,1)S(1)}, bf16[192,768]{1,0:T(8,128)(2,1)S(1)}, u32[]{:S(2)}, u32[]{:S(2)}) collective-permute-start(bf16[192,768]{1,0:T(8,128)(2,1)S(1)} %get-tuple-element.17), channel_id=1, source_target_pairs={{0,8},{4,12},{8,0},{12,4},{1,9},{5,13},{9,1},{13,5},{2,10},{6,14},... | collective-permute-start | bytes 884744 | tf_op jit(solution)/shard_map/ppermute | solution.py:183
  11.3 24.6 %collective-permute-start = (bf16[192,768]{1,0:T(8,128)(2,1)S(1)}, bf16[192,768]{1,0:T(8,128)(2,1)S(1)}, u32[]{:S(2)}, u32[]{:S(2)}) collective-permute-start(bf16[192,768]{1,0:T(8,128)(2,1)S(1)} %get-tuple-element.17), channel_id=1, source_target_pairs={{0,4},{4,0},{8,12},{12,8},{1,5},{5,1},{9,13},{13,9},{2,6},{6,2},{1... | collective-permute-start | bytes 884744 | tf_op jit(solution)/shard_map/ppermute | solution.py:183
  35.9 6.0 %copy-start.1 = (bf16[6,640,256]{2,1,0:T(8,128)(2,1)S(1)}, bf16[6,640,256]{2,1,0:T(8,128)(2,1)}, u32[]{:S(2)}) copy-start(bf16[6,640,256]{2,1,0:T(8,128)(2,1)} %panel.3) | copy-start | bytes 5898244
  35.9 6.0 %copy-start.5 = (s32[6,5]{1,0:T(8,128)S(1)}, s32[6,5]{1,0:T(8,128)}, u32[]{:S(2)}) copy-start(s32[6,5]{1,0:T(8,128)} %pat.3) | copy-start | bytes 364
  36.0 8.3 %collective-permute-start.7 = (bf16[768,768]{1,0:T(8,128)(2,1)S(1)}, bf16[768,768]{1,0:T(8,128)(2,1)S(1)}, u32[]{:S(2)}, u32[]{:S(2)}) collective-permute-start(bf16[768,768]{1,0:T(8,128)(2,1)S(1)} %constant_dynamic-update-slice_fusion.a), channel_id=1, source_target_pairs={{0,1},{1,0},{2,3},{3,2},{4,5},{5,4},{6,7},{7,6},{8,9},{9,8},{10,11... | collective-permute-start | bytes 3538952 | tf_op jit(solution)/shard_map/ppermute | solution.py:165
  36.1 5.9 %collective-permute-start.9 = (bf16[6,640,128]{2,1,0:T(8,128)(2,1)S(1)}, bf16[6,640,128]{2,1,0:T(8,128)(2,1)S(1)}, u32[]{:S(2)}, u32[]{:S(2)}) collective-permute-start(bf16[6,640,128]{2,1,0:T(8,128)(2,1)S(1)} %collective-permute-done.8.same), channel_id=1, source_target_pairs={{0,1},{1,0},{2,3},{3,2},{4,5},{5,4},{6,7},{7,6},{8,9},{9,8},{10,11... | collective-permute-start | bytes 2949128 | tf_op jit(solution)/shard_map/ppermute | solution.py:165
  36.6 15.1 %collective-permute-start.6 = (bf16[288,768]{1,0:T(8,128)(2,1)S(1)}, bf16[288,768]{1,0:T(8,128)(2,1)S(1)}, u32[]{:S(2)}, u32[]{:S(2)}) collective-permute-start(bf16[288,768]{1,0:T(8,128)(2,1)S(1)} %pad_maximum_fusion.1), channel_id=1, source_target_pairs={{0,2},{2,0},{1,3},{3,1},{4,6},{6,4},{5,7},{7,5},{8,10},{10,8},{9,1... | collective-permute-start | bytes 1327112 | tf_op jit(solution)/shard_map/ppermute | solution.py:190
  38.2 13.5 %collective-permute-start.4 = (bf16[192,768]{1,0:T(8,128)(2,1)S(1)}, bf16[192,768]{1,0:T(8,128)(2,1)S(1)}, u32[]{:S(2)}, u32[]{:S(2)}) collective-permute-start(bf16[192,768]{1,0:T(8,128)(2,1)S(1)} %collective-permute-done.3), channel_id=1, source_target_pairs={{0,4},{4,0},{8,12},{12,8},{1,5},{5,1},{9,13},{13,9},{2,6},{6,2},{1... | collective-permute-start | bytes 884744 | tf_op jit(solution)/shard_map/ppermute | solution.py:188
  39.4 4.9 %copy-start.3 = (bf16[384,768]{1,0:T(8,128)(2,1)S(1)}, bf16[384,768]{1,0:T(8,128)(2,1)}, u32[]{:S(2)}) copy-start(bf16[384,768]{1,0:T(8,128)(2,1)} %parent.3) | copy-start | bytes 1769476
  39.4 12.3 %collective-permute-start.5 = (bf16[96,768]{1,0:T(8,128)(2,1)S(1)}, bf16[96,768]{1,0:T(8,128)(2,1)S(1)}, u32[]{:S(2)}, u32[]{:S(2)}) collective-permute-start(bf16[96,768]{1,0:T(8,128)(2,1)S(1)} %slice.12), channel_id=1, source_target_pairs={{0,12},{4,8},{8,4},{12,0},{1,13},{5,9},{9,5},{13,1},{2,14},{6,10},... | collective-permute-start | bytes 442376 | tf_op jit(solution)/shard_map/ppermute | solution.py:189
  51.7 2.6 %copy-start.4 = (bf16[6,256,128]{2,1,0:T(8,128)(2,1)S(1)}, bf16[6,256,128]{2,1,0:T(8,128)(2,1)}, u32[]{:S(2)}) copy-start(bf16[6,256,128]{2,1,0:T(8,128)(2,1)} %dinv.1) | copy-start | bytes 1179652
  51.7 2.6 %copy-start.6 = (s32[6]{0:T(128)S(1)}, s32[6]{0:T(128)}, u32[]{:S(2)}) copy-start(s32[6]{0:T(128)} %widths.1) | copy-start | bytes 76
  51.8 2.5 %collective-permute-start.10 = (bf16[576,768]{1,0:T(8,128)(2,1)S(1)}, bf16[576,768]{1,0:T(8,128)(2,1)S(1)}, u32[]{:S(2)}, u32[]{:S(2)}) collective-permute-start(bf16[576,768]{1,0:T(8,128)(2,1)S(1)} %pad_maximum_fusion.b), channel_id=1, source_target_pairs={{0,1},{1,0},{2,3},{3,2},{4,5},{5,4},{6,7},{7,6},{8,9},{9,8},{10,11... | collective-permute-start | bytes 2654216 | tf_op jit(solution)/shard_map/ppermute | solution.py:165

commit v3 on v2

v3 whole, which is shorter than its diff:
```python
import jax
import jax.numpy as jnp
from jax import lax
from jax.experimental import pallas as pl
from jax.experimental.pallas import tpu as pltpu
from jax.sharding import PartitionSpec as P

SWAP = [(0, 1), (1, 0)]
F32 = jnp.float32
BF16 = jnp.bfloat16


def generic(parent_inverse, panel, diag_inverse, pattern, widths):
    block_size = panel.shape[2]
    half_cols = block_size // lax.axis_size("sub")
    sub_idx = lax.axis_index("sub")
    col_idx = lax.axis_index("col")
    col_mask = jnp.arange(block_size)[None, :] < widths[:, None]
    masked = panel * col_mask[:, None, :].astype(BF16)
    half_panel = lax.dynamic_slice_in_dim(masked, sub_idx * half_cols, half_cols, 2)
    full_panel = lax.all_gather(half_panel, "col", axis=1, tiled=True)
    columns = lax.all_gather(parent_inverse, "row", axis=0, tiled=True)
    pat_blocks = pattern.shape[1]
    local_blocks = columns.shape[1] // block_size
    anc_count = columns.shape[0] // block_size
    blocks_all = columns.reshape(anc_count, block_size, columns.shape[1])
    owned_ids = col_idx * local_blocks + jnp.arange(local_blocks, dtype=jnp.int32)

    def one_child(child_items):
        chosen, slab_cols = child_items
        sel_rows = jnp.take(blocks_all, chosen, axis=0).reshape(pat_blocks * block_size, columns.shape[1])
        onehot = (owned_ids[:, None] == chosen[None, :]).astype(BF16)
        slab = slab_cols.reshape(pat_blocks, block_size, half_cols)
        placed = jnp.einsum("km,mbc->kbc", onehot, slab, preferred_element_type=F32)
        placed = placed.astype(BF16).reshape(local_blocks * block_size, half_cols)
        return jnp.dot(sel_rows, placed, preferred_element_type=F32)

    partial_value = lax.map(one_child, (pattern, full_panel))
    summed = lax.psum_scatter(partial_value, "col", scatter_dimension=1, tiled=True)
    off_block = (-summed).astype(BF16)
    diag_terms = jnp.einsum("jrb,jrc->jbc", masked, off_block, preferred_element_type=F32)
    diag_total = lax.psum(diag_terms, "col")
    mask_half = lax.dynamic_slice_in_dim(col_mask, sub_idx * half_cols, half_cols, 1)
    diag_mask = (col_mask[:, :, None] & mask_half[:, None, :]).astype(F32)
    diag_block = (diag_inverse.astype(F32) * diag_mask - diag_total).astype(BF16)
    return (off_block, diag_block)


def places(ids, pat, blocks, width, children, chunks):
    c = ids[1]
    per_col = blocks // 2
    for j in range(children):
        for q in range(2 * chunks):
            g = (c if q < chunks else 1 - c) * chunks + q % chunks
            anc = pat[j, g // 2]
            side = jnp.where(anc // per_col == c, 0, per_col)
            start = (side + anc % per_col) * width + (g % 2) * 128
            yield j, q, pl.ds(pl.multiple_of(start, 128), 128)


def spread_kernel(ids, pat, panel, same, out):
    children, rows, width = panel.shape
    lane = width // 2
    chunks = rows // 128
    low = pl.ds(pl.multiple_of(ids[2] * lane, 128), lane)
    out[...] = jnp.zeros_like(out)
    for j, q, here in places(ids, pat, out.shape[0] // width, width, children, chunks):
        mine = slice(j * lane, (j + 1) * lane)
        band = slice(q % chunks * 128, (q % chunks + 1) * 128)
        if q < chunks:
            out[here, mine] = panel[j, band, low]
        else:
            out[here, mine] = same[j, band, :]


def widen_kernel(ids, pat, panel, same, *refs):
    *cross, out = refs
    children, rows, width = panel.shape
    lane = width // 2
    s = ids[2]
    chunks = rows // 128
    out[...] = jnp.zeros_like(out)
    for j, q, here in places(ids, pat, out.shape[0] // width, width, children, chunks):
        band = slice(q % chunks * 128, (q % chunks + 1) * 128)
        if q < chunks:
            out[here, j * width : (j + 1) * width] = panel[j, band, :]
        else:
            part, at = divmod(j, cross[0].shape[0])
            out[here, pl.ds(pl.multiple_of(j * width + s * lane, 128), lane)] = same[j, band, :]
            out[here, pl.ds(pl.multiple_of(j * width + (1 - s) * lane, 128), lane)] = cross[part][at, band, :]


def pick(s, out, first, second):
    @pl.when(s == 0)
    def _():
        out[...] = first[...]

    @pl.when(s == 1)
    def _():
        out[...] = second[...]


def early_kernel(ids, parent, z1, z1_sib, z2, z2_sib, spread, y0, acc, rows):
    s = ids[2]
    tall, wide = parent.shape
    rows[:, :wide] = parent[...]
    pick(s, rows.at[:, wide:], z2_sib, z2)
    y0[...] = (-jnp.dot(rows[...], spread[...], preferred_element_type=F32)).astype(BF16)
    for k, first, second in ((1, z1_sib, z1), (2, z2, z2_sib), (3, z1, z1_sib)):
        pick(s, rows.at[:, :wide], first, second)
        acc[(k - 1) * tall : k * tall, :] = jnp.dot(rows[:, :wide], spread[:wide, :], preferred_element_type=F32)


def final_kernel(
    ids, pat, widths, q1, q1_sib, q2, q2_sib, spread, full, y0, acc, dinv, off_out, diag_out, rows, y_all
):
    r, c, s = ids[0], ids[1], ids[2]
    children, width, lane = dinv.shape
    tall, wide = rows.shape
    total = y_all.shape[0]

    def place(k, y):
        at = lax.rem(jnp.bitwise_xor(r, k) * tall + c * wide, total)
        y_all[pl.ds(pl.multiple_of(at, 128), tall), :] = y

    place(0, y0[...])
    cut = q2.shape[0]
    for k, first, second in ((1, q1_sib, q1), (2, q1, q1_sib), (3, q2_sib, q2)):
        if k < 3:
            pick(s, rows, first, second)
        else:
            pick(s, rows.at[:cut, :], first, second)
            pick(s, rows.at[cut:, :], second, first)
        term = jnp.dot(rows[...], spread[wide:, :], preferred_element_type=F32)
        place(k, (-(acc[(k - 1) * tall : k * tall, :] + term)).astype(BF16))
    chunks = off_out.shape[1] // 128
    for j in range(children):
        w = widths[j]
        mine = slice(j * lane, (j + 1) * lane)
        keep_b = s * lane + lax.broadcasted_iota(jnp.int32, (1, lane), 1) < w
        keep_a = lax.broadcasted_iota(jnp.int32, (width, 1), 0) < w
        for q in range(chunks):
            g = c * chunks + q
            start = lax.rem(pat[j, g // 2] * width + (g % 2) * 128 + c * wide, total)
            got = y_all[pl.ds(pl.multiple_of(start, 128), 128), mine]
            off_out[j, q * 128 : (q + 1) * 128, :] = jnp.where(keep_b, got, jnp.zeros_like(got))
        terms = lax.dot_general(
            y_all[:, mine], full[:, j * width : (j + 1) * width], (((0,), (0,)), ((), ())), preferred_element_type=F32
        )
        diag = dinv[j].astype(F32) - terms.T
        diag_out[j] = jnp.where(keep_a & keep_b, diag, 0.0).astype(BF16)


VMEM = pl.BlockSpec(memory_space=pltpu.VMEM)
SMEM = pl.BlockSpec(memory_space=pltpu.SMEM)


def cost(flops):
    return pl.CostEstimate(flops=flops, bytes_accessed=0, transcendentals=0)


FREE = cost(0)


def gathered(parent, panel, diag_inverse, pattern, widths):
    r, c, s = lax.axis_index("row"), lax.axis_index("col"), lax.axis_index("sub")
    children, rows, width = panel.shape
    lane = width // 2
    tall, wide = parent.shape
    lanes = children * lane
    ids = jnp.stack([r, c, s]).astype(jnp.int32)

    def core(first, second):
        pairs = []
        for row in range(4):
            for col in range(2):
                for sub, to in enumerate((first, second)):
                    if to is not None:
                        to_row, to_col = to(row, col)
                        pairs.append(((row * 2 + col) * 2 + sub, (to_row * 2 + to_col) * 2 + sub))
        return pairs

    def along(d):
        return lambda row, col: (row ^ d, col)

    def across(row, col):
        return row, 1 - col

    def send(x, first, second):
        return lax.ppermute(x, ("row", "col", "sub"), core(first, second))

    def sib(x):
        return lax.ppermute(x, "sub", SWAP)

    def params(mib):
        return pltpu.CompilerParams(vmem_limit_bytes=mib << 20)

    z1 = send(parent, along(3), along(1))
    z2 = send(parent, along(2), across)
    mine = lax.dynamic_slice_in_dim(panel, s * lane, lane, 2)
    same = lax.ppermute(mine, "col", SWAP)
    q1 = send(z2, across, along(1))
    cut = tall // 2
    q2 = send(jnp.where(s == 0, z1[cut:], z2[:cut]), across, along(3))
    cross = [sib(same[: children // 2]), sib(same[children // 2 :])]

    spread = pl.pallas_call(
        spread_kernel,
        out_shape=jax.ShapeDtypeStruct((2 * wide, lanes), BF16),
        in_specs=[SMEM, SMEM] + [VMEM] * 2,
        out_specs=VMEM,
        cost_estimate=cost(500000000),
        compiler_params=params(8),
        name="spread",
    )(ids, pattern, panel, same)
    full = pl.pallas_call(
        widen_kernel,
        out_shape=jax.ShapeDtypeStruct((2 * wide, 2 * lanes), BF16),
        in_specs=[SMEM, SMEM] + [VMEM] * 4,
        out_specs=VMEM,
        cost_estimate=FREE,
        compiler_params=params(8),
        name="widen",
    )(ids, pattern, panel, same, *cross)
    y0, acc = pl.pallas_call(
        early_kernel,
        out_shape=(
            jax.ShapeDtypeStruct((tall, lanes), BF16),
            jax.ShapeDtypeStruct((3 * tall, lanes), F32),
        ),
        in_specs=[SMEM] + [VMEM] * 6,
        out_specs=(VMEM, VMEM),
        scratch_shapes=[pltpu.VMEM((tall, 2 * wide), BF16)],
        cost_estimate=cost(800000000),
        compiler_params=params(12),
        name="early",
    )(ids, parent, z1, sib(z1), z2, sib(z2), spread)
    q2, y0, acc = lax.optimization_barrier((q2, y0, acc))
    return pl.pallas_call(
        final_kernel,
        out_shape=(
            jax.ShapeDtypeStruct((children, rows, lane), BF16),
            jax.ShapeDtypeStruct((children, width, lane), BF16),
        ),
        in_specs=[SMEM, SMEM, SMEM] + [VMEM] * 9,
        out_specs=(VMEM, VMEM),
        scratch_shapes=[
            pltpu.VMEM((tall, wide), BF16),
            pltpu.VMEM((4 * tall, lanes), BF16),
        ],
        cost_estimate=FREE,
        compiler_params=params(16),
        name="final",
    )(ids, pattern, widths, q1, sib(q1), q2, sib(q2), spread, full, y0, acc, diag_inverse)


def solution(mesh):
    placed = (
        P(("pole", "row"), "col"),
        P(("pole", "row"), "col", None),
        P(("pole", "row"), None, "sub"),
        P("row", None),
        P("row"),
    )
    shape = dict(mesh.shape)
    fits = (shape["row"], shape["col"], shape["sub"]) == (4, 2, 2)
    return jax.shard_map(
        gathered if fits else generic,
        mesh=mesh,
        in_specs=placed,
        out_specs=(P(("pole", "row"), "col", "sub"), P(("pole", "row"), None, "sub")),
        check_vma=False,
    )
```

time: 59.1 us -> 54 us (0.914)
  waiting for transfers between devices: 30.7 us -> 23.7 us
  Pallas kernels: 10.7 us -> 13.9 us
  starting transfers between devices: 13.7 us -> 11.9 us
  other arithmetic: 0.17 us -> 1.07 us
    ppermute x7 -> x4, waiting for transfers between devices: 28.3 us -> 23.7 us  [send(): return lax.ppermute(x, ('row', 'col', 'sub'), core(first, second))]
    unnamed x17 -> x10, local copies, waits for them, and re-layouts: 2.71 us -> 0.02 us
    ppermute x3 -> x6, waiting for transfers between devices: 2.42 us -> 0.02 us  [sib(): return lax.ppermute(x, 'sub', SWAP)]
    dynamic_slice x0 -> x1, local copies, waits for them, and re-layouts: none -> 2.35 us  [gathered(): mine = lax.dynamic_slice_in_dim(panel, s * lane, lane, 2)]
    pallas_call x1, Pallas kernels: 3.09 us -> 4.91 us  [gathered(): pl.pallas_call(early_kernel, out_shape=(jax.ShapeDtypeStruct((tall, lanes...]
    ppermute x1, starting transfers between devices: 3 us -> 1.49 us  [gathered(): same = lax.ppermute(mine, 'col', SWAP)]
    pallas_call x1, Pallas kernels: 4.52 us -> 5.52 us  [gathered(): pl.pallas_call(final_kernel, out_shape=(jax.ShapeDtypeStruct((children, r...]
    select_n x0 -> x1, other arithmetic: none -> 0.99 us  [gathered(): q2 = send(jnp.where(s == 0, z1[cut:], z2[:cut]), across, along(3))]
  transfers between devices with their start and end apart: 11 -> 11, of which waited for: 4 -> 3; matrix products, arithmetic and copies ran while one was open for 0% -> 6% of each run, Pallas kernels for 9% -> 16%
where the time goes in v3:
time: 54 us; the launch traced here: 53.8 us
  waiting for transfers between devices  23.7 us (44%)
  Pallas kernels  13.9 us (26%)
  starting transfers between devices  11.9 us (22%)
  local copies, waits for them, and re-layouts  2.44 us (5%)
  other arithmetic  1.07 us (2%)
  between operations  0.75 us (1%)
    ppermute x4, waiting for transfers between devices, send(): return lax.ppermute(x, ('row', 'col', 'sub'), core(first, second))  23.7 us
    ppermute x4, starting transfers between devices, send(): return lax.ppermute(x, ('row', 'col', 'sub'), core(first, second))  9.16 us
    pallas_call x1, Pallas kernels, gathered(): pl.pallas_call(final_kernel, out_shape=(jax.ShapeDtypeStruct((children, r...  5.52 us
    pallas_call x1, Pallas kernels, gathered(): pl.pallas_call(early_kernel, out_shape=(jax.ShapeDtypeStruct((tall, lanes...  4.91 us
    dynamic_slice x1, local copies, waits for them, and re-layouts, gathered(): mine = lax.dynamic_slice_in_dim(panel, s * lane, lane, 2)  2.35 us
    pallas_call x1, Pallas kernels, gathered(): pl.pallas_call(widen_kernel, out_shape=jax.ShapeDtypeStruct((2 * wide, 2...  1.86 us
    pallas_call x1, Pallas kernels, gathered(): pl.pallas_call(spread_kernel, out_shape=jax.ShapeDtypeStruct((2 * wide, l...  1.59 us
    ppermute x1, starting transfers between devices, gathered(): same = lax.ppermute(mine, 'col', SWAP)  1.49 us
  transfers between devices with their start and end apart: 11, of which 3 were waited for; matrix products, arithmetic and copies ran while one was open for 6% of the time, Pallas kernels for 16%

profile of v3, /device:TPU:0, one launch (start us, length us, event | category | flops | bytes accessed | tf_op | source)
XLA Modules:
  0.0 53.8 jit_solution(11998420100052696300)
XLA Ops:
  0.6 4.1 %collective-permute-start = (bf16[384,768]{1,0:T(8,128)(2,1)}, bf16[384,768]{1,0:T(8,128)(2,1)S(1)}, u32[]{:S(2)}, u32[]{:S(2)}) collective-permute-start(bf16[384,768]{1,0:T(8,128)(2,1)} %parent.1), channel_id=1, source_target_pairs={{0,8},{1,3},{2,10},{3,1},{4,12},{5,7},{6,14},{7,5},{8,0},{9,11},{1... | collective-permute-start | bytes 1769480 | tf_op jit(solution)/shard_map/ppermute | solution.py:190
  4.7 2.3 %constant_dynamic-slice_fusion = bf16[6,640,128]{2,1,0:T(8,128)(2,1)} fusion(bf16[6,640,256]{2,1,0:T(8,128)(2,1)} %panel.3, s32[]{:T(128)S(6)} %select_n.13), kind=kLoop, calls=%fused_computation.2 | loop fusion | bytes 1966084 | tf_op jit(solution)/shard_map/dynamic_slice | solution.py:200
  7.1 1.5 %collective-permute-start.7 = (bf16[6,640,128]{2,1,0:T(8,128)(2,1)}, bf16[6,640,128]{2,1,0:T(8,128)(2,1)S(1)}, u32[]{:S(2)}, u32[]{:S(2)}) collective-permute-start(bf16[6,640,128]{2,1,0:T(8,128)(2,1)} %constant_dynamic-slice_fusion), channel_id=1, source_target_pairs={{0,2},{2,0},{1,3},{3,1},{4,6},{6,4},{5,7},{7,5},{8,10},{10,8},{9,1... | collective-permute-start | bytes 2949128 | tf_op jit(solution)/shard_map/ppermute | solution.py:201
  8.6 1.3 %collective-permute-start.3 = (bf16[384,768]{1,0:T(8,128)(2,1)}, bf16[384,768]{1,0:T(8,128)(2,1)}, u32[]{:S(2)}, u32[]{:S(2)}) collective-permute-start(bf16[384,768]{1,0:T(8,128)(2,1)} %parent.1), channel_id=1, source_target_pairs={{0,12},{1,5},{2,14},{3,7},{4,8},{5,1},{6,10},{7,3},{8,4},{9,13},{1... | collective-permute-start | bytes 1769480 | tf_op jit(solution)/shard_map/ppermute | solution.py:190
  9.9 10.8 %collective-permute-done.z2 = bf16[384,768]{1,0:T(8,128)(2,1)S(1)} collective-permute-done((bf16[384,768]{1,0:T(8,128)(2,1)}, bf16[384,768]{1,0:T(8,128)(2,1)S(1)}, u32[]{:S(2)}, u32[]{:S(2)}) %collective-permute-start) | collective-permute-done | bytes 589856 | tf_op jit(solution)/shard_map/ppermute | solution.py:190
  20.7 2.2 %collective-permute-start.1 = (bf16[384,768]{1,0:T(8,128)(2,1)S(1)}, bf16[384,768]{1,0:T(8,128)(2,1)}, u32[]{:S(2)}, u32[]{:S(2)}) collective-permute-start(bf16[384,768]{1,0:T(8,128)(2,1)S(1)} %collective-permute-done.z2), channel_id=1, source_target_pairs={{0,2},{1,5},{2,0},{3,7},{4,6},{5,1},{6,4},{7,3},{8,10},{9,13},{10,... | collective-permute-start | bytes 1769480 | tf_op jit(solution)/shard_map/ppermute | solution.py:190
  22.9 0.0 collective-permute-start.6
  22.9 7.6 %collective-permute-done.3.z1 = bf16[384,768]{1,0:T(8,128)(2,1)} collective-permute-done((bf16[384,768]{1,0:T(8,128)(2,1)}, bf16[384,768]{1,0:T(8,128)(2,1)}, u32[]{:S(2)}, u32[]{:S(2)}) %collective-permute-start.3) | collective-permute-done | bytes 589856 | tf_op jit(solution)/shard_map/ppermute | solution.py:190
  30.4 0.0 collective-permute-start.5
  30.4 1.0 %slice_select_fusion = bf16[192,768]{1,0:T(8,128)(2,1)S(1)} fusion(bf16[384,768]{1,0:T(8,128)(2,1)S(1)} %collective-permute-done.z2, bf16[384,768]{1,0:T(8,128)(2,1)} %collective-permute-done.3.z1, pred[]{:T(512)S(6)} %eq.3), kind=kLoop, calls=%fused_computation | loop fusion | flops 147456 | bytes 884737 | tf_op jit(solution)/shard_map/jit(_where)/select_n | solution.py:204
  31.4 1.6 %collective-permute-start.4 = (bf16[192,768]{1,0:T(8,128)(2,1)S(1)}, bf16[192,768]{1,0:T(8,128)(2,1)S(1)}, u32[]{:S(2)}, u32[]{:S(2)}) collective-permute-start(bf16[192,768]{1,0:T(8,128)(2,1)S(1)} %slice_select_fusion), channel_id=1, source_target_pairs={{0,2},{1,13},{2,0},{3,15},{4,6},{5,9},{6,4},{7,11},{8,10},{9,5},{1... | collective-permute-start | bytes 884744 | tf_op jit(solution)/shard_map/ppermute | solution.py:190
  33.0 5.3 %collective-permute-done.1.q1 = bf16[384,768]{1,0:T(8,128)(2,1)} collective-permute-done((bf16[384,768]{1,0:T(8,128)(2,1)S(1)}, bf16[384,768]{1,0:T(8,128)(2,1)}, u32[]{:S(2)}, u32[]{:S(2)}) %collective-permute-start.1) | collective-permute-done | bytes 589856 | tf_op jit(solution)/shard_map/ppermute | solution.py:190
  38.3 0.0 collective-permute-start.2
  38.3 0.0 collective-permute-done.7.same
  38.4 0.1 fusion
  38.4 0.6 %collective-permute-start.10 = (bf16[3,640,128]{2,1,0:T(8,128)(2,1)S(1)}, bf16[3,640,128]{2,1,0:T(8,128)(2,1)S(1)}, u32[]{:S(2)}, u32[]{:S(2)}) collective-permute-start(bf16[3,640,128]{2,1,0:T(8,128)(2,1)S(1)} %get-tuple-element.12), channel_id=1, source_target_pairs={{0,1},{1,0},{2,3},{3,2},{4,5},{5,4},{6,7},{7,6},{8,9},{9,8},{10,11... | collective-permute-start | bytes 1474568 | tf_op jit(solution)/shard_map/ppermute | solution.py:193
  39.0 0.0 collective-permute-done.6.z2_sib
  39.0 0.1 collective-permute-start.9
  39.1 0.1 pad_add_fusion.ids
  39.2 1.6 %spread.1 = bf16[1536,768]{1,0:T(8,128)(2,1)S(1)} custom-call(s32[3]{0:T(128)S(1)} %pad_add_fusion.ids, s32[6,5]{1,0:T(8,128)S(1)} %copy-done.3, bf16[6,640,256]{2,1,0:T(8,128)(2,1)S(1)} %copy-done, bf16[6,640,128]{2,1,0:T(8,128)(2,1)S(1)} %collective-permute-done.7.same), custom_call_target="tpu_custom_call" | custom-call | flops 500000000 | tf_op jit(solution)/shard_map/spread/pallas_call | solution.py:207
  40.8 0.0 collective-permute-done.5.z1_sib
  40.8 4.9 %early.1 = (bf16[384,768]{1,0:T(8,128)(2,1)S(1)}, f32[1152,768]{1,0:T(8,128)S(1)}) custom-call(s32[3]{0:T(128)S(1)} %pad_add_fusion.ids, bf16[384,768]{1,0:T(8,128)(2,1)S(1)} %copy-done.1, bf16[384,768]{1,0:T(8,128)(2,1)} %collective-permute-done.3.z1, bf16[384,768]{1,0:T(8,128)(2,1)S(1)} %collective-permute-done.5.z1_sib, ...), custom_call_target="tpu_custom_call" | custom-call | flops 800000000 | tf_op jit(solution)/shard_map/early/pallas_call | solution.py:225
  45.7 0.0 collective-permute-done.4.q2
  45.7 0.0 copy-start.2
  45.7 0.0 copy-start.4
  45.7 0.6 %collective-permute-start.8 = (bf16[192,768]{1,0:T(8,128)(2,1)S(1)}, bf16[192,768]{1,0:T(8,128)(2,1)S(1)}, u32[]{:S(2)}, u32[]{:S(2)}) collective-permute-start(bf16[192,768]{1,0:T(8,128)(2,1)S(1)} %collective-permute-done.4.q2), channel_id=1, source_target_pairs={{0,1},{1,0},{2,3},{3,2},{4,5},{5,4},{6,7},{7,6},{8,9},{9,8},{10,11... | collective-permute-start | bytes 884744 | tf_op jit(solution)/shard_map/ppermute | solution.py:193
  46.3 0.0 collective-permute-done.10.refs_1_
  46.3 0.0 collective-permute-done.9.refs_0_
  46.3 1.9 %widen.1.full = bf16[1536,1536]{1,0:T(8,128)(2,1)S(1)} custom-call(s32[3]{0:T(128)S(1)} %pad_add_fusion.ids, s32[6,5]{1,0:T(8,128)S(1)} %copy-done.3, bf16[6,640,256]{2,1,0:T(8,128)(2,1)S(1)} %copy-done, bf16[6,640,128]{2,1,0:T(8,128)(2,1)S(1)} %collective-permute-done.7.same, bf16[3,640,128]{2,1,0:T(8,128)(2,1)S(1)} %collective-permute-done.9.refs_0_, ...), custom_call_target="tpu_custom_call" | custom-call | tf_op jit(solution)/shard_map/widen/pallas_call | solution.py:216
  48.2 0.0 collective-permute-done.8.q2_sib
  48.2 0.0 collective-permute-done.2.q1_sib
  48.2 5.5 %final.1 = (bf16[6,640,128]{2,1,0:T(8,128)(2,1)}, bf16[6,256,128]{2,1,0:T(8,128)(2,1)}) custom-call(s32[3]{0:T(128)S(1)} %pad_add_fusion.ids, s32[6,5]{1,0:T(8,128)S(1)} %copy-done.3, s32[6]{0:T(128)S(1)} %copy-done.4, bf16[384,768]{1,0:T(8,128)(2,1)} %collective-permute-done.1.q1, bf16[384,768]{1,0:T(8,128)(2,1)S(1)} %collective-permute-done.2.q1_sib, ...), custom_call_target="tpu_custom_call" | custom-call | tf_op jit(solution)/shard_map/final/pallas_call | solution.py:239
  (8 shorter events, 0.0 us)
Async XLA Ops:
  0.6 20.1 %collective-permute-start = (bf16[384,768]{1,0:T(8,128)(2,1)}, bf16[384,768]{1,0:T(8,128)(2,1)S(1)}, u32[]{:S(2)}, u32[]{:S(2)}) collective-permute-start(bf16[384,768]{1,0:T(8,128)(2,1)} %parent.1), channel_id=1, source_target_pairs={{0,8},{1,3},{2,10},{3,1},{4,12},{5,7},{6,14},{7,5},{8,0},{9,11},{1... | collective-permute-start | bytes 1769480 | tf_op jit(solution)/shard_map/ppermute | solution.py:190
  4.7 34.4 %copy-start = (bf16[6,640,256]{2,1,0:T(8,128)(2,1)S(1)}, bf16[6,640,256]{2,1,0:T(8,128)(2,1)}, u32[]{:S(2)}) copy-start(bf16[6,640,256]{2,1,0:T(8,128)(2,1)} %panel.3) | copy-start | bytes 5898244
  4.7 34.4 %copy-start.3 = (s32[6,5]{1,0:T(8,128)S(1)}, s32[6,5]{1,0:T(8,128)}, u32[]{:S(2)}) copy-start(s32[6,5]{1,0:T(8,128)} %pat.5) | copy-start | bytes 364
  7.1 31.3 %collective-permute-start.7 = (bf16[6,640,128]{2,1,0:T(8,128)(2,1)}, bf16[6,640,128]{2,1,0:T(8,128)(2,1)S(1)}, u32[]{:S(2)}, u32[]{:S(2)}) collective-permute-start(bf16[6,640,128]{2,1,0:T(8,128)(2,1)} %constant_dynamic-slice_fusion), channel_id=1, source_target_pairs={{0,2},{2,0},{1,3},{3,1},{4,6},{6,4},{5,7},{7,5},{8,10},{10,8},{9,1... | collective-permute-start | bytes 2949128 | tf_op jit(solution)/shard_map/ppermute | solution.py:201
  8.6 21.9 %collective-permute-start.3 = (bf16[384,768]{1,0:T(8,128)(2,1)}, bf16[384,768]{1,0:T(8,128)(2,1)}, u32[]{:S(2)}, u32[]{:S(2)}) collective-permute-start(bf16[384,768]{1,0:T(8,128)(2,1)} %parent.1), channel_id=1, source_target_pairs={{0,12},{1,5},{2,14},{3,7},{4,8},{5,1},{6,10},{7,3},{8,4},{9,13},{1... | collective-permute-start | bytes 1769480 | tf_op jit(solution)/shard_map/ppermute | solution.py:190
  20.7 17.6 %collective-permute-start.1 = (bf16[384,768]{1,0:T(8,128)(2,1)S(1)}, bf16[384,768]{1,0:T(8,128)(2,1)}, u32[]{:S(2)}, u32[]{:S(2)}) collective-permute-start(bf16[384,768]{1,0:T(8,128)(2,1)S(1)} %collective-permute-done.z2), channel_id=1, source_target_pairs={{0,2},{1,5},{2,0},{3,7},{4,6},{5,1},{6,4},{7,3},{8,10},{9,13},{10,... | collective-permute-start | bytes 1769480 | tf_op jit(solution)/shard_map/ppermute | solution.py:190
  22.9 16.1 %collective-permute-start.6 = (bf16[384,768]{1,0:T(8,128)(2,1)S(1)}, bf16[384,768]{1,0:T(8,128)(2,1)}, u32[]{:S(2)}, u32[]{:S(2)}) collective-permute-start(bf16[384,768]{1,0:T(8,128)(2,1)S(1)} %collective-permute-done.z2), channel_id=1, source_target_pairs={{0,1},{1,0},{2,3},{3,2},{4,5},{5,4},{6,7},{7,6},{8,9},{9,8},{10,11... | collective-permute-start | bytes 1769480 | tf_op jit(solution)/shard_map/ppermute | solution.py:193
  30.4 10.3 %collective-permute-start.5 = (bf16[384,768]{1,0:T(8,128)(2,1)}, bf16[384,768]{1,0:T(8,128)(2,1)S(1)}, u32[]{:S(2)}, u32[]{:S(2)}) collective-permute-start(bf16[384,768]{1,0:T(8,128)(2,1)} %collective-permute-done.3.z1), channel_id=1, source_target_pairs={{0,1},{1,0},{2,3},{3,2},{4,5},{5,4},{6,7},{7,6},{8,9},{9,8},{10,11... | collective-permute-start | bytes 1769480 | tf_op jit(solution)/shard_map/ppermute | solution.py:193
  31.4 14.3 %collective-permute-start.4 = (bf16[192,768]{1,0:T(8,128)(2,1)S(1)}, bf16[192,768]{1,0:T(8,128)(2,1)S(1)}, u32[]{:S(2)}, u32[]{:S(2)}) collective-permute-start(bf16[192,768]{1,0:T(8,128)(2,1)S(1)} %slice_select_fusion), channel_id=1, source_target_pairs={{0,2},{1,13},{2,0},{3,15},{4,6},{5,9},{6,4},{7,11},{8,10},{9,5},{1... | collective-permute-start | bytes 884744 | tf_op jit(solution)/shard_map/ppermute | solution.py:190
  38.3 9.9 %collective-permute-start.2 = (bf16[384,768]{1,0:T(8,128)(2,1)}, bf16[384,768]{1,0:T(8,128)(2,1)S(1)}, u32[]{:S(2)}, u32[]{:S(2)}) collective-permute-start(bf16[384,768]{1,0:T(8,128)(2,1)} %collective-permute-done.1.q1), channel_id=1, source_target_pairs={{0,1},{1,0},{2,3},{3,2},{4,5},{5,4},{6,7},{7,6},{8,9},{9,8},{10,11... | collective-permute-start | bytes 1769480 | tf_op jit(solution)/shard_map/ppermute | solution.py:193
  38.4 7.9 %collective-permute-start.10 = (bf16[3,640,128]{2,1,0:T(8,128)(2,1)S(1)}, bf16[3,640,128]{2,1,0:T(8,128)(2,1)S(1)}, u32[]{:S(2)}, u32[]{:S(2)}) collective-permute-start(bf16[3,640,128]{2,1,0:T(8,128)(2,1)S(1)} %get-tuple-element.12), channel_id=1, source_target_pairs={{0,1},{1,0},{2,3},{3,2},{4,5},{5,4},{6,7},{7,6},{8,9},{9,8},{10,11... | collective-permute-start | bytes 1474568 | tf_op jit(solution)/shard_map/ppermute | solution.py:193
  39.0 7.3 %collective-permute-start.9 = (bf16[3,640,128]{2,1,0:T(8,128)(2,1)S(1)}, bf16[3,640,128]{2,1,0:T(8,128)(2,1)S(1)}, u32[]{:S(2)}, u32[]{:S(2)}) collective-permute-start(bf16[3,640,128]{2,1,0:T(8,128)(2,1)S(1)} %get-tuple-element.13), channel_id=1, source_target_pairs={{0,1},{1,0},{2,3},{3,2},{4,5},{5,4},{6,7},{7,6},{8,9},{9,8},{10,11... | collective-permute-start | bytes 1474568 | tf_op jit(solution)/shard_map/ppermute | solution.py:193
  39.2 1.6 %copy-start.1 = (bf16[384,768]{1,0:T(8,128)(2,1)S(1)}, bf16[384,768]{1,0:T(8,128)(2,1)}, u32[]{:S(2)}) copy-start(bf16[384,768]{1,0:T(8,128)(2,1)} %parent.1) | copy-start | bytes 1769476
  45.7 2.5 %copy-start.2 = (bf16[6,256,128]{2,1,0:T(8,128)(2,1)S(1)}, bf16[6,256,128]{2,1,0:T(8,128)(2,1)}, u32[]{:S(2)}) copy-start(bf16[6,256,128]{2,1,0:T(8,128)(2,1)} %dinv.1) | copy-start | bytes 1179652
  45.7 2.5 %copy-start.4 = (s32[6]{0:T(128)S(1)}, s32[6]{0:T(128)}, u32[]{:S(2)}) copy-start(s32[6]{0:T(128)} %widths.1) | copy-start | bytes 76
  45.7 2.5 %collective-permute-start.8 = (bf16[192,768]{1,0:T(8,128)(2,1)S(1)}, bf16[192,768]{1,0:T(8,128)(2,1)S(1)}, u32[]{:S(2)}, u32[]{:S(2)}) collective-permute-start(bf16[192,768]{1,0:T(8,128)(2,1)S(1)} %collective-permute-done.4.q2), channel_id=1, source_target_pairs={{0,1},{1,0},{2,3},{3,2},{4,5},{5,4},{6,7},{7,6},{8,9},{9,8},{10,11... | collective-permute-start | bytes 884744 | tf_op jit(solution)/shard_map/ppermute | solution.py:193

commit v4 on v3

--- a/solution.py
+++ b/solution.py
@@ -90,49 +90,47 @@
             out[here, pl.ds(pl.multiple_of(j * width + (1 - s) * lane, 128), lane)] = cross[part][at, band, :]
 
 
-def pick(s, out, first, second):
-    @pl.when(s == 0)
-    def _():
-        out[...] = first[...]
-
-    @pl.when(s == 1)
-    def _():
-        out[...] = second[...]
-
-
-def early_kernel(ids, parent, z1, z1_sib, z2, z2_sib, spread, y0, acc, rows):
+def pick(s, first, second):
+    return jnp.where(s == 0, first[...], second[...])
+
+
+def product(rows, spread):
+    return jnp.dot(rows, spread, preferred_element_type=F32)
+
+
+def stage_kernel(a, b, a_out, b_out):
+    a_out[...] = a[...]
+    b_out[...] = b[...]
+
+
+def early_kernel(ids, parent, z1, z1_sib, z2, z2_sib, spread, y0, acc):
     s = ids[2]
     tall, wide = parent.shape
-    rows[:, :wide] = parent[...]
-    pick(s, rows.at[:, wide:], z2_sib, z2)
-    y0[...] = (-jnp.dot(rows[...], spread[...], preferred_element_type=F32)).astype(BF16)
+    low, high = spread[:wide, :], spread[wide:, :]
+    y0[...] = (-(product(parent[...], low) + product(pick(s, z2_sib, z2), high))).astype(BF16)
     for k, first, second in ((1, z1_sib, z1), (2, z2, z2_sib), (3, z1, z1_sib)):
-        pick(s, rows.at[:, :wide], first, second)
-        acc[(k - 1) * tall : k * tall, :] = jnp.dot(rows[:, :wide], spread[:wide, :], preferred_element_type=F32)
+        acc[(k - 1) * tall : k * tall, :] = product(pick(s, first, second), low)
 
 
 def final_kernel(
-    ids, pat, widths, q1, q1_sib, q2, q2_sib, spread, full, y0, acc, dinv, off_out, diag_out, rows, y_all
+    ids, pat, widths, q1, q1_sib, q2, q2_sib, spread, full, y0, acc, dinv, off_out, diag_out, y_all
 ):
     r, c, s = ids[0], ids[1], ids[2]
     children, width, lane = dinv.shape
-    tall, wide = rows.shape
+    tall, wide = q1.shape
     total = y_all.shape[0]
-
-    def place(k, y):
-        at = lax.rem(jnp.bitwise_xor(r, k) * tall + c * wide, total)
-        y_all[pl.ds(pl.multiple_of(at, 128), tall), :] = y
+    high = spread[wide:, :]
+
+    def place(k, y, first=0):
+        at = lax.rem(jnp.bitwise_xor(r, k) * tall + c * wide, total) + first
+        y_all[pl.ds(pl.multiple_of(at, 64), y.shape[0]), :] = y
 
     place(0, y0[...])
     cut = q2.shape[0]
-    for k, first, second in ((1, q1_sib, q1), (2, q1, q1_sib), (3, q2_sib, q2)):
-        if k < 3:
-            pick(s, rows, first, second)
-        else:
-            pick(s, rows.at[:cut, :], first, second)
-            pick(s, rows.at[cut:, :], second, first)
-        term = jnp.dot(rows[...], spread[wide:, :], preferred_element_type=F32)
-        place(k, (-(acc[(k - 1) * tall : k * tall, :] + term)).astype(BF16))
+    for k, first, second, begin in ((3, q2_sib, q2, 0), (3, q2, q2_sib, cut), (1, q1_sib, q1, 0), (2, q1, q1_sib, 0)):
+        at = (k - 1) * tall + begin
+        rows = pick(s, first, second)
+        place(k, (-(acc[at : at + rows.shape[0], :] + product(rows, high))).astype(BF16), begin)
     chunks = off_out.shape[1] // 128
     for j in range(children):
         w = widths[j]
@@ -222,6 +220,17 @@
         compiler_params=params(8),
         name="widen",
     )(ids, pattern, panel, same, *cross)
+    z1_sib, z2_sib = sib(z1), sib(z2)
+    z1_near, z2_sib = pl.pallas_call(
+        stage_kernel,
+        out_shape=(jax.ShapeDtypeStruct(z1.shape, BF16),) * 2,
+        in_specs=[VMEM] * 2,
+        out_specs=(VMEM, VMEM),
+        cost_estimate=FREE,
+        compiler_params=params(8),
+        name="stage",
+    )(z1, z2_sib)
+    q1, z1_near, z2_sib = lax.optimization_barrier((q1, z1_near, z2_sib))
     y0, acc = pl.pallas_call(
         early_kernel,
         out_shape=(
@@ -230,11 +239,10 @@
         ),
         in_specs=[SMEM] + [VMEM] * 6,
         out_specs=(VMEM, VMEM),
-        scratch_shapes=[pltpu.VMEM((tall, 2 * wide), BF16)],
         cost_estimate=cost(800000000),
         compiler_params=params(12),
         name="early",
-    )(ids, parent, z1, sib(z1), z2, sib(z2), spread)
+    )(ids, parent, z1_near, z1_sib, z2, z2_sib, spread)
     q2, y0, acc = lax.optimization_barrier((q2, y0, acc))
     return pl.pallas_call(
         final_kernel,
@@ -244,10 +252,7 @@
         ),
         in_specs=[SMEM, SMEM, SMEM] + [VMEM] * 9,
         out_specs=(VMEM, VMEM),
-        scratch_shapes=[
-            pltpu.VMEM((tall, wide), BF16),
-            pltpu.VMEM((4 * tall, lanes), BF16),
-        ],
+        scratch_shapes=[pltpu.VMEM((4 * tall, lanes), BF16)],
         cost_estimate=FREE,
         compiler_params=params(16),
         name="final",

time: 54 us -> 51.6 us (0.956)
  Pallas kernels: 13.9 us -> 12.7 us
  waiting for transfers between devices: 23.7 us -> 22.7 us
    pallas_call x1, Pallas kernels: 4.91 us -> 3.53 us  [gathered(): pl.pallas_call(early_kernel, out_shape=(jax.ShapeDtypeStruct((tall, lanes...]
    pallas_call x0 -> x1, Pallas kernels: none -> 1.14 us  [gathered(): pl.pallas_call(stage_kernel, out_shape=(jax.ShapeDtypeStruct(z1.shape, BF...]
    ppermute x4, waiting for transfers between devices: 23.7 us -> 22.7 us  [send(): return lax.ppermute(x, ('row', 'col', 'sub'), core(first, second))]
    pallas_call x1, Pallas kernels: 5.52 us -> 4.56 us  [gathered(): pl.pallas_call(final_kernel, out_shape=(jax.ShapeDtypeStruct((children, r...]
  transfers between devices with their start and end apart: 11 -> 11, of which waited for: 3 -> 3; matrix products, arithmetic and copies ran while one was open for 6% -> 7% of each run, Pallas kernels for 16% -> 16%
where the time goes in v4:
time: 51.6 us; the launch traced here: 51.3 us
  waiting for transfers between devices  22.7 us (44%)
  Pallas kernels  12.7 us (25%)
  starting transfers between devices  11.8 us (23%)
  local copies, waits for them, and re-layouts  2.3 us (4%)
  other arithmetic  1.07 us (2%)
  between operations  0.75 us (1%)
    ppermute x4, waiting for transfers between devices, send(): return lax.ppermute(x, ('row', 'col', 'sub'), core(first, second))  22.7 us
    ppermute x4, starting transfers between devices, send(): return lax.ppermute(x, ('row', 'col', 'sub'), core(first, second))  9.16 us
    pallas_call x1, Pallas kernels, gathered(): pl.pallas_call(final_kernel, out_shape=(jax.ShapeDtypeStruct((children, r...  4.56 us
    pallas_call x1, Pallas kernels, gathered(): pl.pallas_call(early_kernel, out_shape=(jax.ShapeDtypeStruct((tall, lanes...  3.53 us
    dynamic_slice x1, local copies, waits for them, and re-layouts, gathered(): mine = lax.dynamic_slice_in_dim(panel, s * lane, lane, 2)  2.21 us
    pallas_call x1, Pallas kernels, gathered(): pl.pallas_call(widen_kernel, out_shape=jax.ShapeDtypeStruct((2 * wide, 2...  1.86 us
    pallas_call x1, Pallas kernels, gathered(): pl.pallas_call(spread_kernel, out_shape=jax.ShapeDtypeStruct((2 * wide, l...  1.59 us
    ppermute x1, starting transfers between devices, gathered(): same = lax.ppermute(mine, 'col', SWAP)  1.49 us
  transfers between devices with their start and end apart: 11, of which 3 were waited for; matrix products, arithmetic and copies ran while one was open for 7% of the time, Pallas kernels for 16%

profile of v4, /device:TPU:0, one launch (start us, length us, event | category | flops | bytes accessed | tf_op | source)
XLA Modules:
  0.0 51.3 jit_solution(12451328728787326435)
XLA Ops:
  0.6 4.1 %collective-permute-start = (bf16[384,768]{1,0:T(8,128)(2,1)}, bf16[384,768]{1,0:T(8,128)(2,1)}, u32[]{:S(2)}, u32[]{:S(2)}) collective-permute-start(bf16[384,768]{1,0:T(8,128)(2,1)} %parent.1), channel_id=1, source_target_pairs={{0,8},{1,3},{2,10},{3,1},{4,12},{5,7},{6,14},{7,5},{8,0},{9,11},{1... | collective-permute-start | bytes 1769480 | tf_op jit(solution)/shard_map/ppermute | solution.py:188
  4.7 2.2 %constant_dynamic-slice_fusion = bf16[6,640,128]{2,1,0:T(8,128)(2,1)} fusion(bf16[6,640,256]{2,1,0:T(8,128)(2,1)} %panel.3, s32[]{:T(128)S(6)} %select_n.13), kind=kLoop, calls=%fused_computation.2 | loop fusion | bytes 1966084 | tf_op jit(solution)/shard_map/dynamic_slice | solution.py:198
  6.9 1.5 %collective-permute-start.7 = (bf16[6,640,128]{2,1,0:T(8,128)(2,1)}, bf16[6,640,128]{2,1,0:T(8,128)(2,1)S(1)}, u32[]{:S(2)}, u32[]{:S(2)}) collective-permute-start(bf16[6,640,128]{2,1,0:T(8,128)(2,1)} %constant_dynamic-slice_fusion), channel_id=1, source_target_pairs={{0,2},{2,0},{1,3},{3,1},{4,6},{6,4},{5,7},{7,5},{8,10},{10,8},{9,1... | collective-permute-start | bytes 2949128 | tf_op jit(solution)/shard_map/ppermute | solution.py:199
  8.4 1.3 %collective-permute-start.2 = (bf16[384,768]{1,0:T(8,128)(2,1)}, bf16[384,768]{1,0:T(8,128)(2,1)S(1)}, u32[]{:S(2)}, u32[]{:S(2)}) collective-permute-start(bf16[384,768]{1,0:T(8,128)(2,1)} %parent.1), channel_id=1, source_target_pairs={{0,12},{1,5},{2,14},{3,7},{4,8},{5,1},{6,10},{7,3},{8,4},{9,13},{1... | collective-permute-start | bytes 1769480 | tf_op jit(solution)/shard_map/ppermute | solution.py:188
  9.8 10.9 %collective-permute-done.z2 = bf16[384,768]{1,0:T(8,128)(2,1)} collective-permute-done((bf16[384,768]{1,0:T(8,128)(2,1)}, bf16[384,768]{1,0:T(8,128)(2,1)}, u32[]{:S(2)}, u32[]{:S(2)}) %collective-permute-start) | collective-permute-done | bytes 589856 | tf_op jit(solution)/shard_map/ppermute | solution.py:188
  20.7 0.0 collective-permute-start.3
  20.7 2.2 %collective-permute-start.1 = (bf16[384,768]{1,0:T(8,128)(2,1)}, bf16[384,768]{1,0:T(8,128)(2,1)}, u32[]{:S(2)}, u32[]{:S(2)}) collective-permute-start(bf16[384,768]{1,0:T(8,128)(2,1)} %collective-permute-done.z2), channel_id=1, source_target_pairs={{0,2},{1,5},{2,0},{3,7},{4,6},{5,1},{6,4},{7,3},{8,10},{9,13},{10,... | collective-permute-start | bytes 1769480 | tf_op jit(solution)/shard_map/ppermute | solution.py:188
  22.8 4.6 %collective-permute-done.2.a = bf16[384,768]{1,0:T(8,128)(2,1)S(1)} collective-permute-done((bf16[384,768]{1,0:T(8,128)(2,1)}, bf16[384,768]{1,0:T(8,128)(2,1)S(1)}, u32[]{:S(2)}, u32[]{:S(2)}) %collective-permute-start.2) | collective-permute-done | bytes 589856 | tf_op jit(solution)/shard_map/ppermute | solution.py:188
  27.4 0.0 collective-permute-start.6
  27.4 1.0 %slice_select_fusion = bf16[192,768]{1,0:T(8,128)(2,1)S(1)} fusion(bf16[384,768]{1,0:T(8,128)(2,1)} %collective-permute-done.z2, bf16[384,768]{1,0:T(8,128)(2,1)S(1)} %collective-permute-done.2.a, pred[]{:T(512)S(6)} %eq.3), kind=kLoop, calls=%fused_computation | loop fusion | flops 147456 | bytes 884737 | tf_op jit(solution)/shard_map/jit(_where)/select_n | solution.py:202
  28.4 1.6 %collective-permute-start.5 = (bf16[192,768]{1,0:T(8,128)(2,1)S(1)}, bf16[192,768]{1,0:T(8,128)(2,1)S(1)}, u32[]{:S(2)}, u32[]{:S(2)}) collective-permute-start(bf16[192,768]{1,0:T(8,128)(2,1)S(1)} %slice_select_fusion), channel_id=1, source_target_pairs={{0,2},{1,13},{2,0},{3,15},{4,6},{5,9},{6,4},{7,11},{8,10},{9,5},{1... | collective-permute-start | bytes 884744 | tf_op jit(solution)/shard_map/ppermute | solution.py:188
  29.9 0.0 collective-permute-done.3.b
  30.0 1.1 %stage.1 = (bf16[384,768]{1,0:T(8,128)(2,1)S(1)}, bf16[384,768]{1,0:T(8,128)(2,1)S(1)}) custom-call(bf16[384,768]{1,0:T(8,128)(2,1)S(1)} %collective-permute-done.2.a, bf16[384,768]{1,0:T(8,128)(2,1)} %collective-permute-done.3.b), custom_call_target="tpu_custom_call" | custom-call | tf_op jit(solution)/shard_map/stage/pallas_call | solution.py:224
  31.1 7.2 %collective-permute-done.1.q1 = bf16[384,768]{1,0:T(8,128)(2,1)} collective-permute-done((bf16[384,768]{1,0:T(8,128)(2,1)}, bf16[384,768]{1,0:T(8,128)(2,1)}, u32[]{:S(2)}, u32[]{:S(2)}) %collective-permute-start.1) | collective-permute-done | bytes 589856 | tf_op jit(solution)/shard_map/ppermute | solution.py:188
  38.3 0.0 collective-permute-start.4
  38.3 0.0 collective-permute-done.7.same
  38.4 0.1 fusion
  38.4 0.6 %collective-permute-start.10 = (bf16[3,640,128]{2,1,0:T(8,128)(2,1)S(1)}, bf16[3,640,128]{2,1,0:T(8,128)(2,1)S(1)}, u32[]{:S(2)}, u32[]{:S(2)}) collective-permute-start(bf16[3,640,128]{2,1,0:T(8,128)(2,1)S(1)} %get-tuple-element.22), channel_id=1, source_target_pairs={{0,1},{1,0},{2,3},{3,2},{4,5},{5,4},{6,7},{7,6},{8,9},{9,8},{10,11... | collective-permute-start | bytes 1474568 | tf_op jit(solution)/shard_map/ppermute | solution.py:191
  39.0 0.1 collective-permute-start.9
  39.1 0.1 pad_add_fusion.ids
  39.2 1.6 %spread.1 = bf16[1536,768]{1,0:T(8,128)(2,1)S(1)} custom-call(s32[3]{0:T(128)S(1)} %pad_add_fusion.ids, s32[6,5]{1,0:T(8,128)S(1)} %copy-done.3, bf16[6,640,256]{2,1,0:T(8,128)(2,1)S(1)} %copy-done, bf16[6,640,128]{2,1,0:T(8,128)(2,1)S(1)} %collective-permute-done.7.same), custom_call_target="tpu_custom_call" | custom-call | flops 500000000 | tf_op jit(solution)/shard_map/spread/pallas_call | solution.py:205
  40.8 0.0 collective-permute-done.6.z1_sib
  40.8 3.5 %early.1 = (bf16[384,768]{1,0:T(8,128)(2,1)S(1)}, f32[1152,768]{1,0:T(8,128)S(1)}) custom-call(s32[3]{0:T(128)S(1)} %pad_add_fusion.ids, bf16[384,768]{1,0:T(8,128)(2,1)S(1)} %copy-done.1, bf16[384,768]{1,0:T(8,128)(2,1)S(1)} %get-tuple-element.15.z1, bf16[384,768]{1,0:T(8,128)(2,1)S(1)} %collective-permute-done.6.z1_sib, ...), custom_call_target="tpu_custom_call" | custom-call | flops 800000000 | tf_op jit(solution)/shard_map/early/pallas_call | solution.py:234
  44.3 0.0 collective-permute-done.5.q2
  44.3 0.0 copy-start.2
  44.3 0.0 copy-start.4
  44.3 0.5 collective-permute-start.8
  44.8 0.0 collective-permute-done.10.refs_1_
  44.8 0.0 collective-permute-done.9.refs_0_
  44.8 1.9 %widen.1.full = bf16[1536,1536]{1,0:T(8,128)(2,1)S(1)} custom-call(s32[3]{0:T(128)S(1)} %pad_add_fusion.ids, s32[6,5]{1,0:T(8,128)S(1)} %copy-done.3, bf16[6,640,256]{2,1,0:T(8,128)(2,1)S(1)} %copy-done, bf16[6,640,128]{2,1,0:T(8,128)(2,1)S(1)} %collective-permute-done.7.same, bf16[3,640,128]{2,1,0:T(8,128)(2,1)S(1)} %collective-permute-done.9.refs_0_, ...), custom_call_target="tpu_custom_call" | custom-call | tf_op jit(solution)/shard_map/widen/pallas_call | solution.py:214
  46.7 0.0 collective-permute-done.8.q2_sib
  46.8 4.6 %final.1 = (bf16[6,640,128]{2,1,0:T(8,128)(2,1)}, bf16[6,256,128]{2,1,0:T(8,128)(2,1)}) custom-call(s32[3]{0:T(128)S(1)} %pad_add_fusion.ids, s32[6,5]{1,0:T(8,128)S(1)} %copy-done.3, s32[6]{0:T(128)S(1)} %copy-done.4, bf16[384,768]{1,0:T(8,128)(2,1)} %collective-permute-done.1.q1, bf16[384,768]{1,0:T(8,128)(2,1)S(1)} %collective-permute-done.4.q1_sib, ...), custom_call_target="tpu_custom_call" | custom-call | tf_op jit(solution)/shard_map/final/pallas_call | solution.py:247
  (9 shorter events, 0.0 us)
Async XLA Ops:
  0.6 20.0 %collective-permute-start = (bf16[384,768]{1,0:T(8,128)(2,1)}, bf16[384,768]{1,0:T(8,128)(2,1)}, u32[]{:S(2)}, u32[]{:S(2)}) collective-permute-start(bf16[384,768]{1,0:T(8,128)(2,1)} %parent.1), channel_id=1, source_target_pairs={{0,8},{1,3},{2,10},{3,1},{4,12},{5,7},{6,14},{7,5},{8,0},{9,11},{1... | collective-permute-start | bytes 1769480 | tf_op jit(solution)/shard_map/ppermute | solution.py:188
  6.9 32.2 %copy-start = (bf16[6,640,256]{2,1,0:T(8,128)(2,1)S(1)}, bf16[6,640,256]{2,1,0:T(8,128)(2,1)}, u32[]{:S(2)}) copy-start(bf16[6,640,256]{2,1,0:T(8,128)(2,1)} %panel.3) | copy-start | bytes 5898244
  6.9 32.2 %copy-start.3 = (s32[6,5]{1,0:T(8,128)S(1)}, s32[6,5]{1,0:T(8,128)}, u32[]{:S(2)}) copy-start(s32[6,5]{1,0:T(8,128)} %pat.5) | copy-start | bytes 364
  6.9 31.4 %collective-permute-start.7 = (bf16[6,640,128]{2,1,0:T(8,128)(2,1)}, bf16[6,640,128]{2,1,0:T(8,128)(2,1)S(1)}, u32[]{:S(2)}, u32[]{:S(2)}) collective-permute-start(bf16[6,640,128]{2,1,0:T(8,128)(2,1)} %constant_dynamic-slice_fusion), channel_id=1, source_target_pairs={{0,2},{2,0},{1,3},{3,1},{4,6},{6,4},{5,7},{7,5},{8,10},{10,8},{9,1... | collective-permute-start | bytes 2949128 | tf_op jit(solution)/shard_map/ppermute | solution.py:199
  8.4 19.0 %collective-permute-start.2 = (bf16[384,768]{1,0:T(8,128)(2,1)}, bf16[384,768]{1,0:T(8,128)(2,1)S(1)}, u32[]{:S(2)}, u32[]{:S(2)}) collective-permute-start(bf16[384,768]{1,0:T(8,128)(2,1)} %parent.1), channel_id=1, source_target_pairs={{0,12},{1,5},{2,14},{3,7},{4,8},{5,1},{6,10},{7,3},{8,4},{9,13},{1... | collective-permute-start | bytes 1769480 | tf_op jit(solution)/shard_map/ppermute | solution.py:188
  20.7 9.3 %collective-permute-start.3 = (bf16[384,768]{1,0:T(8,128)(2,1)}, bf16[384,768]{1,0:T(8,128)(2,1)}, u32[]{:S(2)}, u32[]{:S(2)}) collective-permute-start(bf16[384,768]{1,0:T(8,128)(2,1)} %collective-permute-done.z2), channel_id=1, source_target_pairs={{0,1},{1,0},{2,3},{3,2},{4,5},{5,4},{6,7},{7,6},{8,9},{9,8},{10,11... | collective-permute-start | bytes 1769480 | tf_op jit(solution)/shard_map/ppermute | solution.py:191
  20.7 17.7 %collective-permute-start.1 = (bf16[384,768]{1,0:T(8,128)(2,1)}, bf16[384,768]{1,0:T(8,128)(2,1)}, u32[]{:S(2)}, u32[]{:S(2)}) collective-permute-start(bf16[384,768]{1,0:T(8,128)(2,1)} %collective-permute-done.z2), channel_id=1, source_target_pairs={{0,2},{1,5},{2,0},{3,7},{4,6},{5,1},{6,4},{7,3},{8,10},{9,13},{10,... | collective-permute-start | bytes 1769480 | tf_op jit(solution)/shard_map/ppermute | solution.py:188
  27.4 13.4 %collective-permute-start.6 = (bf16[384,768]{1,0:T(8,128)(2,1)S(1)}, bf16[384,768]{1,0:T(8,128)(2,1)S(1)}, u32[]{:S(2)}, u32[]{:S(2)}) collective-permute-start(bf16[384,768]{1,0:T(8,128)(2,1)S(1)} %collective-permute-done.2.a), channel_id=1, source_target_pairs={{0,1},{1,0},{2,3},{3,2},{4,5},{5,4},{6,7},{7,6},{8,9},{9,8},{10,11... | collective-permute-start | bytes 1769480 | tf_op jit(solution)/shard_map/ppermute | solution.py:191
  28.4 15.9 %collective-permute-start.5 = (bf16[192,768]{1,0:T(8,128)(2,1)S(1)}, bf16[192,768]{1,0:T(8,128)(2,1)S(1)}, u32[]{:S(2)}, u32[]{:S(2)}) collective-permute-start(bf16[192,768]{1,0:T(8,128)(2,1)S(1)} %slice_select_fusion), channel_id=1, source_target_pairs={{0,2},{1,13},{2,0},{3,15},{4,6},{5,9},{6,4},{7,11},{8,10},{9,5},{1... | collective-permute-start | bytes 884744 | tf_op jit(solution)/shard_map/ppermute | solution.py:188
  38.3 8.4 %collective-permute-start.4 = (bf16[384,768]{1,0:T(8,128)(2,1)}, bf16[384,768]{1,0:T(8,128)(2,1)S(1)}, u32[]{:S(2)}, u32[]{:S(2)}) collective-permute-start(bf16[384,768]{1,0:T(8,128)(2,1)} %collective-permute-done.1.q1), channel_id=1, source_target_pairs={{0,1},{1,0},{2,3},{3,2},{4,5},{5,4},{6,7},{7,6},{8,9},{9,8},{10,11... | collective-permute-start | bytes 1769480 | tf_op jit(solution)/shard_map/ppermute | solution.py:191
  38.4 6.4 %collective-permute-start.10 = (bf16[3,640,128]{2,1,0:T(8,128)(2,1)S(1)}, bf16[3,640,128]{2,1,0:T(8,128)(2,1)S(1)}, u32[]{:S(2)}, u32[]{:S(2)}) collective-permute-start(bf16[3,640,128]{2,1,0:T(8,128)(2,1)S(1)} %get-tuple-element.22), channel_id=1, source_target_pairs={{0,1},{1,0},{2,3},{3,2},{4,5},{5,4},{6,7},{7,6},{8,9},{9,8},{10,11... | collective-permute-start | bytes 1474568 | tf_op jit(solution)/shard_map/ppermute | solution.py:191
  39.0 5.9 %collective-permute-start.9 = (bf16[3,640,128]{2,1,0:T(8,128)(2,1)S(1)}, bf16[3,640,128]{2,1,0:T(8,128)(2,1)S(1)}, u32[]{:S(2)}, u32[]{:S(2)}) collective-permute-start(bf16[3,640,128]{2,1,0:T(8,128)(2,1)S(1)} %get-tuple-element.23), channel_id=1, source_target_pairs={{0,1},{1,0},{2,3},{3,2},{4,5},{5,4},{6,7},{7,6},{8,9},{9,8},{10,11... | collective-permute-start | bytes 1474568 | tf_op jit(solution)/shard_map/ppermute | solution.py:191
  39.2 1.6 %copy-start.1 = (bf16[384,768]{1,0:T(8,128)(2,1)S(1)}, bf16[384,768]{1,0:T(8,128)(2,1)}, u32[]{:S(2)}) copy-start(bf16[384,768]{1,0:T(8,128)(2,1)} %parent.1) | copy-start | bytes 1769476
  44.3 2.4 %copy-start.2 = (bf16[6,256,128]{2,1,0:T(8,128)(2,1)S(1)}, bf16[6,256,128]{2,1,0:T(8,128)(2,1)}, u32[]{:S(2)}) copy-start(bf16[6,256,128]{2,1,0:T(8,128)(2,1)} %dinv.1) | copy-start | bytes 1179652
  44.3 2.4 %copy-start.4 = (s32[6]{0:T(128)S(1)}, s32[6]{0:T(128)}, u32[]{:S(2)}) copy-start(s32[6]{0:T(128)} %widths.1) | copy-start | bytes 76
  44.3 2.4 %collective-permute-start.8 = (bf16[192,768]{1,0:T(8,128)(2,1)S(1)}, bf16[192,768]{1,0:T(8,128)(2,1)S(1)}, u32[]{:S(2)}, u32[]{:S(2)}) collective-permute-start(bf16[192,768]{1,0:T(8,128)(2,1)S(1)} %collective-permute-done.5.q2), channel_id=1, source_target_pairs={{0,1},{1,0},{2,3},{3,2},{4,5},{5,4},{6,7},{7,6},{8,9},{9,8},{10,11... | collective-permute-start | bytes 884744 | tf_op jit(solution)/shard_map/ppermute | solution.py:191

commit v5 on v4

--- a/solution.py
+++ b/solution.py
@@ -98,22 +98,28 @@
     return jnp.dot(rows, spread, preferred_element_type=F32)
 
 
-def stage_kernel(a, b, a_out, b_out):
-    a_out[...] = a[...]
-    b_out[...] = b[...]
-
-
-def early_kernel(ids, parent, z1, z1_sib, z2, z2_sib, spread, y0, acc):
+def stage_kernel(src, out):
+    out[...] = src[...]
+
+
+def early_kernel(ids, parent, z2, z2_sib, spread, y0, acc2):
     s = ids[2]
-    tall, wide = parent.shape
+    wide = parent.shape[1]
     low, high = spread[:wide, :], spread[wide:, :]
     y0[...] = (-(product(parent[...], low) + product(pick(s, z2_sib, z2), high))).astype(BF16)
-    for k, first, second in ((1, z1_sib, z1), (2, z2, z2_sib), (3, z1, z1_sib)):
-        acc[(k - 1) * tall : k * tall, :] = product(pick(s, first, second), low)
+    acc2[...] = product(pick(s, z2, z2_sib), low)
+
+
+def middle_kernel(ids, z1, z1_sib, spread, acc13):
+    s = ids[2]
+    tall, wide = z1.shape
+    low = spread[:wide, :]
+    acc13[:tall, :] = product(pick(s, z1_sib, z1), low)
+    acc13[tall:, :] = product(pick(s, z1, z1_sib), low)
 
 
 def final_kernel(
-    ids, pat, widths, q1, q1_sib, q2, q2_sib, spread, full, y0, acc, dinv, off_out, diag_out, y_all
+    ids, pat, widths, q1, q1_sib, q2, q2_sib, spread, full, y0, acc2, acc13, dinv, off_out, diag_out, y_all
 ):
     r, c, s = ids[0], ids[1], ids[2]
     children, width, lane = dinv.shape
@@ -127,10 +133,13 @@
 
     place(0, y0[...])
     cut = q2.shape[0]
-    for k, first, second, begin in ((3, q2_sib, q2, 0), (3, q2, q2_sib, cut), (1, q1_sib, q1, 0), (2, q1, q1_sib, 0)):
-        at = (k - 1) * tall + begin
-        rows = pick(s, first, second)
-        place(k, (-(acc[at : at + rows.shape[0], :] + product(rows, high))).astype(BF16), begin)
+    for k, first, second, acc, begin in (
+        (3, q2_sib, q2, acc13.at[tall : tall + cut, :], 0),
+        (3, q2, q2_sib, acc13.at[tall + cut :, :], cut),
+        (1, q1_sib, q1, acc13.at[:tall, :], 0),
+        (2, q1, q1_sib, acc2, 0),
+    ):
+        place(k, (-(acc[...] + product(pick(s, first, second), high))).astype(BF16), begin)
     chunks = off_out.shape[1] // 128
     for j in range(children):
         w = widths[j]
@@ -207,7 +216,7 @@
         out_shape=jax.ShapeDtypeStruct((2 * wide, lanes), BF16),
         in_specs=[SMEM, SMEM] + [VMEM] * 2,
         out_specs=VMEM,
-        cost_estimate=cost(500000000),
+        cost_estimate=cost(300000000),
         compiler_params=params(8),
         name="spread",
     )(ids, pattern, panel, same)
@@ -220,43 +229,49 @@
         compiler_params=params(8),
         name="widen",
     )(ids, pattern, panel, same, *cross)
-    z1_sib, z2_sib = sib(z1), sib(z2)
-    z1_near, z2_sib = pl.pallas_call(
+    y_shape = jax.ShapeDtypeStruct((tall, lanes), BF16)
+    z1_near = pl.pallas_call(
         stage_kernel,
-        out_shape=(jax.ShapeDtypeStruct(z1.shape, BF16),) * 2,
-        in_specs=[VMEM] * 2,
-        out_specs=(VMEM, VMEM),
+        out_shape=jax.ShapeDtypeStruct(z1.shape, BF16),
+        in_specs=[VMEM],
+        out_specs=VMEM,
         cost_estimate=FREE,
         compiler_params=params(8),
         name="stage",
-    )(z1, z2_sib)
-    q1, z1_near, z2_sib = lax.optimization_barrier((q1, z1_near, z2_sib))
-    y0, acc = pl.pallas_call(
+    )(z1)
+    y0, acc2 = pl.pallas_call(
         early_kernel,
-        out_shape=(
-            jax.ShapeDtypeStruct((tall, lanes), BF16),
-            jax.ShapeDtypeStruct((3 * tall, lanes), F32),
-        ),
-        in_specs=[SMEM] + [VMEM] * 6,
+        out_shape=(y_shape, jax.ShapeDtypeStruct((tall, lanes), F32)),
+        in_specs=[SMEM] + [VMEM] * 4,
         out_specs=(VMEM, VMEM),
-        cost_estimate=cost(800000000),
+        cost_estimate=cost(300000000),
         compiler_params=params(12),
         name="early",
-    )(ids, parent, z1_near, z1_sib, z2, z2_sib, spread)
-    q2, y0, acc = lax.optimization_barrier((q2, y0, acc))
+    )(ids, parent, z2, sib(z2), spread)
+    acc13 = pl.pallas_call(
+        middle_kernel,
+        out_shape=jax.ShapeDtypeStruct((2 * tall, lanes), F32),
+        in_specs=[SMEM] + [VMEM] * 3,
+        out_specs=VMEM,
+        cost_estimate=FREE,
+        compiler_params=params(12),
+        name="middle",
+    )(ids, z1_near, sib(z1), spread)
+    q1, *_ = lax.optimization_barrier((q1, z1_near, spread, y0, acc2))
+    q2, *_ = lax.optimization_barrier((q2, acc13))
     return pl.pallas_call(
         final_kernel,
         out_shape=(
             jax.ShapeDtypeStruct((children, rows, lane), BF16),
             jax.ShapeDtypeStruct((children, width, lane), BF16),
         ),
-        in_specs=[SMEM, SMEM, SMEM] + [VMEM] * 9,
+        in_specs=[SMEM, SMEM, SMEM] + [VMEM] * 10,
         out_specs=(VMEM, VMEM),
         scratch_shapes=[pltpu.VMEM((4 * tall, lanes), BF16)],
         cost_estimate=FREE,
         compiler_params=params(16),
         name="final",
-    )(ids, pattern, widths, q1, sib(q1), q2, sib(q2), spread, full, y0, acc, diag_inverse)
+    )(ids, pattern, widths, q1, sib(q1), q2, sib(q2), spread, full, y0, acc2, acc13, diag_inverse)
 
 
 def solution(mesh):

time: 51.6 us -> 49.5 us (0.959)
  the two profiles are of different devices: /device:TPU:0 before, /device:TPU:9 now
where the time goes in v5:
time: 49.5 us; the launch traced here: 49.2 us
  starting transfers between devices  25.3 us (51%)
  Pallas kernels  13.3 us (27%)
  waiting for transfers between devices  6.33 us (13%)
  local copies, waits for them, and re-layouts  2.3 us (5%)
  other arithmetic  1.07 us (2%)
  between operations  0.82 us (2%)
    ppermute x6, starting transfers between devices, sib(): return lax.ppermute(x, 'sub', SWAP)  20.8 us
    ppermute x4, waiting for transfers between devices, send(): return lax.ppermute(x, ('row', 'col', 'sub'), core(first, second))  5.79 us
    pallas_call x1, Pallas kernels, gathered(): pl.pallas_call(final_kernel, out_shape=(jax.ShapeDtypeStruct((children, r...  4.56 us
    ppermute x4, starting transfers between devices, send(): return lax.ppermute(x, ('row', 'col', 'sub'), core(first, second))  4.1 us
    pallas_call x1, Pallas kernels, gathered(): pl.pallas_call(early_kernel, out_shape=(y_shape, jax.ShapeDtypeStruct((ta...  2.61 us
    dynamic_slice x1, local copies, waits for them, and re-layouts, gathered(): mine = lax.dynamic_slice_in_dim(panel, s * lane, lane, 2)  2.21 us
    pallas_call x1, Pallas kernels, gathered(): pl.pallas_call(widen_kernel, out_shape=jax.ShapeDtypeStruct((2 * wide, 2...  1.86 us
    pallas_call x1, Pallas kernels, gathered(): pl.pallas_call(middle_kernel, out_shape=jax.ShapeDtypeStruct((2 * tall, l...  1.62 us
  transfers between devices with their start and end apart: 11, of which 3 were waited for; matrix products, arithmetic and copies ran while one was open for 7% of the time, Pallas kernels for 18%

profile of v5, /device:TPU:9, one launch (start us, length us, event | category | flops | bytes accessed | tf_op | source)
XLA Modules:
  0.0 49.2 jit_solution(2055485974158127451)
XLA Ops:
  0.6 1.3 %collective-permute-start = (bf16[384,768]{1,0:T(8,128)(2,1)}, bf16[384,768]{1,0:T(8,128)(2,1)S(1)}, u32[]{:S(2)}, u32[]{:S(2)}) collective-permute-start(bf16[384,768]{1,0:T(8,128)(2,1)} %parent.1), channel_id=1, source_target_pairs={{0,8},{1,3},{2,10},{3,1},{4,12},{5,7},{6,14},{7,5},{8,0},{9,11},{1... | collective-permute-start | bytes 1769480 | tf_op jit(solution)/shard_map/ppermute | solution.py:197
  1.9 2.2 %constant_dynamic-slice_fusion = bf16[6,640,128]{2,1,0:T(8,128)(2,1)} fusion(bf16[6,640,256]{2,1,0:T(8,128)(2,1)} %panel.3, s32[]{:T(128)S(6)} %select_n.11), kind=kLoop, calls=%fused_computation.2 | loop fusion | bytes 1966084 | tf_op jit(solution)/shard_map/dynamic_slice | solution.py:207
  4.1 0.4 collective-permute-start.3
  4.6 0.0 collective-permute-start.2
  4.6 5.7 %collective-permute-done.z2 = bf16[384,768]{1,0:T(8,128)(2,1)S(1)} collective-permute-done((bf16[384,768]{1,0:T(8,128)(2,1)}, bf16[384,768]{1,0:T(8,128)(2,1)S(1)}, u32[]{:S(2)}, u32[]{:S(2)}) %collective-permute-start) | collective-permute-done | bytes 589856 | tf_op jit(solution)/shard_map/ppermute | solution.py:197
  10.3 9.3 %collective-permute-start.4 = (bf16[384,768]{1,0:T(8,128)(2,1)S(1)}, bf16[384,768]{1,0:T(8,128)(2,1)}, u32[]{:S(2)}, u32[]{:S(2)}) collective-permute-start(bf16[384,768]{1,0:T(8,128)(2,1)S(1)} %collective-permute-done.z2), channel_id=1, source_target_pairs={{0,1},{1,0},{2,3},{3,2},{4,5},{5,4},{6,7},{7,6},{8,9},{9,8},{10,11... | collective-permute-start | bytes 1769480 | tf_op jit(solution)/shard_map/ppermute | solution.py:200
  19.6 0.6 %collective-permute-start.1 = (bf16[384,768]{1,0:T(8,128)(2,1)S(1)}, bf16[384,768]{1,0:T(8,128)(2,1)}, u32[]{:S(2)}, u32[]{:S(2)}) collective-permute-start(bf16[384,768]{1,0:T(8,128)(2,1)S(1)} %collective-permute-done.z2), channel_id=1, source_target_pairs={{0,2},{1,5},{2,0},{3,7},{4,6},{5,1},{6,4},{7,3},{8,10},{9,13},{10,... | collective-permute-start | bytes 1769480 | tf_op jit(solution)/shard_map/ppermute | solution.py:197
  20.1 0.1 pad_add_fusion.ids
  20.2 0.1 collective-permute-done.2.src
  20.3 10.3 %collective-permute-start.7 = (bf16[384,768]{1,0:T(8,128)(2,1)}, bf16[384,768]{1,0:T(8,128)(2,1)S(1)}, u32[]{:S(2)}, u32[]{:S(2)}) collective-permute-start(bf16[384,768]{1,0:T(8,128)(2,1)} %collective-permute-done.2.src), channel_id=1, source_target_pairs={{0,1},{1,0},{2,3},{3,2},{4,5},{5,4},{6,7},{7,6},{8,9},{9,8},{10,11... | collective-permute-start | bytes 1769480 | tf_op jit(solution)/shard_map/ppermute | solution.py:200
  30.6 1.0 %slice_select_fusion = bf16[192,768]{1,0:T(8,128)(2,1)S(1)} fusion(bf16[384,768]{1,0:T(8,128)(2,1)S(1)} %collective-permute-done.z2, bf16[384,768]{1,0:T(8,128)(2,1)} %collective-permute-done.2.src, pred[]{:T(512)S(6)} %eq.3), kind=kLoop, calls=%fused_computation | loop fusion | flops 147456 | bytes 884737 | tf_op jit(solution)/shard_map/jit(_where)/select_n | solution.py:211
  31.6 2.3 %collective-permute-start.6 = (bf16[192,768]{1,0:T(8,128)(2,1)S(1)}, bf16[192,768]{1,0:T(8,128)(2,1)S(1)}, u32[]{:S(2)}, u32[]{:S(2)}) collective-permute-start(bf16[192,768]{1,0:T(8,128)(2,1)S(1)} %slice_select_fusion), channel_id=1, source_target_pairs={{0,2},{1,13},{2,0},{3,15},{4,6},{5,9},{6,4},{7,11},{8,10},{9,5},{1... | collective-permute-start | bytes 884744 | tf_op jit(solution)/shard_map/ppermute | solution.py:197
  33.9 1.1 %stage.1.z1 = bf16[384,768]{1,0:T(8,128)(2,1)S(1)} custom-call(bf16[384,768]{1,0:T(8,128)(2,1)} %collective-permute-done.2.src), custom_call_target="tpu_custom_call" | custom-call | tf_op jit(solution)/shard_map/stage/pallas_call | solution.py:233
  35.0 0.0 copy-start.1
  35.0 0.0 collective-permute-done.3.same
  35.0 1.6 %spread.1 = bf16[1536,768]{1,0:T(8,128)(2,1)S(1)} custom-call(s32[3]{0:T(128)S(1)} %pad_add_fusion.ids, s32[6,5]{1,0:T(8,128)S(1)} %copy-done.3, bf16[6,640,256]{2,1,0:T(8,128)(2,1)S(1)} %copy-done, bf16[6,640,128]{2,1,0:T(8,128)(2,1)S(1)} %collective-permute-done.3.same), custom_call_target="tpu_custom_call" | custom-call | flops 300000000 | tf_op jit(solution)/shard_map/spread/pallas_call | solution.py:214
  36.6 0.0 collective-permute-done.4.z2_sib
  36.6 2.6 %early.1 = (bf16[384,768]{1,0:T(8,128)(2,1)S(1)}, f32[384,768]{1,0:T(8,128)S(1)}) custom-call(s32[3]{0:T(128)S(1)} %pad_add_fusion.ids, bf16[384,768]{1,0:T(8,128)(2,1)S(1)} %copy-done.1, bf16[384,768]{1,0:T(8,128)(2,1)S(1)} %collective-permute-done.z2, bf16[384,768]{1,0:T(8,128)(2,1)} %collective-permute-done.4.z2_sib, bf16[1536,768]{1,0:T(8,128)(2,1)S(1)} %spread.1), custom_call_target="tpu_custom_call" | custom-call | flops 300000000 | tf_op jit(solution)/shard_map/early/pallas_call | solution.py:242
  39.2 0.0 collective-permute-done.1.q1
  39.2 0.1 collective-permute-start.5
  39.3 0.1 fusion
  39.4 0.6 %collective-permute-start.10 = (bf16[3,640,128]{2,1,0:T(8,128)(2,1)S(1)}, bf16[3,640,128]{2,1,0:T(8,128)(2,1)S(1)}, u32[]{:S(2)}, u32[]{:S(2)}) collective-permute-start(bf16[3,640,128]{2,1,0:T(8,128)(2,1)S(1)} %get-tuple-element.10), channel_id=1, source_target_pairs={{0,1},{1,0},{2,3},{3,2},{4,5},{5,4},{6,7},{7,6},{8,9},{9,8},{10,11... | collective-permute-start | bytes 1474568 | tf_op jit(solution)/shard_map/ppermute | solution.py:200
  40.0 0.1 collective-permute-start.9
  40.0 1.6 %middle.1.acc13 = f32[768,768]{1,0:T(8,128)S(1)} custom-call(s32[3]{0:T(128)S(1)} %pad_add_fusion.ids, bf16[384,768]{1,0:T(8,128)(2,1)S(1)} %stage.1.z1, bf16[384,768]{1,0:T(8,128)(2,1)S(1)} %collective-permute-done.7.z1_sib, bf16[1536,768]{1,0:T(8,128)(2,1)S(1)} %spread.1), custom_call_target="tpu_custom_call" | custom-call | tf_op jit(solution)/shard_map/middle/pallas_call | solution.py:251
  41.7 0.0 copy-start.2
  41.7 0.0 copy-start.4
  41.7 0.5 %collective-permute-start.8 = (bf16[192,768]{1,0:T(8,128)(2,1)S(1)}, bf16[192,768]{1,0:T(8,128)(2,1)S(1)}, u32[]{:S(2)}, u32[]{:S(2)}) collective-permute-start(bf16[192,768]{1,0:T(8,128)(2,1)S(1)} %collective-permute-done.6.q2), channel_id=1, source_target_pairs={{0,1},{1,0},{2,3},{3,2},{4,5},{5,4},{6,7},{7,6},{8,9},{9,8},{10,11... | collective-permute-start | bytes 884744 | tf_op jit(solution)/shard_map/ppermute | solution.py:200
  42.2 0.0 collective-permute-done.10.refs_1_
  42.2 0.5 %collective-permute-done.9.refs_0_ = bf16[3,640,128]{2,1,0:T(8,128)(2,1)S(1)} collective-permute-done((bf16[3,640,128]{2,1,0:T(8,128)(2,1)S(1)}, bf16[3,640,128]{2,1,0:T(8,128)(2,1)S(1)}, u32[]{:S(2)}, u32[]{:S(2)}) %collective-permute-start.9) | collective-permute-done | bytes 491552 | tf_op jit(solution)/shard_map/ppermute | solution.py:200
  42.7 1.9 %widen.1.full = bf16[1536,1536]{1,0:T(8,128)(2,1)S(1)} custom-call(s32[3]{0:T(128)S(1)} %pad_add_fusion.ids, s32[6,5]{1,0:T(8,128)S(1)} %copy-done.3, bf16[6,640,256]{2,1,0:T(8,128)(2,1)S(1)} %copy-done, bf16[6,640,128]{2,1,0:T(8,128)(2,1)S(1)} %collective-permute-done.3.same, bf16[3,640,128]{2,1,0:T(8,128)(2,1)S(1)} %collective-permute-done.9.refs_0_, ...), custom_call_target="tpu_custom_call" | custom-call | tf_op jit(solution)/shard_map/widen/pallas_call | solution.py:223
  44.6 0.0 collective-permute-done.8.q2_sib
  44.6 4.6 %final.1 = (bf16[6,640,128]{2,1,0:T(8,128)(2,1)}, bf16[6,256,128]{2,1,0:T(8,128)(2,1)}) custom-call(s32[3]{0:T(128)S(1)} %pad_add_fusion.ids, s32[6,5]{1,0:T(8,128)S(1)} %copy-done.3, s32[6]{0:T(128)S(1)} %copy-done.4, bf16[384,768]{1,0:T(8,128)(2,1)} %collective-permute-done.1.q1, bf16[384,768]{1,0:T(8,128)(2,1)S(1)} %collective-permute-done.5.q1_sib, ...), custom_call_target="tpu_custom_call" | custom-call | tf_op jit(solution)/shard_map/final/pallas_call | solution.py:262
  (10 shorter events, 0.0 us)
Async XLA Ops:
  0.6 34.4 %copy-start = (bf16[6,640,256]{2,1,0:T(8,128)(2,1)S(1)}, bf16[6,640,256]{2,1,0:T(8,128)(2,1)}, u32[]{:S(2)}) copy-start(bf16[6,640,256]{2,1,0:T(8,128)(2,1)} %panel.3) | copy-start | bytes 5898244
  0.6 34.4 %copy-start.3 = (s32[6,5]{1,0:T(8,128)S(1)}, s32[6,5]{1,0:T(8,128)}, u32[]{:S(2)}) copy-start(s32[6,5]{1,0:T(8,128)} %pat.5) | copy-start | bytes 364
  0.6 9.6 %collective-permute-start = (bf16[384,768]{1,0:T(8,128)(2,1)}, bf16[384,768]{1,0:T(8,128)(2,1)S(1)}, u32[]{:S(2)}, u32[]{:S(2)}) collective-permute-start(bf16[384,768]{1,0:T(8,128)(2,1)} %parent.1), channel_id=1, source_target_pairs={{0,8},{1,3},{2,10},{3,1},{4,12},{5,7},{6,14},{7,5},{8,0},{9,11},{1... | collective-permute-start | bytes 1769480 | tf_op jit(solution)/shard_map/ppermute | solution.py:197
  4.1 30.8 %collective-permute-start.3 = (bf16[6,640,128]{2,1,0:T(8,128)(2,1)}, bf16[6,640,128]{2,1,0:T(8,128)(2,1)S(1)}, u32[]{:S(2)}, u32[]{:S(2)}) collective-permute-start(bf16[6,640,128]{2,1,0:T(8,128)(2,1)} %constant_dynamic-slice_fusion), channel_id=1, source_target_pairs={{0,2},{2,0},{1,3},{3,1},{4,6},{6,4},{5,7},{7,5},{8,10},{10,8},{9,1... | collective-permute-start | bytes 2949128 | tf_op jit(solution)/shard_map/ppermute | solution.py:208
  4.6 15.7 %collective-permute-start.2 = (bf16[384,768]{1,0:T(8,128)(2,1)}, bf16[384,768]{1,0:T(8,128)(2,1)}, u32[]{:S(2)}, u32[]{:S(2)}) collective-permute-start(bf16[384,768]{1,0:T(8,128)(2,1)} %parent.1), channel_id=1, source_target_pairs={{0,12},{1,5},{2,14},{3,7},{4,8},{5,1},{6,10},{7,3},{8,4},{9,13},{1... | collective-permute-start | bytes 1769480 | tf_op jit(solution)/shard_map/ppermute | solution.py:197
  10.3 26.3 %collective-permute-start.4 = (bf16[384,768]{1,0:T(8,128)(2,1)S(1)}, bf16[384,768]{1,0:T(8,128)(2,1)}, u32[]{:S(2)}, u32[]{:S(2)}) collective-permute-start(bf16[384,768]{1,0:T(8,128)(2,1)S(1)} %collective-permute-done.z2), channel_id=1, source_target_pairs={{0,1},{1,0},{2,3},{3,2},{4,5},{5,4},{6,7},{7,6},{8,9},{9,8},{10,11... | collective-permute-start | bytes 1769480 | tf_op jit(solution)/shard_map/ppermute | solution.py:200
  19.6 19.7 %collective-permute-start.1 = (bf16[384,768]{1,0:T(8,128)(2,1)S(1)}, bf16[384,768]{1,0:T(8,128)(2,1)}, u32[]{:S(2)}, u32[]{:S(2)}) collective-permute-start(bf16[384,768]{1,0:T(8,128)(2,1)S(1)} %collective-permute-done.z2), channel_id=1, source_target_pairs={{0,2},{1,5},{2,0},{3,7},{4,6},{5,1},{6,4},{7,3},{8,10},{9,13},{10,... | collective-permute-start | bytes 1769480 | tf_op jit(solution)/shard_map/ppermute | solution.py:197
  20.3 19.8 %collective-permute-start.7 = (bf16[384,768]{1,0:T(8,128)(2,1)}, bf16[384,768]{1,0:T(8,128)(2,1)S(1)}, u32[]{:S(2)}, u32[]{:S(2)}) collective-permute-start(bf16[384,768]{1,0:T(8,128)(2,1)} %collective-permute-done.2.src), channel_id=1, source_target_pairs={{0,1},{1,0},{2,3},{3,2},{4,5},{5,4},{6,7},{7,6},{8,9},{9,8},{10,11... | collective-permute-start | bytes 1769480 | tf_op jit(solution)/shard_map/ppermute | solution.py:200
  31.6 10.1 %collective-permute-start.6 = (bf16[192,768]{1,0:T(8,128)(2,1)S(1)}, bf16[192,768]{1,0:T(8,128)(2,1)S(1)}, u32[]{:S(2)}, u32[]{:S(2)}) collective-permute-start(bf16[192,768]{1,0:T(8,128)(2,1)S(1)} %slice_select_fusion), channel_id=1, source_target_pairs={{0,2},{1,13},{2,0},{3,15},{4,6},{5,9},{6,4},{7,11},{8,10},{9,5},{1... | collective-permute-start | bytes 884744 | tf_op jit(solution)/shard_map/ppermute | solution.py:197
  35.0 1.6 %copy-start.1 = (bf16[384,768]{1,0:T(8,128)(2,1)S(1)}, bf16[384,768]{1,0:T(8,128)(2,1)}, u32[]{:S(2)}) copy-start(bf16[384,768]{1,0:T(8,128)(2,1)} %parent.1) | copy-start | bytes 1769476
  39.2 5.4 %collective-permute-start.5 = (bf16[384,768]{1,0:T(8,128)(2,1)}, bf16[384,768]{1,0:T(8,128)(2,1)S(1)}, u32[]{:S(2)}, u32[]{:S(2)}) collective-permute-start(bf16[384,768]{1,0:T(8,128)(2,1)} %collective-permute-done.1.q1), channel_id=1, source_target_pairs={{0,1},{1,0},{2,3},{3,2},{4,5},{5,4},{6,7},{7,6},{8,9},{9,8},{10,11... | collective-permute-start | bytes 1769480 | tf_op jit(solution)/shard_map/ppermute | solution.py:200
  39.4 2.8 %collective-permute-start.10 = (bf16[3,640,128]{2,1,0:T(8,128)(2,1)S(1)}, bf16[3,640,128]{2,1,0:T(8,128)(2,1)S(1)}, u32[]{:S(2)}, u32[]{:S(2)}) collective-permute-start(bf16[3,640,128]{2,1,0:T(8,128)(2,1)S(1)} %get-tuple-element.10), channel_id=1, source_target_pairs={{0,1},{1,0},{2,3},{3,2},{4,5},{5,4},{6,7},{7,6},{8,9},{9,8},{10,11... | collective-permute-start | bytes 1474568 | tf_op jit(solution)/shard_map/ppermute | solution.py:200
  40.0 2.8 %collective-permute-start.9 = (bf16[3,640,128]{2,1,0:T(8,128)(2,1)S(1)}, bf16[3,640,128]{2,1,0:T(8,128)(2,1)S(1)}, u32[]{:S(2)}, u32[]{:S(2)}) collective-permute-start(bf16[3,640,128]{2,1,0:T(8,128)(2,1)S(1)} %get-tuple-element.11), channel_id=1, source_target_pairs={{0,1},{1,0},{2,3},{3,2},{4,5},{5,4},{6,7},{7,6},{8,9},{9,8},{10,11... | collective-permute-start | bytes 1474568 | tf_op jit(solution)/shard_map/ppermute | solution.py:200
  41.7 2.9 %copy-start.2 = (bf16[6,256,128]{2,1,0:T(8,128)(2,1)S(1)}, bf16[6,256,128]{2,1,0:T(8,128)(2,1)}, u32[]{:S(2)}) copy-start(bf16[6,256,128]{2,1,0:T(8,128)(2,1)} %dinv.1) | copy-start | bytes 1179652
  41.7 2.9 %copy-start.4 = (s32[6]{0:T(128)S(1)}, s32[6]{0:T(128)}, u32[]{:S(2)}) copy-start(s32[6]{0:T(128)} %widths.1) | copy-start | bytes 76
  41.7 2.9 %collective-permute-start.8 = (bf16[192,768]{1,0:T(8,128)(2,1)S(1)}, bf16[192,768]{1,0:T(8,128)(2,1)S(1)}, u32[]{:S(2)}, u32[]{:S(2)}) collective-permute-start(bf16[192,768]{1,0:T(8,128)(2,1)S(1)} %collective-permute-done.6.q2), channel_id=1, source_target_pairs={{0,1},{1,0},{2,3},{3,2},{4,5},{5,4},{6,7},{7,6},{8,9},{9,8},{10,11... | collective-permute-start | bytes 884744 | tf_op jit(solution)/shard_map/ppermute | solution.py:200

commit v6 on v5

--- a/solution.py
+++ b/solution.py
@@ -58,33 +58,38 @@
             yield j, q, pl.ds(pl.multiple_of(start, 128), 128)
 
 
-def spread_kernel(ids, pat, panel, same, out):
+def ready_kernel(ids, pat, panel, out, wide_out):
     children, rows, width = panel.shape
     lane = width // 2
     chunks = rows // 128
     low = pl.ds(pl.multiple_of(ids[2] * lane, 128), lane)
     out[...] = jnp.zeros_like(out)
+    wide_out[...] = jnp.zeros_like(wide_out)
     for j, q, here in places(ids, pat, out.shape[0] // width, width, children, chunks):
-        mine = slice(j * lane, (j + 1) * lane)
-        band = slice(q % chunks * 128, (q % chunks + 1) * 128)
         if q < chunks:
-            out[here, mine] = panel[j, band, low]
-        else:
-            out[here, mine] = same[j, band, :]
-
-
-def widen_kernel(ids, pat, panel, same, *refs):
-    *cross, out = refs
-    children, rows, width = panel.shape
-    lane = width // 2
+            band = slice(q * 128, (q + 1) * 128)
+            out[here, j * lane : (j + 1) * lane] = panel[j, band, low]
+            wide_out[here, j * width : (j + 1) * width] = panel[j, band, :]
+
+
+def spread_kernel(ids, pat, same, ready, out):
+    children, rows, lane = same.shape
+    width, chunks = 2 * lane, rows // 128
+    out[...] = ready[...]
+    for j, q, here in places(ids, pat, out.shape[0] // width, width, children, chunks):
+        if q >= chunks:
+            out[here, j * lane : (j + 1) * lane] = same[j, (q - chunks) * 128 : (q - chunks + 1) * 128, :]
+
+
+def widen_kernel(ids, pat, same, *refs):
+    *cross, ready, out = refs
+    children, rows, lane = same.shape
+    width, chunks = 2 * lane, rows // 128
     s = ids[2]
-    chunks = rows // 128
-    out[...] = jnp.zeros_like(out)
+    out[...] = ready[...]
     for j, q, here in places(ids, pat, out.shape[0] // width, width, children, chunks):
-        band = slice(q % chunks * 128, (q % chunks + 1) * 128)
-        if q < chunks:
-            out[here, j * width : (j + 1) * width] = panel[j, band, :]
-        else:
+        if q >= chunks:
+            band = slice((q - chunks) * 128, (q - chunks + 1) * 128)
             part, at = divmod(j, cross[0].shape[0])
             out[here, pl.ds(pl.multiple_of(j * width + s * lane, 128), lane)] = same[j, band, :]
             out[here, pl.ds(pl.multiple_of(j * width + (1 - s) * lane, 128), lane)] = cross[part][at, band, :]
@@ -96,10 +101,6 @@
 
 def product(rows, spread):
     return jnp.dot(rows, spread, preferred_element_type=F32)
-
-
-def stage_kernel(src, out):
-    out[...] = src[...]
 
 
 def early_kernel(ids, parent, z2, z2_sib, spread, y0, acc2):
@@ -114,8 +115,8 @@
     s = ids[2]
     tall, wide = z1.shape
     low = spread[:wide, :]
-    acc13[:tall, :] = product(pick(s, z1_sib, z1), low)
-    acc13[tall:, :] = product(pick(s, z1, z1_sib), low)
+    acc13[pl.ds(pl.multiple_of(s * tall, 128), tall), :] = product(z1_sib[...], low)
+    acc13[pl.ds(pl.multiple_of((1 - s) * tall, 128), tall), :] = product(z1[...], low)
 
 
 def final_kernel(
@@ -160,6 +161,7 @@
 
 VMEM = pl.BlockSpec(memory_space=pltpu.VMEM)
 SMEM = pl.BlockSpec(memory_space=pltpu.SMEM)
+ANY = pl.BlockSpec(memory_space=pl.ANY)
 
 
 def cost(flops):
@@ -211,40 +213,44 @@
     q2 = send(jnp.where(s == 0, z1[cut:], z2[:cut]), across, along(3))
     cross = [sib(same[: children // 2]), sib(same[children // 2 :])]
 
+    placed = (
+        jax.ShapeDtypeStruct((2 * wide, lanes), BF16),
+        jax.ShapeDtypeStruct((2 * wide, 2 * lanes), BF16),
+    )
+    ready, wide_ready = pl.pallas_call(
+        ready_kernel,
+        out_shape=placed,
+        in_specs=[SMEM, SMEM, VMEM],
+        out_specs=(VMEM, VMEM),
+        cost_estimate=FREE,
+        compiler_params=params(8),
+        name="ready",
+    )(ids, pattern, panel)
     spread = pl.pallas_call(
         spread_kernel,
-        out_shape=jax.ShapeDtypeStruct((2 * wide, lanes), BF16),
-        in_specs=[SMEM, SMEM] + [VMEM] * 2,
+        out_shape=placed[0],
+        in_specs=[SMEM, SMEM, VMEM, VMEM],
         out_specs=VMEM,
-        cost_estimate=cost(300000000),
+        cost_estimate=cost(0),
         compiler_params=params(8),
         name="spread",
-    )(ids, pattern, panel, same)
+    )(ids, pattern, same, ready)
     full = pl.pallas_call(
         widen_kernel,
-        out_shape=jax.ShapeDtypeStruct((2 * wide, 2 * lanes), BF16),
+        out_shape=placed[1],
         in_specs=[SMEM, SMEM] + [VMEM] * 4,
         out_specs=VMEM,
         cost_estimate=FREE,
         compiler_params=params(8),
         name="widen",
-    )(ids, pattern, panel, same, *cross)
+    )(ids, pattern, same, *cross, wide_ready)
     y_shape = jax.ShapeDtypeStruct((tall, lanes), BF16)
-    z1_near = pl.pallas_call(
-        stage_kernel,
-        out_shape=jax.ShapeDtypeStruct(z1.shape, BF16),
-        in_specs=[VMEM],
-        out_specs=VMEM,
-        cost_estimate=FREE,
-        compiler_params=params(8),
-        name="stage",
-    )(z1)
     y0, acc2 = pl.pallas_call(
         early_kernel,
         out_shape=(y_shape, jax.ShapeDtypeStruct((tall, lanes), F32)),
         in_specs=[SMEM] + [VMEM] * 4,
         out_specs=(VMEM, VMEM),
-        cost_estimate=cost(300000000),
+        cost_estimate=cost(0),
         compiler_params=params(12),
         name="early",
     )(ids, parent, z2, sib(z2), spread)
@@ -256,8 +262,8 @@
         cost_estimate=FREE,
         compiler_params=params(12),
         name="middle",
-    )(ids, z1_near, sib(z1), spread)
-    q1, *_ = lax.optimization_barrier((q1, z1_near, spread, y0, acc2))
+    )(ids, z1, sib(z1), spread)
+    q1, *_ = lax.optimization_barrier((q1, spread, y0, acc2))
     q2, *_ = lax.optimization_barrier((q2, acc13))
     return pl.pallas_call(
         final_kernel,

time: 49.5 us -> 48.1 us (0.972)
  the two profiles are of different devices: /device:TPU:9 before, /device:TPU:0 now
where the time goes in v6:
time: 48.1 us; the launch traced here: 47.8 us
  waiting for transfers between devices  18.5 us (38%)
  Pallas kernels  13.1 us (27%)
  starting transfers between devices  11.4 us (24%)
  local copies, waits for them, and re-layouts  2.98 us (6%)
  other arithmetic  1.07 us (2%)
  between operations  0.75 us (2%)
    ppermute x4, waiting for transfers between devices, send(): return lax.ppermute(x, ('row', 'col', 'sub'), core(first, second))  16.3 us
    ppermute x4, starting transfers between devices, send(): return lax.ppermute(x, ('row', 'col', 'sub'), core(first, second))  9.28 us
    pallas_call x1, Pallas kernels, gathered(): pl.pallas_call(final_kernel, out_shape=(jax.ShapeDtypeStruct((children, r...  4.56 us
    pallas_call x1, Pallas kernels, gathered(): pl.pallas_call(early_kernel, out_shape=(y_shape, jax.ShapeDtypeStruct((ta...  2.8 us
    dynamic_slice x1, local copies, waits for them, and re-layouts, gathered(): mine = lax.dynamic_slice_in_dim(panel, s * lane, lane, 2)  2.21 us
    ppermute x1, waiting for transfers between devices, gathered(): same = lax.ppermute(mine, 'col', SWAP)  1.89 us
    pallas_call x1, Pallas kernels, gathered(): pl.pallas_call(middle_kernel, out_shape=jax.ShapeDtypeStruct((2 * tall, l...  1.63 us
    pallas_call x1, Pallas kernels, gathered(): pl.pallas_call(ready_kernel, out_shape=placed, in_specs=[SMEM, SMEM, VMEM...  1.52 us
  transfers between devices with their start and end apart: 11, of which 6 were waited for; matrix products, arithmetic and copies ran while one was open for 7% of the time, Pallas kernels for 18%

profile of v6, /device:TPU:0, one launch (start us, length us, event | category | flops | bytes accessed | tf_op | source)
XLA Modules:
  0.0 47.8 jit_solution(7721733580837995508)
XLA Ops:
  0.6 4.1 %collective-permute-start = (bf16[384,768]{1,0:T(8,128)(2,1)}, bf16[384,768]{1,0:T(8,128)(2,1)}, u32[]{:S(2)}, u32[]{:S(2)}) collective-permute-start(bf16[384,768]{1,0:T(8,128)(2,1)} %parent.1), channel_id=1, source_target_pairs={{0,8},{1,3},{2,10},{3,1},{4,12},{5,7},{6,14},{7,5},{8,0},{9,11},{1... | collective-permute-start | bytes 1769480 | tf_op jit(solution)/shard_map/ppermute | solution.py:199
  4.7 2.2 %constant_dynamic-slice_fusion = bf16[6,640,128]{2,1,0:T(8,128)(2,1)} fusion(bf16[6,640,256]{2,1,0:T(8,128)(2,1)} %panel.1, s32[]{:T(128)S(6)} %select_n.11), kind=kLoop, calls=%fused_computation.2 | loop fusion | bytes 1966084 | tf_op jit(solution)/shard_map/dynamic_slice | solution.py:209
  6.9 1.5 %collective-permute-start.2 = (bf16[6,640,128]{2,1,0:T(8,128)(2,1)}, bf16[6,640,128]{2,1,0:T(8,128)(2,1)S(1)}, u32[]{:S(2)}, u32[]{:S(2)}) collective-permute-start(bf16[6,640,128]{2,1,0:T(8,128)(2,1)} %constant_dynamic-slice_fusion), channel_id=1, source_target_pairs={{0,2},{2,0},{1,3},{3,1},{4,6},{6,4},{5,7},{7,5},{8,10},{10,8},{9,1... | collective-permute-start | bytes 2949128 | tf_op jit(solution)/shard_map/ppermute | solution.py:210
  8.4 1.5 %collective-permute-start.5 = (bf16[384,768]{1,0:T(8,128)(2,1)}, bf16[384,768]{1,0:T(8,128)(2,1)S(1)}, u32[]{:S(2)}, u32[]{:S(2)}) collective-permute-start(bf16[384,768]{1,0:T(8,128)(2,1)} %parent.1), channel_id=1, source_target_pairs={{0,12},{1,5},{2,14},{3,7},{4,8},{5,1},{6,10},{7,3},{8,4},{9,13},{1... | collective-permute-start | bytes 1769480 | tf_op jit(solution)/shard_map/ppermute | solution.py:199
  10.0 10.9 %collective-permute-done.z2 = bf16[384,768]{1,0:T(8,128)(2,1)} collective-permute-done((bf16[384,768]{1,0:T(8,128)(2,1)}, bf16[384,768]{1,0:T(8,128)(2,1)}, u32[]{:S(2)}, u32[]{:S(2)}) %collective-permute-start) | collective-permute-done | bytes 589856 | tf_op jit(solution)/shard_map/ppermute | solution.py:199
  20.8 0.0 collective-permute-start.3
  20.8 2.0 %collective-permute-start.1 = (bf16[384,768]{1,0:T(8,128)(2,1)}, bf16[384,768]{1,0:T(8,128)(2,1)}, u32[]{:S(2)}, u32[]{:S(2)}) collective-permute-start(bf16[384,768]{1,0:T(8,128)(2,1)} %collective-permute-done.z2), channel_id=1, source_target_pairs={{0,2},{1,5},{2,0},{3,7},{4,6},{5,1},{6,4},{7,3},{8,10},{9,13},{10,... | collective-permute-start | bytes 1769480 | tf_op jit(solution)/shard_map/ppermute | solution.py:199
  22.8 0.1 pad_add_fusion.ids
  22.9 0.7 %copy-done.3 = s32[6,5]{1,0:T(8,128)S(1)} copy-done((s32[6,5]{1,0:T(8,128)S(1)}, s32[6,5]{1,0:T(8,128)}, u32[]{:S(2)}) %copy-start.3) | copy-done | bytes 144
  23.6 1.5 %ready.1 = (bf16[1536,768]{1,0:T(8,128)(2,1)S(1)}, bf16[1536,1536]{1,0:T(8,128)(2,1)S(1)}) custom-call(s32[3]{0:T(128)S(1)} %pad_add_fusion.ids, s32[6,5]{1,0:T(8,128)S(1)} %copy-done.3, bf16[6,640,256]{2,1,0:T(8,128)(2,1)S(1)} %copy-done), custom_call_target="tpu_custom_call" | custom-call | tf_op jit(solution)/shard_map/ready/pallas_call | solution.py:220
  25.1 2.2 %collective-permute-done.5.z1 = bf16[384,768]{1,0:T(8,128)(2,1)S(1)} collective-permute-done((bf16[384,768]{1,0:T(8,128)(2,1)}, bf16[384,768]{1,0:T(8,128)(2,1)S(1)}, u32[]{:S(2)}, u32[]{:S(2)}) %collective-permute-start.5) | collective-permute-done | bytes 589856 | tf_op jit(solution)/shard_map/ppermute | solution.py:199
  27.3 0.0 collective-permute-start.7
  27.3 1.0 %slice_select_fusion = bf16[192,768]{1,0:T(8,128)(2,1)S(1)} fusion(bf16[384,768]{1,0:T(8,128)(2,1)} %collective-permute-done.z2, bf16[384,768]{1,0:T(8,128)(2,1)S(1)} %collective-permute-done.5.z1, pred[]{:T(512)S(6)} %eq.3), kind=kLoop, calls=%fused_computation | loop fusion | flops 147456 | bytes 884737 | tf_op jit(solution)/shard_map/jit(_where)/select_n | solution.py:213
  28.3 1.7 %collective-permute-start.6 = (bf16[192,768]{1,0:T(8,128)(2,1)S(1)}, bf16[192,768]{1,0:T(8,128)(2,1)S(1)}, u32[]{:S(2)}, u32[]{:S(2)}) collective-permute-start(bf16[192,768]{1,0:T(8,128)(2,1)S(1)} %slice_select_fusion), channel_id=1, source_target_pairs={{0,2},{1,13},{2,0},{3,15},{4,6},{5,9},{6,4},{7,11},{8,10},{9,5},{1... | collective-permute-start | bytes 884744 | tf_op jit(solution)/shard_map/ppermute | solution.py:199
  30.0 1.9 %collective-permute-done.2.same = bf16[6,640,128]{2,1,0:T(8,128)(2,1)S(1)} collective-permute-done((bf16[6,640,128]{2,1,0:T(8,128)(2,1)}, bf16[6,640,128]{2,1,0:T(8,128)(2,1)S(1)}, u32[]{:S(2)}, u32[]{:S(2)}) %collective-permute-start.2) | collective-permute-done | bytes 983072 | tf_op jit(solution)/shard_map/ppermute | solution.py:210
  31.9 1.1 %spread.1 = bf16[1536,768]{1,0:T(8,128)(2,1)S(1)} custom-call(s32[3]{0:T(128)S(1)} %pad_add_fusion.ids, s32[6,5]{1,0:T(8,128)S(1)} %copy-done.3, bf16[6,640,128]{2,1,0:T(8,128)(2,1)S(1)} %collective-permute-done.2.same, bf16[1536,768]{1,0:T(8,128)(2,1)S(1)} %get-tuple-element.8.ready), custom_call_target="tpu_custom_call" | custom-call | tf_op jit(solution)/shard_map/spread/pallas_call | solution.py:229
  33.0 0.0 collective-permute-done.3.z2_sib
  33.0 2.8 %early.1 = (bf16[384,768]{1,0:T(8,128)(2,1)S(1)}, f32[384,768]{1,0:T(8,128)S(1)}) custom-call(s32[3]{0:T(128)S(1)} %pad_add_fusion.ids, bf16[384,768]{1,0:T(8,128)(2,1)S(1)} %copy-done.1, bf16[384,768]{1,0:T(8,128)(2,1)} %collective-permute-done.z2, bf16[384,768]{1,0:T(8,128)(2,1)} %collective-permute-done.3.z2_sib, bf16[1536,768]{1,0:T(8,128)(2,1)S(1)} %spread.1), custom_call_target="tpu_custom_call" | custom-call | tf_op jit(solution)/shard_map/early/pallas_call | solution.py:248
  35.8 2.6 %collective-permute-done.1.q1 = bf16[384,768]{1,0:T(8,128)(2,1)} collective-permute-done((bf16[384,768]{1,0:T(8,128)(2,1)}, bf16[384,768]{1,0:T(8,128)(2,1)}, u32[]{:S(2)}, u32[]{:S(2)}) %collective-permute-start.1) | collective-permute-done | bytes 589856 | tf_op jit(solution)/shard_map/ppermute | solution.py:199
  38.4 0.0 collective-permute-start.4
  38.4 0.1 fusion
  38.4 0.6 %collective-permute-start.10 = (bf16[3,640,128]{2,1,0:T(8,128)(2,1)S(1)}, bf16[3,640,128]{2,1,0:T(8,128)(2,1)S(1)}, u32[]{:S(2)}, u32[]{:S(2)}) collective-permute-start(bf16[3,640,128]{2,1,0:T(8,128)(2,1)S(1)} %get-tuple-element.14), channel_id=1, source_target_pairs={{0,1},{1,0},{2,3},{3,2},{4,5},{5,4},{6,7},{7,6},{8,9},{9,8},{10,11... | collective-permute-start | bytes 1474568 | tf_op jit(solution)/shard_map/ppermute | solution.py:202
  39.0 0.1 collective-permute-start.9
  39.1 0.0 collective-permute-done.7.z1_sib
  39.1 1.6 %middle.1.acc13 = f32[768,768]{1,0:T(8,128)S(1)} custom-call(s32[3]{0:T(128)S(1)} %pad_add_fusion.ids, bf16[384,768]{1,0:T(8,128)(2,1)S(1)} %collective-permute-done.5.z1, bf16[384,768]{1,0:T(8,128)(2,1)S(1)} %collective-permute-done.7.z1_sib, bf16[1536,768]{1,0:T(8,128)(2,1)S(1)} %spread.1), custom_call_target="tpu_custom_call" | custom-call | tf_op jit(solution)/shard_map/middle/pallas_call | solution.py:257
  40.7 0.7 %collective-permute-done.6.q2 = bf16[192,768]{1,0:T(8,128)(2,1)S(1)} collective-permute-done((bf16[192,768]{1,0:T(8,128)(2,1)S(1)}, bf16[192,768]{1,0:T(8,128)(2,1)S(1)}, u32[]{:S(2)}, u32[]{:S(2)}) %collective-permute-start.6) | collective-permute-done | bytes 294944 | tf_op jit(solution)/shard_map/ppermute | solution.py:199
  41.4 0.0 collective-permute-start.8
  41.4 0.0 collective-permute-done.10.refs_1_
  41.4 0.3 collective-permute-done.9.refs_0_
  41.8 1.4 %widen.1.full = bf16[1536,1536]{1,0:T(8,128)(2,1)S(1)} custom-call(s32[3]{0:T(128)S(1)} %pad_add_fusion.ids, s32[6,5]{1,0:T(8,128)S(1)} %copy-done.4, bf16[6,640,128]{2,1,0:T(8,128)(2,1)S(1)} %collective-permute-done.2.same, bf16[3,640,128]{2,1,0:T(8,128)(2,1)S(1)} %collective-permute-done.9.refs_0_, ...), custom_call_target="tpu_custom_call" | custom-call | tf_op jit(solution)/shard_map/widen/pallas_call | solution.py:238
  43.2 0.0 collective-permute-done.4.q1_sib
  43.3 4.6 %final.1 = (bf16[6,640,128]{2,1,0:T(8,128)(2,1)}, bf16[6,256,128]{2,1,0:T(8,128)(2,1)}) custom-call(s32[3]{0:T(128)S(1)} %pad_add_fusion.ids, s32[6,5]{1,0:T(8,128)S(1)} %copy-done.4, s32[6]{0:T(128)S(1)} %copy-done.5, bf16[384,768]{1,0:T(8,128)(2,1)} %collective-permute-done.1.q1, bf16[384,768]{1,0:T(8,128)(2,1)S(1)} %collective-permute-done.4.q1_sib, ...), custom_call_target="tpu_custom_call" | custom-call | tf_op jit(solution)/shard_map/final/pallas_call | solution.py:268
  (12 shorter events, 0.0 us)
Async XLA Ops:
  0.6 22.3 %copy-start = (bf16[6,640,256]{2,1,0:T(8,128)(2,1)S(1)}, bf16[6,640,256]{2,1,0:T(8,128)(2,1)}, u32[]{:S(2)}) copy-start(bf16[6,640,256]{2,1,0:T(8,128)(2,1)} %panel.1) | copy-start | bytes 5898244
  0.6 20.2 %collective-permute-start = (bf16[384,768]{1,0:T(8,128)(2,1)}, bf16[384,768]{1,0:T(8,128)(2,1)}, u32[]{:S(2)}, u32[]{:S(2)}) collective-permute-start(bf16[384,768]{1,0:T(8,128)(2,1)} %parent.1), channel_id=1, source_target_pairs={{0,8},{1,3},{2,10},{3,1},{4,12},{5,7},{6,14},{7,5},{8,0},{9,11},{1... | collective-permute-start | bytes 1769480 | tf_op jit(solution)/shard_map/ppermute | solution.py:199
  6.9 24.9 %collective-permute-start.2 = (bf16[6,640,128]{2,1,0:T(8,128)(2,1)}, bf16[6,640,128]{2,1,0:T(8,128)(2,1)S(1)}, u32[]{:S(2)}, u32[]{:S(2)}) collective-permute-start(bf16[6,640,128]{2,1,0:T(8,128)(2,1)} %constant_dynamic-slice_fusion), channel_id=1, source_target_pairs={{0,2},{2,0},{1,3},{3,1},{4,6},{6,4},{5,7},{7,5},{8,10},{10,8},{9,1... | collective-permute-start | bytes 2949128 | tf_op jit(solution)/shard_map/ppermute | solution.py:210
  8.4 18.9 %collective-permute-start.5 = (bf16[384,768]{1,0:T(8,128)(2,1)}, bf16[384,768]{1,0:T(8,128)(2,1)S(1)}, u32[]{:S(2)}, u32[]{:S(2)}) collective-permute-start(bf16[384,768]{1,0:T(8,128)(2,1)} %parent.1), channel_id=1, source_target_pairs={{0,12},{1,5},{2,14},{3,7},{4,8},{5,1},{6,10},{7,3},{8,4},{9,13},{1... | collective-permute-start | bytes 1769480 | tf_op jit(solution)/shard_map/ppermute | solution.py:199
  20.8 12.1 %collective-permute-start.3 = (bf16[384,768]{1,0:T(8,128)(2,1)}, bf16[384,768]{1,0:T(8,128)(2,1)}, u32[]{:S(2)}, u32[]{:S(2)}) collective-permute-start(bf16[384,768]{1,0:T(8,128)(2,1)} %collective-permute-done.z2), channel_id=1, source_target_pairs={{0,1},{1,0},{2,3},{3,2},{4,5},{5,4},{6,7},{7,6},{8,9},{9,8},{10,11... | collective-permute-start | bytes 1769480 | tf_op jit(solution)/shard_map/ppermute | solution.py:202
  20.8 17.5 %collective-permute-start.1 = (bf16[384,768]{1,0:T(8,128)(2,1)}, bf16[384,768]{1,0:T(8,128)(2,1)}, u32[]{:S(2)}, u32[]{:S(2)}) collective-permute-start(bf16[384,768]{1,0:T(8,128)(2,1)} %collective-permute-done.z2), channel_id=1, source_target_pairs={{0,2},{1,5},{2,0},{3,7},{4,6},{5,1},{6,4},{7,3},{8,10},{9,13},{10,... | collective-permute-start | bytes 1769480 | tf_op jit(solution)/shard_map/ppermute | solution.py:199
  22.9 0.7 %copy-start.3 = (s32[6,5]{1,0:T(8,128)S(1)}, s32[6,5]{1,0:T(8,128)}, u32[]{:S(2)}) copy-start(s32[6,5]{1,0:T(8,128)} %pat.7) | copy-start | bytes 364
  27.3 11.8 %collective-permute-start.7 = (bf16[384,768]{1,0:T(8,128)(2,1)S(1)}, bf16[384,768]{1,0:T(8,128)(2,1)S(1)}, u32[]{:S(2)}, u32[]{:S(2)}) collective-permute-start(bf16[384,768]{1,0:T(8,128)(2,1)S(1)} %collective-permute-done.5.z1), channel_id=1, source_target_pairs={{0,1},{1,0},{2,3},{3,2},{4,5},{5,4},{6,7},{7,6},{8,9},{9,8},{10,11... | collective-permute-start | bytes 1769480 | tf_op jit(solution)/shard_map/ppermute | solution.py:202
  28.3 13.1 %collective-permute-start.6 = (bf16[192,768]{1,0:T(8,128)(2,1)S(1)}, bf16[192,768]{1,0:T(8,128)(2,1)S(1)}, u32[]{:S(2)}, u32[]{:S(2)}) collective-permute-start(bf16[192,768]{1,0:T(8,128)(2,1)S(1)} %slice_select_fusion), channel_id=1, source_target_pairs={{0,2},{1,13},{2,0},{3,15},{4,6},{5,9},{6,4},{7,11},{8,10},{9,5},{1... | collective-permute-start | bytes 884744 | tf_op jit(solution)/shard_map/ppermute | solution.py:199
  31.9 1.1 %copy-start.1 = (bf16[384,768]{1,0:T(8,128)(2,1)S(1)}, bf16[384,768]{1,0:T(8,128)(2,1)}, u32[]{:S(2)}) copy-start(bf16[384,768]{1,0:T(8,128)(2,1)} %parent.1) | copy-start | bytes 1769476
  38.4 4.9 %collective-permute-start.4 = (bf16[384,768]{1,0:T(8,128)(2,1)}, bf16[384,768]{1,0:T(8,128)(2,1)S(1)}, u32[]{:S(2)}, u32[]{:S(2)}) collective-permute-start(bf16[384,768]{1,0:T(8,128)(2,1)} %collective-permute-done.1.q1), channel_id=1, source_target_pairs={{0,1},{1,0},{2,3},{3,2},{4,5},{5,4},{6,7},{7,6},{8,9},{9,8},{10,11... | collective-permute-start | bytes 1769480 | tf_op jit(solution)/shard_map/ppermute | solution.py:202
  38.4 3.0 %collective-permute-start.10 = (bf16[3,640,128]{2,1,0:T(8,128)(2,1)S(1)}, bf16[3,640,128]{2,1,0:T(8,128)(2,1)S(1)}, u32[]{:S(2)}, u32[]{:S(2)}) collective-permute-start(bf16[3,640,128]{2,1,0:T(8,128)(2,1)S(1)} %get-tuple-element.14), channel_id=1, source_target_pairs={{0,1},{1,0},{2,3},{3,2},{4,5},{5,4},{6,7},{7,6},{8,9},{9,8},{10,11... | collective-permute-start | bytes 1474568 | tf_op jit(solution)/shard_map/ppermute | solution.py:202
  39.0 2.8 %copy-start.4 = (s32[6,5]{1,0:T(8,128)S(1)}, s32[6,5]{1,0:T(8,128)}, u32[]{:S(2)}) copy-start(s32[6,5]{1,0:T(8,128)} %pat.7) | copy-start | bytes 364
  39.0 2.8 %collective-permute-start.9 = (bf16[3,640,128]{2,1,0:T(8,128)(2,1)S(1)}, bf16[3,640,128]{2,1,0:T(8,128)(2,1)S(1)}, u32[]{:S(2)}, u32[]{:S(2)}) collective-permute-start(bf16[3,640,128]{2,1,0:T(8,128)(2,1)S(1)} %get-tuple-element.15), channel_id=1, source_target_pairs={{0,1},{1,0},{2,3},{3,2},{4,5},{5,4},{6,7},{7,6},{8,9},{9,8},{10,11... | collective-permute-start | bytes 1474568 | tf_op jit(solution)/shard_map/ppermute | solution.py:202
  41.4 1.8 %collective-permute-start.8 = (bf16[192,768]{1,0:T(8,128)(2,1)S(1)}, bf16[192,768]{1,0:T(8,128)(2,1)S(1)}, u32[]{:S(2)}, u32[]{:S(2)}) collective-permute-start(bf16[192,768]{1,0:T(8,128)(2,1)S(1)} %collective-permute-done.6.q2), channel_id=1, source_target_pairs={{0,1},{1,0},{2,3},{3,2},{4,5},{5,4},{6,7},{7,6},{8,9},{9,8},{10,11... | collective-permute-start | bytes 884744 | tf_op jit(solution)/shard_map/ppermute | solution.py:202
  41.8 1.5 %copy-start.2 = (bf16[6,256,128]{2,1,0:T(8,128)(2,1)S(1)}, bf16[6,256,128]{2,1,0:T(8,128)(2,1)}, u32[]{:S(2)}) copy-start(bf16[6,256,128]{2,1,0:T(8,128)(2,1)} %dinv.1) | copy-start | bytes 1179652
  41.8 1.5 %copy-start.5 = (s32[6]{0:T(128)S(1)}, s32[6]{0:T(128)}, u32[]{:S(2)}) copy-start(s32[6]{0:T(128)} %widths.1) | copy-start | bytes 76

commit v7 on v6

--- a/solution.py
+++ b/solution.py
@@ -111,7 +111,8 @@
     acc2[...] = product(pick(s, z2, z2_sib), low)
 
 
-def middle_kernel(ids, z1, z1_sib, spread, acc13):
+def middle_kernel(ids, z1, z1_sib, spread, tile, acc13, tile_out):
+    tile_out[...] = tile[...]
     s = ids[2]
     tall, wide = z1.shape
     low = spread[:wide, :]
@@ -254,16 +255,17 @@
         compiler_params=params(12),
         name="early",
     )(ids, parent, z2, sib(z2), spread)
-    acc13 = pl.pallas_call(
+    q1, *_ = lax.optimization_barrier((q1, spread, y0, acc2))
+    q1_sib = sib(q1)
+    acc13, q1 = pl.pallas_call(
         middle_kernel,
-        out_shape=jax.ShapeDtypeStruct((2 * tall, lanes), F32),
-        in_specs=[SMEM] + [VMEM] * 3,
-        out_specs=VMEM,
+        out_shape=(jax.ShapeDtypeStruct((2 * tall, lanes), F32), jax.ShapeDtypeStruct(q1.shape, BF16)),
+        in_specs=[SMEM] + [VMEM] * 4,
+        out_specs=(VMEM, VMEM),
         cost_estimate=FREE,
         compiler_params=params(12),
         name="middle",
-    )(ids, z1, sib(z1), spread)
-    q1, *_ = lax.optimization_barrier((q1, spread, y0, acc2))
+    )(ids, z1, sib(z1), spread, q1)
     q2, *_ = lax.optimization_barrier((q2, acc13))
     return pl.pallas_call(
         final_kernel,
@@ -277,7 +279,7 @@
         cost_estimate=FREE,
         compiler_params=params(16),
         name="final",
-    )(ids, pattern, widths, q1, sib(q1), q2, sib(q2), spread, full, y0, acc2, acc13, diag_inverse)
+    )(ids, pattern, widths, q1, q1_sib, q2, sib(q2), spread, full, y0, acc2, acc13, diag_inverse)
 
 
 def solution(mesh):

time: 48.1 us -> 47.7 us (level)
  waiting for transfers between devices: 18.5 us -> 17.6 us
    ppermute x4, waiting for transfers between devices: 16.3 us -> 15.7 us  [send(): return lax.ppermute(x, ('row', 'col', 'sub'), core(first, second))]
    pallas_call x1, Pallas kernels: 1.63 us -> 2.2 us  [gathered(): pl.pallas_call(middle_kernel, out_shape=(jax.ShapeDtypeStruct((2 * tall,...]
  transfers between devices with their start and end apart: 11 -> 11, of which waited for: 6 -> 5; matrix products, arithmetic and copies ran while one was open for 7% -> 7% of each run, Pallas kernels for 18% -> 19%
where the time goes in v7:
time: 47.7 us; the launch traced here: 47.4 us
  waiting for transfers between devices  17.6 us (37%)
  Pallas kernels  13.2 us (28%)
  starting transfers between devices  11.8 us (25%)
  local copies, waits for them, and re-layouts  2.99 us (6%)
  other arithmetic  1.07 us (2%)
  between operations  0.77 us (2%)
    ppermute x4, waiting for transfers between devices, send(): return lax.ppermute(x, ('row', 'col', 'sub'), core(first, second))  15.7 us
    ppermute x4, starting transfers between devices, send(): return lax.ppermute(x, ('row', 'col', 'sub'), core(first, second))  9.28 us
    pallas_call x1, Pallas kernels, gathered(): pl.pallas_call(final_kernel, out_shape=(jax.ShapeDtypeStruct((children, r...  4.1 us
    pallas_call x1, Pallas kernels, gathered(): pl.pallas_call(early_kernel, out_shape=(y_shape, jax.ShapeDtypeStruct((ta...  2.8 us
    dynamic_slice x1, local copies, waits for them, and re-layouts, gathered(): mine = lax.dynamic_slice_in_dim(panel, s * lane, lane, 2)  2.21 us
    pallas_call x1, Pallas kernels, gathered(): pl.pallas_call(middle_kernel, out_shape=(jax.ShapeDtypeStruct((2 * tall,...  2.2 us
    ppermute x1, waiting for transfers between devices, gathered(): same = lax.ppermute(mine, 'col', SWAP)  1.89 us
    pallas_call x1, Pallas kernels, gathered(): pl.pallas_call(ready_kernel, out_shape=placed, in_specs=[SMEM, SMEM, VMEM...  1.52 us
  transfers between devices with their start and end apart: 11, of which 5 were waited for; matrix products, arithmetic and copies ran while one was open for 7% of the time, Pallas kernels for 19%

profile of v7, /device:TPU:0, one launch (start us, length us, event | category | flops | bytes accessed | tf_op | source)
XLA Modules:
  0.0 47.4 jit_solution(3102126874427008074)
XLA Ops:
  0.6 4.1 %collective-permute-start.3 = (bf16[384,768]{1,0:T(8,128)(2,1)}, bf16[384,768]{1,0:T(8,128)(2,1)}, u32[]{:S(2)}, u32[]{:S(2)}) collective-permute-start(bf16[384,768]{1,0:T(8,128)(2,1)} %parent.1), channel_id=1, source_target_pairs={{0,8},{1,3},{2,10},{3,1},{4,12},{5,7},{6,14},{7,5},{8,0},{9,11},{1... | collective-permute-start | bytes 1769480 | tf_op jit(solution)/shard_map/ppermute | solution.py:200
  4.7 2.2 %constant_dynamic-slice_fusion = bf16[6,640,128]{2,1,0:T(8,128)(2,1)} fusion(bf16[6,640,256]{2,1,0:T(8,128)(2,1)} %panel.1, s32[]{:T(128)S(6)} %select_n.11), kind=kLoop, calls=%fused_computation.2 | loop fusion | bytes 1966084 | tf_op jit(solution)/shard_map/dynamic_slice | solution.py:210
  6.9 1.5 %collective-permute-start.2 = (bf16[6,640,128]{2,1,0:T(8,128)(2,1)}, bf16[6,640,128]{2,1,0:T(8,128)(2,1)S(1)}, u32[]{:S(2)}, u32[]{:S(2)}) collective-permute-start(bf16[6,640,128]{2,1,0:T(8,128)(2,1)} %constant_dynamic-slice_fusion), channel_id=1, source_target_pairs={{0,2},{2,0},{1,3},{3,1},{4,6},{6,4},{5,7},{7,5},{8,10},{10,8},{9,1... | collective-permute-start | bytes 2949128 | tf_op jit(solution)/shard_map/ppermute | solution.py:211
  8.4 1.5 %collective-permute-start = (bf16[384,768]{1,0:T(8,128)(2,1)}, bf16[384,768]{1,0:T(8,128)(2,1)S(1)}, u32[]{:S(2)}, u32[]{:S(2)}) collective-permute-start(bf16[384,768]{1,0:T(8,128)(2,1)} %parent.1), channel_id=1, source_target_pairs={{0,12},{1,5},{2,14},{3,7},{4,8},{5,1},{6,10},{7,3},{8,4},{9,13},{1... | collective-permute-start | bytes 1769480 | tf_op jit(solution)/shard_map/ppermute | solution.py:200
  10.0 10.9 %collective-permute-done.3.z2 = bf16[384,768]{1,0:T(8,128)(2,1)} collective-permute-done((bf16[384,768]{1,0:T(8,128)(2,1)}, bf16[384,768]{1,0:T(8,128)(2,1)}, u32[]{:S(2)}, u32[]{:S(2)}) %collective-permute-start.3) | collective-permute-done | bytes 589856 | tf_op jit(solution)/shard_map/ppermute | solution.py:200
  20.8 0.0 collective-permute-start.5
  20.8 2.0 %collective-permute-start.4 = (bf16[384,768]{1,0:T(8,128)(2,1)}, bf16[384,768]{1,0:T(8,128)(2,1)}, u32[]{:S(2)}, u32[]{:S(2)}) collective-permute-start(bf16[384,768]{1,0:T(8,128)(2,1)} %collective-permute-done.3.z2), channel_id=1, source_target_pairs={{0,2},{1,5},{2,0},{3,7},{4,6},{5,1},{6,4},{7,3},{8,10},{9,13},{10,... | collective-permute-start | bytes 1769480 | tf_op jit(solution)/shard_map/ppermute | solution.py:200
  22.8 0.1 pad_add_fusion.ids
  22.9 0.7 %copy-done.3 = s32[6,5]{1,0:T(8,128)S(1)} copy-done((s32[6,5]{1,0:T(8,128)S(1)}, s32[6,5]{1,0:T(8,128)}, u32[]{:S(2)}) %copy-start.3) | copy-done | bytes 144
  23.6 1.5 %ready.1 = (bf16[1536,768]{1,0:T(8,128)(2,1)S(1)}, bf16[1536,1536]{1,0:T(8,128)(2,1)S(1)}) custom-call(s32[3]{0:T(128)S(1)} %pad_add_fusion.ids, s32[6,5]{1,0:T(8,128)S(1)} %copy-done.3, bf16[6,640,256]{2,1,0:T(8,128)(2,1)S(1)} %copy-done), custom_call_target="tpu_custom_call" | custom-call | tf_op jit(solution)/shard_map/ready/pallas_call | solution.py:221
  25.1 2.2 %collective-permute-done.z1 = bf16[384,768]{1,0:T(8,128)(2,1)S(1)} collective-permute-done((bf16[384,768]{1,0:T(8,128)(2,1)}, bf16[384,768]{1,0:T(8,128)(2,1)S(1)}, u32[]{:S(2)}, u32[]{:S(2)}) %collective-permute-start) | collective-permute-done | bytes 589856 | tf_op jit(solution)/shard_map/ppermute | solution.py:200
  27.3 0.0 collective-permute-start.1
  27.3 1.0 %slice_select_fusion = bf16[192,768]{1,0:T(8,128)(2,1)S(1)} fusion(bf16[384,768]{1,0:T(8,128)(2,1)} %collective-permute-done.3.z2, bf16[384,768]{1,0:T(8,128)(2,1)S(1)} %collective-permute-done.z1, pred[]{:T(512)S(6)} %eq.3), kind=kLoop, calls=%fused_computation | loop fusion | flops 147456 | bytes 884737 | tf_op jit(solution)/shard_map/jit(_where)/select_n | solution.py:214
  28.3 1.7 %collective-permute-start.7 = (bf16[192,768]{1,0:T(8,128)(2,1)S(1)}, bf16[192,768]{1,0:T(8,128)(2,1)S(1)}, u32[]{:S(2)}, u32[]{:S(2)}) collective-permute-start(bf16[192,768]{1,0:T(8,128)(2,1)S(1)} %slice_select_fusion), channel_id=1, source_target_pairs={{0,2},{1,13},{2,0},{3,15},{4,6},{5,9},{6,4},{7,11},{8,10},{9,5},{1... | collective-permute-start | bytes 884744 | tf_op jit(solution)/shard_map/ppermute | solution.py:200
  30.0 1.9 %collective-permute-done.2.same = bf16[6,640,128]{2,1,0:T(8,128)(2,1)S(1)} collective-permute-done((bf16[6,640,128]{2,1,0:T(8,128)(2,1)}, bf16[6,640,128]{2,1,0:T(8,128)(2,1)S(1)}, u32[]{:S(2)}, u32[]{:S(2)}) %collective-permute-start.2) | collective-permute-done | bytes 983072 | tf_op jit(solution)/shard_map/ppermute | solution.py:211
  31.9 1.1 %spread.1 = bf16[1536,768]{1,0:T(8,128)(2,1)S(1)} custom-call(s32[3]{0:T(128)S(1)} %pad_add_fusion.ids, s32[6,5]{1,0:T(8,128)S(1)} %copy-done.3, bf16[6,640,128]{2,1,0:T(8,128)(2,1)S(1)} %collective-permute-done.2.same, bf16[1536,768]{1,0:T(8,128)(2,1)S(1)} %get-tuple-element.10.ready), custom_call_target="tpu_custom_call" | custom-call | tf_op jit(solution)/shard_map/spread/pallas_call | solution.py:230
  33.0 2.8 %early.1 = (bf16[384,768]{1,0:T(8,128)(2,1)S(1)}, f32[384,768]{1,0:T(8,128)S(1)}) custom-call(s32[3]{0:T(128)S(1)} %pad_add_fusion.ids, bf16[384,768]{1,0:T(8,128)(2,1)S(1)} %copy-done.1, bf16[384,768]{1,0:T(8,128)(2,1)} %collective-permute-done.3.z2, bf16[384,768]{1,0:T(8,128)(2,1)} %collective-permute-done.5.z2_sib, bf16[1536,768]{1,0:T(8,128)(2,1)S(1)} %spread.1), custom_call_target="tpu_custom_call" | custom-call | tf_op jit(solution)/shard_map/early/pallas_call | solution.py:249
  35.8 2.6 %collective-permute-done.4.tile = bf16[384,768]{1,0:T(8,128)(2,1)} collective-permute-done((bf16[384,768]{1,0:T(8,128)(2,1)}, bf16[384,768]{1,0:T(8,128)(2,1)}, u32[]{:S(2)}, u32[]{:S(2)}) %collective-permute-start.4) | collective-permute-done | bytes 589856 | tf_op jit(solution)/shard_map/ppermute | solution.py:200
  38.4 0.0 collective-permute-start.6
  38.4 0.1 fusion
  38.4 0.0 copy-start.4
  38.4 0.6 %collective-permute-start.10 = (bf16[3,640,128]{2,1,0:T(8,128)(2,1)S(1)}, bf16[3,640,128]{2,1,0:T(8,128)(2,1)S(1)}, u32[]{:S(2)}, u32[]{:S(2)}) collective-permute-start(bf16[3,640,128]{2,1,0:T(8,128)(2,1)S(1)} %get-tuple-element.18), channel_id=1, source_target_pairs={{0,1},{1,0},{2,3},{3,2},{4,5},{5,4},{6,7},{7,6},{8,9},{9,8},{10,11... | collective-permute-start | bytes 1474568 | tf_op jit(solution)/shard_map/ppermute | solution.py:203
  39.0 0.1 collective-permute-start.9
  39.1 2.2 %middle.1 = (f32[768,768]{1,0:T(8,128)S(1)}, bf16[384,768]{1,0:T(8,128)(2,1)S(1)}) custom-call(s32[3]{0:T(128)S(1)} %pad_add_fusion.ids, bf16[384,768]{1,0:T(8,128)(2,1)S(1)} %collective-permute-done.z1, bf16[384,768]{1,0:T(8,128)(2,1)S(1)} %collective-permute-done.1.z1_sib, bf16[1536,768]{1,0:T(8,128)(2,1)S(1)} %spread.1, ...), custom_call_target="tpu_custom_call" | custom-call | tf_op jit(solution)/shard_map/middle/pallas_call | solution.py:260
  41.3 0.1 collective-permute-done.7.q2
  41.4 0.4 collective-permute-start.8
  41.8 0.0 copy-start.2
  41.8 0.0 copy-start.5
  41.8 1.4 %widen.1.full = bf16[1536,1536]{1,0:T(8,128)(2,1)S(1)} custom-call(s32[3]{0:T(128)S(1)} %pad_add_fusion.ids, s32[6,5]{1,0:T(8,128)S(1)} %copy-done.4, bf16[6,640,128]{2,1,0:T(8,128)(2,1)S(1)} %collective-permute-done.2.same, bf16[3,640,128]{2,1,0:T(8,128)(2,1)S(1)} %collective-permute-done.9.refs_0_, ...), custom_call_target="tpu_custom_call" | custom-call | tf_op jit(solution)/shard_map/widen/pallas_call | solution.py:239
  43.3 0.0 collective-permute-done.8.q2_sib
  43.3 0.0 collective-permute-done.6.q1_sib
  43.3 4.1 %final.1 = (bf16[6,640,128]{2,1,0:T(8,128)(2,1)}, bf16[6,256,128]{2,1,0:T(8,128)(2,1)}) custom-call(s32[3]{0:T(128)S(1)} %pad_add_fusion.ids, s32[6,5]{1,0:T(8,128)S(1)} %copy-done.4, s32[6]{0:T(128)S(1)} %copy-done.5, bf16[384,768]{1,0:T(8,128)(2,1)S(1)} %get-tuple-element.14.q1, bf16[384,768]{1,0:T(8,128)(2,1)S(1)} %collective-permute-done.6.q1_sib, ...), custom_call_target="tpu_custom_call" | custom-call | tf_op jit(solution)/shard_map/final/pallas_call | solution.py:270
  (12 shorter events, 0.0 us)
Async XLA Ops:
  0.6 22.3 %copy-start = (bf16[6,640,256]{2,1,0:T(8,128)(2,1)S(1)}, bf16[6,640,256]{2,1,0:T(8,128)(2,1)}, u32[]{:S(2)}) copy-start(bf16[6,640,256]{2,1,0:T(8,128)(2,1)} %panel.1) | copy-start | bytes 5898244
  0.6 20.2 %collective-permute-start.3 = (bf16[384,768]{1,0:T(8,128)(2,1)}, bf16[384,768]{1,0:T(8,128)(2,1)}, u32[]{:S(2)}, u32[]{:S(2)}) collective-permute-start(bf16[384,768]{1,0:T(8,128)(2,1)} %parent.1), channel_id=1, source_target_pairs={{0,8},{1,3},{2,10},{3,1},{4,12},{5,7},{6,14},{7,5},{8,0},{9,11},{1... | collective-permute-start | bytes 1769480 | tf_op jit(solution)/shard_map/ppermute | solution.py:200
  6.9 24.9 %collective-permute-start.2 = (bf16[6,640,128]{2,1,0:T(8,128)(2,1)}, bf16[6,640,128]{2,1,0:T(8,128)(2,1)S(1)}, u32[]{:S(2)}, u32[]{:S(2)}) collective-permute-start(bf16[6,640,128]{2,1,0:T(8,128)(2,1)} %constant_dynamic-slice_fusion), channel_id=1, source_target_pairs={{0,2},{2,0},{1,3},{3,1},{4,6},{6,4},{5,7},{7,5},{8,10},{10,8},{9,1... | collective-permute-start | bytes 2949128 | tf_op jit(solution)/shard_map/ppermute | solution.py:211
  8.4 18.9 %collective-permute-start = (bf16[384,768]{1,0:T(8,128)(2,1)}, bf16[384,768]{1,0:T(8,128)(2,1)S(1)}, u32[]{:S(2)}, u32[]{:S(2)}) collective-permute-start(bf16[384,768]{1,0:T(8,128)(2,1)} %parent.1), channel_id=1, source_target_pairs={{0,12},{1,5},{2,14},{3,7},{4,8},{5,1},{6,10},{7,3},{8,4},{9,13},{1... | collective-permute-start | bytes 1769480 | tf_op jit(solution)/shard_map/ppermute | solution.py:200
  20.8 12.1 %collective-permute-start.5 = (bf16[384,768]{1,0:T(8,128)(2,1)}, bf16[384,768]{1,0:T(8,128)(2,1)}, u32[]{:S(2)}, u32[]{:S(2)}) collective-permute-start(bf16[384,768]{1,0:T(8,128)(2,1)} %collective-permute-done.3.z2), channel_id=1, source_target_pairs={{0,1},{1,0},{2,3},{3,2},{4,5},{5,4},{6,7},{7,6},{8,9},{9,8},{10,11... | collective-permute-start | bytes 1769480 | tf_op jit(solution)/shard_map/ppermute | solution.py:203
  20.8 17.5 %collective-permute-start.4 = (bf16[384,768]{1,0:T(8,128)(2,1)}, bf16[384,768]{1,0:T(8,128)(2,1)}, u32[]{:S(2)}, u32[]{:S(2)}) collective-permute-start(bf16[384,768]{1,0:T(8,128)(2,1)} %collective-permute-done.3.z2), channel_id=1, source_target_pairs={{0,2},{1,5},{2,0},{3,7},{4,6},{5,1},{6,4},{7,3},{8,10},{9,13},{10,... | collective-permute-start | bytes 1769480 | tf_op jit(solution)/shard_map/ppermute | solution.py:200
  22.9 0.7 %copy-start.3 = (s32[6,5]{1,0:T(8,128)S(1)}, s32[6,5]{1,0:T(8,128)}, u32[]{:S(2)}) copy-start(s32[6,5]{1,0:T(8,128)} %pat.7) | copy-start | bytes 364
  27.3 11.8 %collective-permute-start.1 = (bf16[384,768]{1,0:T(8,128)(2,1)S(1)}, bf16[384,768]{1,0:T(8,128)(2,1)S(1)}, u32[]{:S(2)}, u32[]{:S(2)}) collective-permute-start(bf16[384,768]{1,0:T(8,128)(2,1)S(1)} %collective-permute-done.z1), channel_id=1, source_target_pairs={{0,1},{1,0},{2,3},{3,2},{4,5},{5,4},{6,7},{7,6},{8,9},{9,8},{10,11... | collective-permute-start | bytes 1769480 | tf_op jit(solution)/shard_map/ppermute | solution.py:203
  28.3 13.1 %collective-permute-start.7 = (bf16[192,768]{1,0:T(8,128)(2,1)S(1)}, bf16[192,768]{1,0:T(8,128)(2,1)S(1)}, u32[]{:S(2)}, u32[]{:S(2)}) collective-permute-start(bf16[192,768]{1,0:T(8,128)(2,1)S(1)} %slice_select_fusion), channel_id=1, source_target_pairs={{0,2},{1,13},{2,0},{3,15},{4,6},{5,9},{6,4},{7,11},{8,10},{9,5},{1... | collective-permute-start | bytes 884744 | tf_op jit(solution)/shard_map/ppermute | solution.py:200
  31.9 1.1 %copy-start.1 = (bf16[384,768]{1,0:T(8,128)(2,1)S(1)}, bf16[384,768]{1,0:T(8,128)(2,1)}, u32[]{:S(2)}) copy-start(bf16[384,768]{1,0:T(8,128)(2,1)} %parent.1) | copy-start | bytes 1769476
  38.4 5.0 %collective-permute-start.6 = (bf16[384,768]{1,0:T(8,128)(2,1)}, bf16[384,768]{1,0:T(8,128)(2,1)S(1)}, u32[]{:S(2)}, u32[]{:S(2)}) collective-permute-start(bf16[384,768]{1,0:T(8,128)(2,1)} %collective-permute-done.4.tile), channel_id=1, source_target_pairs={{0,1},{1,0},{2,3},{3,2},{4,5},{5,4},{6,7},{7,6},{8,9},{9,8},{10,11... | collective-permute-start | bytes 1769480 | tf_op jit(solution)/shard_map/ppermute | solution.py:203
  38.4 3.4 %copy-start.4 = (s32[6,5]{1,0:T(8,128)S(1)}, s32[6,5]{1,0:T(8,128)}, u32[]{:S(2)}) copy-start(s32[6,5]{1,0:T(8,128)} %pat.7) | copy-start | bytes 364
  38.4 3.4 %collective-permute-start.10 = (bf16[3,640,128]{2,1,0:T(8,128)(2,1)S(1)}, bf16[3,640,128]{2,1,0:T(8,128)(2,1)S(1)}, u32[]{:S(2)}, u32[]{:S(2)}) collective-permute-start(bf16[3,640,128]{2,1,0:T(8,128)(2,1)S(1)} %get-tuple-element.18), channel_id=1, source_target_pairs={{0,1},{1,0},{2,3},{3,2},{4,5},{5,4},{6,7},{7,6},{8,9},{9,8},{10,11... | collective-permute-start | bytes 1474568 | tf_op jit(solution)/shard_map/ppermute | solution.py:203
  39.0 2.8 %collective-permute-start.9 = (bf16[3,640,128]{2,1,0:T(8,128)(2,1)S(1)}, bf16[3,640,128]{2,1,0:T(8,128)(2,1)S(1)}, u32[]{:S(2)}, u32[]{:S(2)}) collective-permute-start(bf16[3,640,128]{2,1,0:T(8,128)(2,1)S(1)} %get-tuple-element.19), channel_id=1, source_target_pairs={{0,1},{1,0},{2,3},{3,2},{4,5},{5,4},{6,7},{7,6},{8,9},{9,8},{10,11... | collective-permute-start | bytes 1474568 | tf_op jit(solution)/shard_map/ppermute | solution.py:203
  41.4 1.9 %collective-permute-start.8 = (bf16[192,768]{1,0:T(8,128)(2,1)S(1)}, bf16[192,768]{1,0:T(8,128)(2,1)S(1)}, u32[]{:S(2)}, u32[]{:S(2)}) collective-permute-start(bf16[192,768]{1,0:T(8,128)(2,1)S(1)} %collective-permute-done.7.q2), channel_id=1, source_target_pairs={{0,1},{1,0},{2,3},{3,2},{4,5},{5,4},{6,7},{7,6},{8,9},{9,8},{10,11... | collective-permute-start | bytes 884744 | tf_op jit(solution)/shard_map/ppermute | solution.py:203
  41.8 1.5 %copy-start.2 = (bf16[6,256,128]{2,1,0:T(8,128)(2,1)S(1)}, bf16[6,256,128]{2,1,0:T(8,128)(2,1)}, u32[]{:S(2)}) copy-start(bf16[6,256,128]{2,1,0:T(8,128)(2,1)} %dinv.1) | copy-start | bytes 1179652
  41.8 1.5 %copy-start.5 = (s32[6]{0:T(128)S(1)}, s32[6]{0:T(128)}, u32[]{:S(2)}) copy-start(s32[6]{0:T(128)} %widths.1) | copy-start | bytes 76

commit v8 on v7

--- a/solution.py
+++ b/solution.py
@@ -103,21 +103,22 @@
     return jnp.dot(rows, spread, preferred_element_type=F32)
 
 
-def early_kernel(ids, parent, z2, z2_sib, spread, y0, acc2):
+def early_kernel(ids, pat, same, ready, parent, z1, z2, z2_sib, spread, y0, acc2, acc_own):
     s = ids[2]
     wide = parent.shape[1]
+    spread_kernel(ids, pat, same, ready, spread)
     low, high = spread[:wide, :], spread[wide:, :]
     y0[...] = (-(product(parent[...], low) + product(pick(s, z2_sib, z2), high))).astype(BF16)
     acc2[...] = product(pick(s, z2, z2_sib), low)
-
-
-def middle_kernel(ids, z1, z1_sib, spread, tile, acc13, tile_out):
+    acc_own[...] = product(z1[...], low)
+
+
+def middle_kernel(ids, acc_own, z1_sib, spread, tile, acc13, tile_out):
+    s = ids[2]
+    tall, wide = z1_sib.shape
     tile_out[...] = tile[...]
-    s = ids[2]
-    tall, wide = z1.shape
-    low = spread[:wide, :]
-    acc13[pl.ds(pl.multiple_of(s * tall, 128), tall), :] = product(z1_sib[...], low)
-    acc13[pl.ds(pl.multiple_of((1 - s) * tall, 128), tall), :] = product(z1[...], low)
+    acc13[pl.ds(pl.multiple_of(s * tall, 128), tall), :] = product(z1_sib[...], spread[:wide, :])
+    acc13[pl.ds(pl.multiple_of((1 - s) * tall, 128), tall), :] = acc_own[...]
 
 
 def final_kernel(
@@ -227,15 +228,6 @@
         compiler_params=params(8),
         name="ready",
     )(ids, pattern, panel)
-    spread = pl.pallas_call(
-        spread_kernel,
-        out_shape=placed[0],
-        in_specs=[SMEM, SMEM, VMEM, VMEM],
-        out_specs=VMEM,
-        cost_estimate=cost(0),
-        compiler_params=params(8),
-        name="spread",
-    )(ids, pattern, same, ready)
     full = pl.pallas_call(
         widen_kernel,
         out_shape=placed[1],
@@ -246,16 +238,17 @@
         name="widen",
     )(ids, pattern, same, *cross, wide_ready)
     y_shape = jax.ShapeDtypeStruct((tall, lanes), BF16)
-    y0, acc2 = pl.pallas_call(
+    acc_shape = jax.ShapeDtypeStruct((tall, lanes), F32)
+    spread, y0, acc2, acc_own = pl.pallas_call(
         early_kernel,
-        out_shape=(y_shape, jax.ShapeDtypeStruct((tall, lanes), F32)),
-        in_specs=[SMEM] + [VMEM] * 4,
-        out_specs=(VMEM, VMEM),
+        out_shape=(placed[0], y_shape, acc_shape, acc_shape),
+        in_specs=[SMEM, SMEM] + [VMEM] * 6,
+        out_specs=(VMEM,) * 4,
         cost_estimate=cost(0),
         compiler_params=params(12),
         name="early",
-    )(ids, parent, z2, sib(z2), spread)
-    q1, *_ = lax.optimization_barrier((q1, spread, y0, acc2))
+    )(ids, pattern, same, ready, parent, z1, z2, sib(z2))
+    q1, *_ = lax.optimization_barrier((q1, spread, y0, acc2, acc_own))
     q1_sib = sib(q1)
     acc13, q1 = pl.pallas_call(
         middle_kernel,
@@ -265,7 +258,7 @@
         cost_estimate=FREE,
         compiler_params=params(12),
         name="middle",
-    )(ids, z1, sib(z1), spread, q1)
+    )(ids, acc_own, sib(z1), spread, q1)
     q2, *_ = lax.optimization_barrier((q2, acc13))
     return pl.pallas_call(
         final_kernel,

time: 47.7 us -> 47.6 us (level)
  waiting for transfers between devices: 17.6 us -> 18.4 us
  Pallas kernels: 13.2 us -> 12.6 us
    ppermute x4, waiting for transfers between devices: 15.7 us -> 16.4 us  [send(): return lax.ppermute(x, ('row', 'col', 'sub'), core(first, second))]
    pallas_call x2 -> x1, Pallas kernels: 3.9 us -> 3.66 us  [gathered(): pl.pallas_call(early_kernel, out_shape=(placed[0], y_shape, acc_shape, ac...]
  transfers between devices with their start and end apart: 11 -> 11, of which waited for: 5 -> 6; matrix products, arithmetic and copies ran while one was open for 7% -> 7% of each run, Pallas kernels for 19% -> 18%
where the time goes in v8:
time: 47.6 us; the launch traced here: 47.4 us
  waiting for transfers between devices  18.4 us (39%)
  Pallas kernels  12.6 us (26%)
  starting transfers between devices  11.5 us (24%)
  local copies, waits for them, and re-layouts  3.04 us (6%)
  other arithmetic  1.07 us (2%)
  between operations  0.73 us (2%)
    ppermute x4, waiting for transfers between devices, send(): return lax.ppermute(x, ('row', 'col', 'sub'), core(first, second))  16.4 us
    ppermute x4, starting transfers between devices, send(): return lax.ppermute(x, ('row', 'col', 'sub'), core(first, second))  9.28 us
    pallas_call x1, Pallas kernels, gathered(): pl.pallas_call(final_kernel, out_shape=(jax.ShapeDtypeStruct((children, r...  4.1 us
    pallas_call x1, Pallas kernels, gathered(): pl.pallas_call(early_kernel, out_shape=(placed[0], y_shape, acc_shape, ac...  3.66 us
    dynamic_slice x1, local copies, waits for them, and re-layouts, gathered(): mine = lax.dynamic_slice_in_dim(panel, s * lane, lane, 2)  2.22 us
    pallas_call x1, Pallas kernels, gathered(): pl.pallas_call(middle_kernel, out_shape=(jax.ShapeDtypeStruct((2 * tall,...  1.87 us
    ppermute x1, waiting for transfers between devices, gathered(): same = lax.ppermute(mine, 'col', SWAP)  1.71 us
    pallas_call x1, Pallas kernels, gathered(): pl.pallas_call(ready_kernel, out_shape=placed, in_specs=[SMEM, SMEM, VMEM...  1.52 us
  transfers between devices with their start and end apart: 11, of which 6 were waited for; matrix products, arithmetic and copies ran while one was open for 7% of the time, Pallas kernels for 18%

profile of v8, /device:TPU:0, one launch (start us, length us, event | category | flops | bytes accessed | tf_op | source)
XLA Modules:
  0.0 47.4 jit_solution(8164235926785125829)
XLA Ops:
  0.6 4.1 %collective-permute-start.2 = (bf16[384,768]{1,0:T(8,128)(2,1)}, bf16[384,768]{1,0:T(8,128)(2,1)S(1)}, u32[]{:S(2)}, u32[]{:S(2)}) collective-permute-start(bf16[384,768]{1,0:T(8,128)(2,1)} %parent.1), channel_id=1, source_target_pairs={{0,8},{1,3},{2,10},{3,1},{4,12},{5,7},{6,14},{7,5},{8,0},{9,11},{1... | collective-permute-start | bytes 1769480 | tf_op jit(solution)/shard_map/ppermute | solution.py:201
  4.7 2.2 %constant_dynamic-slice_fusion = bf16[6,640,128]{2,1,0:T(8,128)(2,1)} fusion(bf16[6,640,256]{2,1,0:T(8,128)(2,1)} %panel.1, s32[]{:T(128)S(6)} %select_n.11), kind=kLoop, calls=%fused_computation.2 | loop fusion | bytes 1966084 | tf_op jit(solution)/shard_map/dynamic_slice | solution.py:211
  7.0 1.5 %collective-permute-start = (bf16[6,640,128]{2,1,0:T(8,128)(2,1)}, bf16[6,640,128]{2,1,0:T(8,128)(2,1)S(1)}, u32[]{:S(2)}, u32[]{:S(2)}) collective-permute-start(bf16[6,640,128]{2,1,0:T(8,128)(2,1)} %constant_dynamic-slice_fusion), channel_id=1, source_target_pairs={{0,2},{2,0},{1,3},{3,1},{4,6},{6,4},{5,7},{7,5},{8,10},{10,8},{9,1... | collective-permute-start | bytes 2949128 | tf_op jit(solution)/shard_map/ppermute | solution.py:212
  8.5 1.5 %collective-permute-start.1 = (bf16[384,768]{1,0:T(8,128)(2,1)}, bf16[384,768]{1,0:T(8,128)(2,1)}, u32[]{:S(2)}, u32[]{:S(2)}) collective-permute-start(bf16[384,768]{1,0:T(8,128)(2,1)} %parent.1), channel_id=1, source_target_pairs={{0,12},{1,5},{2,14},{3,7},{4,8},{5,1},{6,10},{7,3},{8,4},{9,13},{1... | collective-permute-start | bytes 1769480 | tf_op jit(solution)/shard_map/ppermute | solution.py:201
  10.0 10.7 %collective-permute-done.2.z2 = bf16[384,768]{1,0:T(8,128)(2,1)S(1)} collective-permute-done((bf16[384,768]{1,0:T(8,128)(2,1)}, bf16[384,768]{1,0:T(8,128)(2,1)S(1)}, u32[]{:S(2)}, u32[]{:S(2)}) %collective-permute-start.2) | collective-permute-done | bytes 589856 | tf_op jit(solution)/shard_map/ppermute | solution.py:201
  20.7 0.0 collective-permute-start.3
  20.7 2.0 %collective-permute-start.5 = (bf16[384,768]{1,0:T(8,128)(2,1)S(1)}, bf16[384,768]{1,0:T(8,128)(2,1)}, u32[]{:S(2)}, u32[]{:S(2)}) collective-permute-start(bf16[384,768]{1,0:T(8,128)(2,1)S(1)} %collective-permute-done.2.z2), channel_id=1, source_target_pairs={{0,2},{1,5},{2,0},{3,7},{4,6},{5,1},{6,4},{7,3},{8,10},{9,13},{10,... | collective-permute-start | bytes 1769480 | tf_op jit(solution)/shard_map/ppermute | solution.py:201
  22.7 0.1 pad_add_fusion.ids
  22.8 0.7 %copy-done.3 = s32[6,5]{1,0:T(8,128)S(1)} copy-done((s32[6,5]{1,0:T(8,128)S(1)}, s32[6,5]{1,0:T(8,128)}, u32[]{:S(2)}) %copy-start.3) | copy-done | bytes 144
  23.6 1.5 %ready.1 = (bf16[1536,768]{1,0:T(8,128)(2,1)S(1)}, bf16[1536,1536]{1,0:T(8,128)(2,1)S(1)}) custom-call(s32[3]{0:T(128)S(1)} %pad_add_fusion.ids, s32[6,5]{1,0:T(8,128)S(1)} %copy-done.3, bf16[6,640,256]{2,1,0:T(8,128)(2,1)S(1)} %copy-done), custom_call_target="tpu_custom_call" | custom-call | tf_op jit(solution)/shard_map/ready/pallas_call | solution.py:222
  25.1 2.4 %collective-permute-done.1.z1 = bf16[384,768]{1,0:T(8,128)(2,1)} collective-permute-done((bf16[384,768]{1,0:T(8,128)(2,1)}, bf16[384,768]{1,0:T(8,128)(2,1)}, u32[]{:S(2)}, u32[]{:S(2)}) %collective-permute-start.1) | collective-permute-done | bytes 589856 | tf_op jit(solution)/shard_map/ppermute | solution.py:201
  27.5 0.0 collective-permute-start.4
  27.5 1.0 %slice_select_fusion = bf16[192,768]{1,0:T(8,128)(2,1)S(1)} fusion(bf16[384,768]{1,0:T(8,128)(2,1)S(1)} %collective-permute-done.2.z2, bf16[384,768]{1,0:T(8,128)(2,1)} %collective-permute-done.1.z1, pred[]{:T(512)S(6)} %eq.3), kind=kLoop, calls=%fused_computation | loop fusion | flops 147456 | bytes 884737 | tf_op jit(solution)/shard_map/jit(_where)/select_n | solution.py:215
  28.5 1.6 %collective-permute-start.7 = (bf16[192,768]{1,0:T(8,128)(2,1)S(1)}, bf16[192,768]{1,0:T(8,128)(2,1)S(1)}, u32[]{:S(2)}, u32[]{:S(2)}) collective-permute-start(bf16[192,768]{1,0:T(8,128)(2,1)S(1)} %slice_select_fusion), channel_id=1, source_target_pairs={{0,2},{1,13},{2,0},{3,15},{4,6},{5,9},{6,4},{7,11},{8,10},{9,5},{1... | collective-permute-start | bytes 884744 | tf_op jit(solution)/shard_map/ppermute | solution.py:201
  30.2 1.7 %collective-permute-done.same = bf16[6,640,128]{2,1,0:T(8,128)(2,1)S(1)} collective-permute-done((bf16[6,640,128]{2,1,0:T(8,128)(2,1)}, bf16[6,640,128]{2,1,0:T(8,128)(2,1)S(1)}, u32[]{:S(2)}, u32[]{:S(2)}) %collective-permute-start) | collective-permute-done | bytes 983072 | tf_op jit(solution)/shard_map/ppermute | solution.py:212
  31.9 0.0 collective-permute-done.3.z2_sib
  31.9 3.7 %early.1 = (bf16[1536,768]{1,0:T(8,128)(2,1)S(1)}, bf16[384,768]{1,0:T(8,128)(2,1)S(1)}, f32[384,768]{1,0:T(8,128)S(1)}, f32[384,768]{1,0:T(8,128)S(1)}) custom-call(s32[3]{0:T(128)S(1)} %pad_add_fusion.ids, s32[6,5]{1,0:T(8,128)S(1)} %copy-done.4, bf16[6,640,128]{2,1,0:T(8,128)(2,1)S(1)} %collective-permute-done.same, ...), custom_call_target="tpu_custom_call" | custom-call | tf_op jit(solution)/shard_map/early/pallas_call | solution.py:242
  35.5 2.8 %collective-permute-done.5.tile = bf16[384,768]{1,0:T(8,128)(2,1)} collective-permute-done((bf16[384,768]{1,0:T(8,128)(2,1)S(1)}, bf16[384,768]{1,0:T(8,128)(2,1)}, u32[]{:S(2)}, u32[]{:S(2)}) %collective-permute-start.5) | collective-permute-done | bytes 589856 | tf_op jit(solution)/shard_map/ppermute | solution.py:201
  38.4 0.0 collective-permute-start.6
  38.4 0.1 fusion
  38.4 0.6 %collective-permute-start.10 = (bf16[3,640,128]{2,1,0:T(8,128)(2,1)S(1)}, bf16[3,640,128]{2,1,0:T(8,128)(2,1)S(1)}, u32[]{:S(2)}, u32[]{:S(2)}) collective-permute-start(bf16[3,640,128]{2,1,0:T(8,128)(2,1)S(1)} %get-tuple-element.22), channel_id=1, source_target_pairs={{0,1},{1,0},{2,3},{3,2},{4,5},{5,4},{6,7},{7,6},{8,9},{9,8},{10,11... | collective-permute-start | bytes 1474568 | tf_op jit(solution)/shard_map/ppermute | solution.py:204
  39.0 0.1 collective-permute-start.9
  39.1 0.0 collective-permute-done.4.z1_sib
  39.1 1.9 %middle.1 = (f32[768,768]{1,0:T(8,128)S(1)}, bf16[384,768]{1,0:T(8,128)(2,1)S(1)}) custom-call(s32[3]{0:T(128)S(1)} %pad_add_fusion.ids, f32[384,768]{1,0:T(8,128)S(1)} %get-tuple-element.13.acc_own, bf16[384,768]{1,0:T(8,128)(2,1)S(1)} %collective-permute-done.4.z1_sib, bf16[1536,768]{1,0:T(8,128)(2,1)S(1)} %get-tuple-element.14.spread, ...), custom_call_target="tpu_custom_call" | custom-call | tf_op jit(solution)/shard_map/middle/pallas_call | solution.py:253
  41.0 0.5 collective-permute-done.7.q2
  41.4 0.1 collective-permute-start.8
  41.5 0.0 collective-permute-done.10.refs_1_
  41.5 0.3 collective-permute-done.9.refs_0_
  41.8 1.4 %widen.1.full = bf16[1536,1536]{1,0:T(8,128)(2,1)S(1)} custom-call(s32[3]{0:T(128)S(1)} %pad_add_fusion.ids, s32[6,5]{1,0:T(8,128)S(1)} %copy-done.4, bf16[6,640,128]{2,1,0:T(8,128)(2,1)S(1)} %collective-permute-done.same, bf16[3,640,128]{2,1,0:T(8,128)(2,1)S(1)} %collective-permute-done.9.refs_0_, bf16[3,640,128]{2,1,0:T(8,128)(2,1)S(1)} %collective-permute-done.10.refs_1_, ...), custom_call_target="tpu_custom_call" | custom-call | tf_op jit(solution)/shard_map/widen/pallas_call | solution.py:231
  43.2 0.0 collective-permute-done.8.q2_sib
  43.2 0.0 collective-permute-done.6.q1_sib
  43.3 4.1 %final.1 = (bf16[6,640,128]{2,1,0:T(8,128)(2,1)}, bf16[6,256,128]{2,1,0:T(8,128)(2,1)}) custom-call(s32[3]{0:T(128)S(1)} %pad_add_fusion.ids, s32[6,5]{1,0:T(8,128)S(1)} %copy-done.4, s32[6]{0:T(128)S(1)} %copy-done.5, bf16[384,768]{1,0:T(8,128)(2,1)S(1)} %get-tuple-element.18.q1, bf16[384,768]{1,0:T(8,128)(2,1)S(1)} %collective-permute-done.6.q1_sib, ...), custom_call_target="tpu_custom_call" | custom-call | tf_op jit(solution)/shard_map/final/pallas_call | solution.py:263
  (11 shorter events, 0.0 us)
Async XLA Ops:
  0.6 22.2 %copy-start = (bf16[6,640,256]{2,1,0:T(8,128)(2,1)S(1)}, bf16[6,640,256]{2,1,0:T(8,128)(2,1)}, u32[]{:S(2)}) copy-start(bf16[6,640,256]{2,1,0:T(8,128)(2,1)} %panel.1) | copy-start | bytes 5898244
  0.6 20.1 %collective-permute-start.2 = (bf16[384,768]{1,0:T(8,128)(2,1)}, bf16[384,768]{1,0:T(8,128)(2,1)S(1)}, u32[]{:S(2)}, u32[]{:S(2)}) collective-permute-start(bf16[384,768]{1,0:T(8,128)(2,1)} %parent.1), channel_id=1, source_target_pairs={{0,8},{1,3},{2,10},{3,1},{4,12},{5,7},{6,14},{7,5},{8,0},{9,11},{1... | collective-permute-start | bytes 1769480 | tf_op jit(solution)/shard_map/ppermute | solution.py:201
  4.7 27.1 %copy-start.4 = (s32[6,5]{1,0:T(8,128)S(1)}, s32[6,5]{1,0:T(8,128)}, u32[]{:S(2)}) copy-start(s32[6,5]{1,0:T(8,128)} %pat.7) | copy-start | bytes 364
  7.0 24.9 %collective-permute-start = (bf16[6,640,128]{2,1,0:T(8,128)(2,1)}, bf16[6,640,128]{2,1,0:T(8,128)(2,1)S(1)}, u32[]{:S(2)}, u32[]{:S(2)}) collective-permute-start(bf16[6,640,128]{2,1,0:T(8,128)(2,1)} %constant_dynamic-slice_fusion), channel_id=1, source_target_pairs={{0,2},{2,0},{1,3},{3,1},{4,6},{6,4},{5,7},{7,5},{8,10},{10,8},{9,1... | collective-permute-start | bytes 2949128 | tf_op jit(solution)/shard_map/ppermute | solution.py:212
  8.5 19.1 %collective-permute-start.1 = (bf16[384,768]{1,0:T(8,128)(2,1)}, bf16[384,768]{1,0:T(8,128)(2,1)}, u32[]{:S(2)}, u32[]{:S(2)}) collective-permute-start(bf16[384,768]{1,0:T(8,128)(2,1)} %parent.1), channel_id=1, source_target_pairs={{0,12},{1,5},{2,14},{3,7},{4,8},{5,1},{6,10},{7,3},{8,4},{9,13},{1... | collective-permute-start | bytes 1769480 | tf_op jit(solution)/shard_map/ppermute | solution.py:201
  20.7 11.1 %collective-permute-start.3 = (bf16[384,768]{1,0:T(8,128)(2,1)S(1)}, bf16[384,768]{1,0:T(8,128)(2,1)}, u32[]{:S(2)}, u32[]{:S(2)}) collective-permute-start(bf16[384,768]{1,0:T(8,128)(2,1)S(1)} %collective-permute-done.2.z2), channel_id=1, source_target_pairs={{0,1},{1,0},{2,3},{3,2},{4,5},{5,4},{6,7},{7,6},{8,9},{9,8},{10,11... | collective-permute-start | bytes 1769480 | tf_op jit(solution)/shard_map/ppermute | solution.py:204
  20.7 17.6 %collective-permute-start.5 = (bf16[384,768]{1,0:T(8,128)(2,1)S(1)}, bf16[384,768]{1,0:T(8,128)(2,1)}, u32[]{:S(2)}, u32[]{:S(2)}) collective-permute-start(bf16[384,768]{1,0:T(8,128)(2,1)S(1)} %collective-permute-done.2.z2), channel_id=1, source_target_pairs={{0,2},{1,5},{2,0},{3,7},{4,6},{5,1},{6,4},{7,3},{8,10},{9,13},{10,... | collective-permute-start | bytes 1769480 | tf_op jit(solution)/shard_map/ppermute | solution.py:201
  22.7 9.1 %copy-start.1 = (bf16[384,768]{1,0:T(8,128)(2,1)S(1)}, bf16[384,768]{1,0:T(8,128)(2,1)}, u32[]{:S(2)}) copy-start(bf16[384,768]{1,0:T(8,128)(2,1)} %parent.1) | copy-start | bytes 1769476
  22.8 0.7 %copy-start.3 = (s32[6,5]{1,0:T(8,128)S(1)}, s32[6,5]{1,0:T(8,128)}, u32[]{:S(2)}) copy-start(s32[6,5]{1,0:T(8,128)} %pat.7) | copy-start | bytes 364
  27.5 11.6 %collective-permute-start.4 = (bf16[384,768]{1,0:T(8,128)(2,1)}, bf16[384,768]{1,0:T(8,128)(2,1)S(1)}, u32[]{:S(2)}, u32[]{:S(2)}) collective-permute-start(bf16[384,768]{1,0:T(8,128)(2,1)} %collective-permute-done.1.z1), channel_id=1, source_target_pairs={{0,1},{1,0},{2,3},{3,2},{4,5},{5,4},{6,7},{7,6},{8,9},{9,8},{10,11... | collective-permute-start | bytes 1769480 | tf_op jit(solution)/shard_map/ppermute | solution.py:204
  28.5 12.9 %collective-permute-start.7 = (bf16[192,768]{1,0:T(8,128)(2,1)S(1)}, bf16[192,768]{1,0:T(8,128)(2,1)S(1)}, u32[]{:S(2)}, u32[]{:S(2)}) collective-permute-start(bf16[192,768]{1,0:T(8,128)(2,1)S(1)} %slice_select_fusion), channel_id=1, source_target_pairs={{0,2},{1,13},{2,0},{3,15},{4,6},{5,9},{6,4},{7,11},{8,10},{9,5},{1... | collective-permute-start | bytes 884744 | tf_op jit(solution)/shard_map/ppermute | solution.py:201
  38.4 4.9 %collective-permute-start.6 = (bf16[384,768]{1,0:T(8,128)(2,1)}, bf16[384,768]{1,0:T(8,128)(2,1)S(1)}, u32[]{:S(2)}, u32[]{:S(2)}) collective-permute-start(bf16[384,768]{1,0:T(8,128)(2,1)} %collective-permute-done.5.tile), channel_id=1, source_target_pairs={{0,1},{1,0},{2,3},{3,2},{4,5},{5,4},{6,7},{7,6},{8,9},{9,8},{10,11... | collective-permute-start | bytes 1769480 | tf_op jit(solution)/shard_map/ppermute | solution.py:204
  38.4 3.0 %collective-permute-start.10 = (bf16[3,640,128]{2,1,0:T(8,128)(2,1)S(1)}, bf16[3,640,128]{2,1,0:T(8,128)(2,1)S(1)}, u32[]{:S(2)}, u32[]{:S(2)}) collective-permute-start(bf16[3,640,128]{2,1,0:T(8,128)(2,1)S(1)} %get-tuple-element.22), channel_id=1, source_target_pairs={{0,1},{1,0},{2,3},{3,2},{4,5},{5,4},{6,7},{7,6},{8,9},{9,8},{10,11... | collective-permute-start | bytes 1474568 | tf_op jit(solution)/shard_map/ppermute | solution.py:204
  39.0 2.8 %collective-permute-start.9 = (bf16[3,640,128]{2,1,0:T(8,128)(2,1)S(1)}, bf16[3,640,128]{2,1,0:T(8,128)(2,1)S(1)}, u32[]{:S(2)}, u32[]{:S(2)}) collective-permute-start(bf16[3,640,128]{2,1,0:T(8,128)(2,1)S(1)} %get-tuple-element.23), channel_id=1, source_target_pairs={{0,1},{1,0},{2,3},{3,2},{4,5},{5,4},{6,7},{7,6},{8,9},{9,8},{10,11... | collective-permute-start | bytes 1474568 | tf_op jit(solution)/shard_map/ppermute | solution.py:204
  41.4 1.8 %collective-permute-start.8 = (bf16[192,768]{1,0:T(8,128)(2,1)S(1)}, bf16[192,768]{1,0:T(8,128)(2,1)S(1)}, u32[]{:S(2)}, u32[]{:S(2)}) collective-permute-start(bf16[192,768]{1,0:T(8,128)(2,1)S(1)} %collective-permute-done.7.q2), channel_id=1, source_target_pairs={{0,1},{1,0},{2,3},{3,2},{4,5},{5,4},{6,7},{7,6},{8,9},{9,8},{10,11... | collective-permute-start | bytes 884744 | tf_op jit(solution)/shard_map/ppermute | solution.py:204
  41.8 1.5 %copy-start.2 = (bf16[6,256,128]{2,1,0:T(8,128)(2,1)S(1)}, bf16[6,256,128]{2,1,0:T(8,128)(2,1)}, u32[]{:S(2)}) copy-start(bf16[6,256,128]{2,1,0:T(8,128)(2,1)} %dinv.1) | copy-start | bytes 1179652
  41.8 1.5 %copy-start.5 = (s32[6]{0:T(128)S(1)}, s32[6]{0:T(128)}, u32[]{:S(2)}) copy-start(s32[6]{0:T(128)} %widths.1) | copy-start | bytes 76

commit v9 on v8

--- a/solution.py
+++ b/solution.py
@@ -137,10 +137,10 @@
     place(0, y0[...])
     cut = q2.shape[0]
     for k, first, second, acc, begin in (
+        (1, q1_sib, q1, acc13.at[:tall, :], 0),
+        (2, q1, q1_sib, acc2, 0),
         (3, q2_sib, q2, acc13.at[tall : tall + cut, :], 0),
         (3, q2, q2_sib, acc13.at[tall + cut :, :], cut),
-        (1, q1_sib, q1, acc13.at[:tall, :], 0),
-        (2, q1, q1_sib, acc2, 0),
     ):
         place(k, (-(acc[...] + product(pick(s, first, second), high))).astype(BF16), begin)
     chunks = off_out.shape[1] // 128

time: 47.6 us -> 47.6 us (level)
  no operation moved by 1% of the time
where the time goes in v9:
time: 47.6 us; the launch traced here: 47.4 us
  waiting for transfers between devices  18.4 us (39%)
  Pallas kernels  12.6 us (26%)
  starting transfers between devices  11.5 us (24%)
  local copies, waits for them, and re-layouts  3.04 us (6%)
  other arithmetic  1.07 us (2%)
  between operations  0.73 us (2%)
    ppermute x4, waiting for transfers between devices, send(): return lax.ppermute(x, ('row', 'col', 'sub'), core(first, second))  16.4 us
    ppermute x4, starting transfers between devices, send(): return lax.ppermute(x, ('row', 'col', 'sub'), core(first, second))  9.28 us
    pallas_call x1, Pallas kernels, gathered(): pl.pallas_call(final_kernel, out_shape=(jax.ShapeDtypeStruct((children, r...  4.1 us
    pallas_call x1, Pallas kernels, gathered(): pl.pallas_call(early_kernel, out_shape=(placed[0], y_shape, acc_shape, ac...  3.66 us
    dynamic_slice x1, local copies, waits for them, and re-layouts, gathered(): mine = lax.dynamic_slice_in_dim(panel, s * lane, lane, 2)  2.22 us
    pallas_call x1, Pallas kernels, gathered(): pl.pallas_call(middle_kernel, out_shape=(jax.ShapeDtypeStruct((2 * tall,...  1.87 us
    ppermute x1, waiting for transfers between devices, gathered(): same = lax.ppermute(mine, 'col', SWAP)  1.71 us
    pallas_call x1, Pallas kernels, gathered(): pl.pallas_call(ready_kernel, out_shape=placed, in_specs=[SMEM, SMEM, VMEM...  1.52 us
  transfers between devices with their start and end apart: 11, of which 6 were waited for; matrix products, arithmetic and copies ran while one was open for 7% of the time, Pallas kernels for 18%

profile of v9, /device:TPU:0, one launch (start us, length us, event | category | flops | bytes accessed | tf_op | source)
XLA Modules:
  0.0 47.4 jit_solution(6249875243349644595)
XLA Ops:
  0.6 4.1 %collective-permute-start.2 = (bf16[384,768]{1,0:T(8,128)(2,1)}, bf16[384,768]{1,0:T(8,128)(2,1)S(1)}, u32[]{:S(2)}, u32[]{:S(2)}) collective-permute-start(bf16[384,768]{1,0:T(8,128)(2,1)} %parent.1), channel_id=1, source_target_pairs={{0,8},{1,3},{2,10},{3,1},{4,12},{5,7},{6,14},{7,5},{8,0},{9,11},{1... | collective-permute-start | bytes 1769480 | tf_op jit(solution)/shard_map/ppermute | solution.py:201
  4.7 2.2 %constant_dynamic-slice_fusion = bf16[6,640,128]{2,1,0:T(8,128)(2,1)} fusion(bf16[6,640,256]{2,1,0:T(8,128)(2,1)} %panel.1, s32[]{:T(128)S(6)} %select_n.11), kind=kLoop, calls=%fused_computation.2 | loop fusion | bytes 1966084 | tf_op jit(solution)/shard_map/dynamic_slice | solution.py:211
  7.0 1.5 %collective-permute-start = (bf16[6,640,128]{2,1,0:T(8,128)(2,1)}, bf16[6,640,128]{2,1,0:T(8,128)(2,1)S(1)}, u32[]{:S(2)}, u32[]{:S(2)}) collective-permute-start(bf16[6,640,128]{2,1,0:T(8,128)(2,1)} %constant_dynamic-slice_fusion), channel_id=1, source_target_pairs={{0,2},{2,0},{1,3},{3,1},{4,6},{6,4},{5,7},{7,5},{8,10},{10,8},{9,1... | collective-permute-start | bytes 2949128 | tf_op jit(solution)/shard_map/ppermute | solution.py:212
  8.5 1.5 %collective-permute-start.1 = (bf16[384,768]{1,0:T(8,128)(2,1)}, bf16[384,768]{1,0:T(8,128)(2,1)}, u32[]{:S(2)}, u32[]{:S(2)}) collective-permute-start(bf16[384,768]{1,0:T(8,128)(2,1)} %parent.1), channel_id=1, source_target_pairs={{0,12},{1,5},{2,14},{3,7},{4,8},{5,1},{6,10},{7,3},{8,4},{9,13},{1... | collective-permute-start | bytes 1769480 | tf_op jit(solution)/shard_map/ppermute | solution.py:201
  10.0 10.7 %collective-permute-done.2.z2 = bf16[384,768]{1,0:T(8,128)(2,1)S(1)} collective-permute-done((bf16[384,768]{1,0:T(8,128)(2,1)}, bf16[384,768]{1,0:T(8,128)(2,1)S(1)}, u32[]{:S(2)}, u32[]{:S(2)}) %collective-permute-start.2) | collective-permute-done | bytes 589856 | tf_op jit(solution)/shard_map/ppermute | solution.py:201
  20.7 0.0 collective-permute-start.3
  20.7 2.0 %collective-permute-start.5 = (bf16[384,768]{1,0:T(8,128)(2,1)S(1)}, bf16[384,768]{1,0:T(8,128)(2,1)}, u32[]{:S(2)}, u32[]{:S(2)}) collective-permute-start(bf16[384,768]{1,0:T(8,128)(2,1)S(1)} %collective-permute-done.2.z2), channel_id=1, source_target_pairs={{0,2},{1,5},{2,0},{3,7},{4,6},{5,1},{6,4},{7,3},{8,10},{9,13},{10,... | collective-permute-start | bytes 1769480 | tf_op jit(solution)/shard_map/ppermute | solution.py:201
  22.7 0.1 pad_add_fusion.ids
  22.8 0.7 %copy-done.3 = s32[6,5]{1,0:T(8,128)S(1)} copy-done((s32[6,5]{1,0:T(8,128)S(1)}, s32[6,5]{1,0:T(8,128)}, u32[]{:S(2)}) %copy-start.3) | copy-done | bytes 144
  23.6 1.5 %ready.1 = (bf16[1536,768]{1,0:T(8,128)(2,1)S(1)}, bf16[1536,1536]{1,0:T(8,128)(2,1)S(1)}) custom-call(s32[3]{0:T(128)S(1)} %pad_add_fusion.ids, s32[6,5]{1,0:T(8,128)S(1)} %copy-done.3, bf16[6,640,256]{2,1,0:T(8,128)(2,1)S(1)} %copy-done), custom_call_target="tpu_custom_call" | custom-call | tf_op jit(solution)/shard_map/ready/pallas_call | solution.py:222
  25.1 2.4 %collective-permute-done.1.z1 = bf16[384,768]{1,0:T(8,128)(2,1)} collective-permute-done((bf16[384,768]{1,0:T(8,128)(2,1)}, bf16[384,768]{1,0:T(8,128)(2,1)}, u32[]{:S(2)}, u32[]{:S(2)}) %collective-permute-start.1) | collective-permute-done | bytes 589856 | tf_op jit(solution)/shard_map/ppermute | solution.py:201
  27.5 0.0 collective-permute-start.4
  27.5 1.0 %slice_select_fusion = bf16[192,768]{1,0:T(8,128)(2,1)S(1)} fusion(bf16[384,768]{1,0:T(8,128)(2,1)S(1)} %collective-permute-done.2.z2, bf16[384,768]{1,0:T(8,128)(2,1)} %collective-permute-done.1.z1, pred[]{:T(512)S(6)} %eq.3), kind=kLoop, calls=%fused_computation | loop fusion | flops 147456 | bytes 884737 | tf_op jit(solution)/shard_map/jit(_where)/select_n | solution.py:215
  28.5 1.6 %collective-permute-start.7 = (bf16[192,768]{1,0:T(8,128)(2,1)S(1)}, bf16[192,768]{1,0:T(8,128)(2,1)S(1)}, u32[]{:S(2)}, u32[]{:S(2)}) collective-permute-start(bf16[192,768]{1,0:T(8,128)(2,1)S(1)} %slice_select_fusion), channel_id=1, source_target_pairs={{0,2},{1,13},{2,0},{3,15},{4,6},{5,9},{6,4},{7,11},{8,10},{9,5},{1... | collective-permute-start | bytes 884744 | tf_op jit(solution)/shard_map/ppermute | solution.py:201
  30.2 1.7 %collective-permute-done.same = bf16[6,640,128]{2,1,0:T(8,128)(2,1)S(1)} collective-permute-done((bf16[6,640,128]{2,1,0:T(8,128)(2,1)}, bf16[6,640,128]{2,1,0:T(8,128)(2,1)S(1)}, u32[]{:S(2)}, u32[]{:S(2)}) %collective-permute-start) | collective-permute-done | bytes 983072 | tf_op jit(solution)/shard_map/ppermute | solution.py:212
  31.9 0.0 collective-permute-done.3.z2_sib
  31.9 3.7 %early.1 = (bf16[1536,768]{1,0:T(8,128)(2,1)S(1)}, bf16[384,768]{1,0:T(8,128)(2,1)S(1)}, f32[384,768]{1,0:T(8,128)S(1)}, f32[384,768]{1,0:T(8,128)S(1)}) custom-call(s32[3]{0:T(128)S(1)} %pad_add_fusion.ids, s32[6,5]{1,0:T(8,128)S(1)} %copy-done.4, bf16[6,640,128]{2,1,0:T(8,128)(2,1)S(1)} %collective-permute-done.same, ...), custom_call_target="tpu_custom_call" | custom-call | tf_op jit(solution)/shard_map/early/pallas_call | solution.py:242
  35.5 2.8 %collective-permute-done.5.tile = bf16[384,768]{1,0:T(8,128)(2,1)} collective-permute-done((bf16[384,768]{1,0:T(8,128)(2,1)S(1)}, bf16[384,768]{1,0:T(8,128)(2,1)}, u32[]{:S(2)}, u32[]{:S(2)}) %collective-permute-start.5) | collective-permute-done | bytes 589856 | tf_op jit(solution)/shard_map/ppermute | solution.py:201
  38.4 0.0 collective-permute-start.6
  38.4 0.1 fusion
  38.4 0.6 %collective-permute-start.10 = (bf16[3,640,128]{2,1,0:T(8,128)(2,1)S(1)}, bf16[3,640,128]{2,1,0:T(8,128)(2,1)S(1)}, u32[]{:S(2)}, u32[]{:S(2)}) collective-permute-start(bf16[3,640,128]{2,1,0:T(8,128)(2,1)S(1)} %get-tuple-element.22), channel_id=1, source_target_pairs={{0,1},{1,0},{2,3},{3,2},{4,5},{5,4},{6,7},{7,6},{8,9},{9,8},{10,11... | collective-permute-start | bytes 1474568 | tf_op jit(solution)/shard_map/ppermute | solution.py:204
  39.0 0.1 collective-permute-start.9
  39.1 0.0 collective-permute-done.4.z1_sib
  39.1 1.9 %middle.1 = (f32[768,768]{1,0:T(8,128)S(1)}, bf16[384,768]{1,0:T(8,128)(2,1)S(1)}) custom-call(s32[3]{0:T(128)S(1)} %pad_add_fusion.ids, f32[384,768]{1,0:T(8,128)S(1)} %get-tuple-element.13.acc_own, bf16[384,768]{1,0:T(8,128)(2,1)S(1)} %collective-permute-done.4.z1_sib, bf16[1536,768]{1,0:T(8,128)(2,1)S(1)} %get-tuple-element.14.spread, ...), custom_call_target="tpu_custom_call" | custom-call | tf_op jit(solution)/shard_map/middle/pallas_call | solution.py:253
  41.0 0.5 collective-permute-done.7.q2
  41.4 0.1 collective-permute-start.8
  41.5 0.0 collective-permute-done.10.refs_1_
  41.5 0.3 collective-permute-done.9.refs_0_
  41.8 1.4 %widen.1.full = bf16[1536,1536]{1,0:T(8,128)(2,1)S(1)} custom-call(s32[3]{0:T(128)S(1)} %pad_add_fusion.ids, s32[6,5]{1,0:T(8,128)S(1)} %copy-done.4, bf16[6,640,128]{2,1,0:T(8,128)(2,1)S(1)} %collective-permute-done.same, bf16[3,640,128]{2,1,0:T(8,128)(2,1)S(1)} %collective-permute-done.9.refs_0_, bf16[3,640,128]{2,1,0:T(8,128)(2,1)S(1)} %collective-permute-done.10.refs_1_, ...), custom_call_target="tpu_custom_call" | custom-call | tf_op jit(solution)/shard_map/widen/pallas_call | solution.py:231
  43.2 0.0 collective-permute-done.8.q2_sib
  43.2 0.0 collective-permute-done.6.q1_sib
  43.3 4.1 %final.1 = (bf16[6,640,128]{2,1,0:T(8,128)(2,1)}, bf16[6,256,128]{2,1,0:T(8,128)(2,1)}) custom-call(s32[3]{0:T(128)S(1)} %pad_add_fusion.ids, s32[6,5]{1,0:T(8,128)S(1)} %copy-done.4, s32[6]{0:T(128)S(1)} %copy-done.5, bf16[384,768]{1,0:T(8,128)(2,1)S(1)} %get-tuple-element.18.q1, bf16[384,768]{1,0:T(8,128)(2,1)S(1)} %collective-permute-done.6.q1_sib, ...), custom_call_target="tpu_custom_call" | custom-call | tf_op jit(solution)/shard_map/final/pallas_call | solution.py:263
  (11 shorter events, 0.0 us)
Async XLA Ops:
  0.6 22.2 %copy-start = (bf16[6,640,256]{2,1,0:T(8,128)(2,1)S(1)}, bf16[6,640,256]{2,1,0:T(8,128)(2,1)}, u32[]{:S(2)}) copy-start(bf16[6,640,256]{2,1,0:T(8,128)(2,1)} %panel.1) | copy-start | bytes 5898244
  0.6 20.1 %collective-permute-start.2 = (bf16[384,768]{1,0:T(8,128)(2,1)}, bf16[384,768]{1,0:T(8,128)(2,1)S(1)}, u32[]{:S(2)}, u32[]{:S(2)}) collective-permute-start(bf16[384,768]{1,0:T(8,128)(2,1)} %parent.1), channel_id=1, source_target_pairs={{0,8},{1,3},{2,10},{3,1},{4,12},{5,7},{6,14},{7,5},{8,0},{9,11},{1... | collective-permute-start | bytes 1769480 | tf_op jit(solution)/shard_map/ppermute | solution.py:201
  4.7 27.1 %copy-start.4 = (s32[6,5]{1,0:T(8,128)S(1)}, s32[6,5]{1,0:T(8,128)}, u32[]{:S(2)}) copy-start(s32[6,5]{1,0:T(8,128)} %pat.7) | copy-start | bytes 364
  7.0 24.9 %collective-permute-start = (bf16[6,640,128]{2,1,0:T(8,128)(2,1)}, bf16[6,640,128]{2,1,0:T(8,128)(2,1)S(1)}, u32[]{:S(2)}, u32[]{:S(2)}) collective-permute-start(bf16[6,640,128]{2,1,0:T(8,128)(2,1)} %constant_dynamic-slice_fusion), channel_id=1, source_target_pairs={{0,2},{2,0},{1,3},{3,1},{4,6},{6,4},{5,7},{7,5},{8,10},{10,8},{9,1... | collective-permute-start | bytes 2949128 | tf_op jit(solution)/shard_map/ppermute | solution.py:212
  8.5 19.1 %collective-permute-start.1 = (bf16[384,768]{1,0:T(8,128)(2,1)}, bf16[384,768]{1,0:T(8,128)(2,1)}, u32[]{:S(2)}, u32[]{:S(2)}) collective-permute-start(bf16[384,768]{1,0:T(8,128)(2,1)} %parent.1), channel_id=1, source_target_pairs={{0,12},{1,5},{2,14},{3,7},{4,8},{5,1},{6,10},{7,3},{8,4},{9,13},{1... | collective-permute-start | bytes 1769480 | tf_op jit(solution)/shard_map/ppermute | solution.py:201
  20.7 11.1 %collective-permute-start.3 = (bf16[384,768]{1,0:T(8,128)(2,1)S(1)}, bf16[384,768]{1,0:T(8,128)(2,1)}, u32[]{:S(2)}, u32[]{:S(2)}) collective-permute-start(bf16[384,768]{1,0:T(8,128)(2,1)S(1)} %collective-permute-done.2.z2), channel_id=1, source_target_pairs={{0,1},{1,0},{2,3},{3,2},{4,5},{5,4},{6,7},{7,6},{8,9},{9,8},{10,11... | collective-permute-start | bytes 1769480 | tf_op jit(solution)/shard_map/ppermute | solution.py:204
  20.7 17.6 %collective-permute-start.5 = (bf16[384,768]{1,0:T(8,128)(2,1)S(1)}, bf16[384,768]{1,0:T(8,128)(2,1)}, u32[]{:S(2)}, u32[]{:S(2)}) collective-permute-start(bf16[384,768]{1,0:T(8,128)(2,1)S(1)} %collective-permute-done.2.z2), channel_id=1, source_target_pairs={{0,2},{1,5},{2,0},{3,7},{4,6},{5,1},{6,4},{7,3},{8,10},{9,13},{10,... | collective-permute-start | bytes 1769480 | tf_op jit(solution)/shard_map/ppermute | solution.py:201
  22.7 9.1 %copy-start.1 = (bf16[384,768]{1,0:T(8,128)(2,1)S(1)}, bf16[384,768]{1,0:T(8,128)(2,1)}, u32[]{:S(2)}) copy-start(bf16[384,768]{1,0:T(8,128)(2,1)} %parent.1) | copy-start | bytes 1769476
  22.8 0.7 %copy-start.3 = (s32[6,5]{1,0:T(8,128)S(1)}, s32[6,5]{1,0:T(8,128)}, u32[]{:S(2)}) copy-start(s32[6,5]{1,0:T(8,128)} %pat.7) | copy-start | bytes 364
  27.5 11.6 %collective-permute-start.4 = (bf16[384,768]{1,0:T(8,128)(2,1)}, bf16[384,768]{1,0:T(8,128)(2,1)S(1)}, u32[]{:S(2)}, u32[]{:S(2)}) collective-permute-start(bf16[384,768]{1,0:T(8,128)(2,1)} %collective-permute-done.1.z1), channel_id=1, source_target_pairs={{0,1},{1,0},{2,3},{3,2},{4,5},{5,4},{6,7},{7,6},{8,9},{9,8},{10,11... | collective-permute-start | bytes 1769480 | tf_op jit(solution)/shard_map/ppermute | solution.py:204
  28.5 12.9 %collective-permute-start.7 = (bf16[192,768]{1,0:T(8,128)(2,1)S(1)}, bf16[192,768]{1,0:T(8,128)(2,1)S(1)}, u32[]{:S(2)}, u32[]{:S(2)}) collective-permute-start(bf16[192,768]{1,0:T(8,128)(2,1)S(1)} %slice_select_fusion), channel_id=1, source_target_pairs={{0,2},{1,13},{2,0},{3,15},{4,6},{5,9},{6,4},{7,11},{8,10},{9,5},{1... | collective-permute-start | bytes 884744 | tf_op jit(solution)/shard_map/ppermute | solution.py:201
  38.4 4.9 %collective-permute-start.6 = (bf16[384,768]{1,0:T(8,128)(2,1)}, bf16[384,768]{1,0:T(8,128)(2,1)S(1)}, u32[]{:S(2)}, u32[]{:S(2)}) collective-permute-start(bf16[384,768]{1,0:T(8,128)(2,1)} %collective-permute-done.5.tile), channel_id=1, source_target_pairs={{0,1},{1,0},{2,3},{3,2},{4,5},{5,4},{6,7},{7,6},{8,9},{9,8},{10,11... | collective-permute-start | bytes 1769480 | tf_op jit(solution)/shard_map/ppermute | solution.py:204
  38.4 3.0 %collective-permute-start.10 = (bf16[3,640,128]{2,1,0:T(8,128)(2,1)S(1)}, bf16[3,640,128]{2,1,0:T(8,128)(2,1)S(1)}, u32[]{:S(2)}, u32[]{:S(2)}) collective-permute-start(bf16[3,640,128]{2,1,0:T(8,128)(2,1)S(1)} %get-tuple-element.22), channel_id=1, source_target_pairs={{0,1},{1,0},{2,3},{3,2},{4,5},{5,4},{6,7},{7,6},{8,9},{9,8},{10,11... | collective-permute-start | bytes 1474568 | tf_op jit(solution)/shard_map/ppermute | solution.py:204
  39.0 2.8 %collective-permute-start.9 = (bf16[3,640,128]{2,1,0:T(8,128)(2,1)S(1)}, bf16[3,640,128]{2,1,0:T(8,128)(2,1)S(1)}, u32[]{:S(2)}, u32[]{:S(2)}) collective-permute-start(bf16[3,640,128]{2,1,0:T(8,128)(2,1)S(1)} %get-tuple-element.23), channel_id=1, source_target_pairs={{0,1},{1,0},{2,3},{3,2},{4,5},{5,4},{6,7},{7,6},{8,9},{9,8},{10,11... | collective-permute-start | bytes 1474568 | tf_op jit(solution)/shard_map/ppermute | solution.py:204
  41.4 1.8 %collective-permute-start.8 = (bf16[192,768]{1,0:T(8,128)(2,1)S(1)}, bf16[192,768]{1,0:T(8,128)(2,1)S(1)}, u32[]{:S(2)}, u32[]{:S(2)}) collective-permute-start(bf16[192,768]{1,0:T(8,128)(2,1)S(1)} %collective-permute-done.7.q2), channel_id=1, source_target_pairs={{0,1},{1,0},{2,3},{3,2},{4,5},{5,4},{6,7},{7,6},{8,9},{9,8},{10,11... | collective-permute-start | bytes 884744 | tf_op jit(solution)/shard_map/ppermute | solution.py:204
  41.8 1.5 %copy-start.2 = (bf16[6,256,128]{2,1,0:T(8,128)(2,1)S(1)}, bf16[6,256,128]{2,1,0:T(8,128)(2,1)}, u32[]{:S(2)}) copy-start(bf16[6,256,128]{2,1,0:T(8,128)(2,1)} %dinv.1) | copy-start | bytes 1179652
  41.8 1.5 %copy-start.5 = (s32[6]{0:T(128)S(1)}, s32[6]{0:T(128)}, u32[]{:S(2)}) copy-start(s32[6]{0:T(128)} %widths.1) | copy-start | bytes 76
